TPU v7x, 128 devices: a whole 4x4x4 slice. The times are simulated.
128 devices in a mesh: shard: 8 (over x, z_lo), replica: 16 (over y, z_hi, core).
Axes of the slice: x: 4, y: 4, z: 4 (z_hi: 2, z_lo: 2; z = z_hi * 2 + z_lo), core: 2. Of those that a mesh axis runs over, the one named last changes fastest.
Arguments:
- tokens: bfloat16 [16, 1024, 1024], P('replica', 'shard'), may hold values from -6 to 6
- seq_lengths: int32 [16, 2], P('replica'), may hold values from 1 to 585, 1024 in all within a row
- token_places: int32 [16, 1024], P('replica'), may hold values from 0 to 1023, each once within a row
- attention_gain: bfloat16 [1024], P('shard'), may hold values from 0.5 to 1.5
- query_weight: bfloat16 [1024, 1024], P('shard'), may hold values from -0.1875 to 0.1875
- key_weight: bfloat16 [1024, 512], P('shard'), may hold values from -0.1875 to 0.1875
- value_weight: bfloat16 [1024, 512], P('shard'), may hold values from -0.1875 to 0.1875
- query_gain: bfloat16 [64], P('shard'), may hold values from 0.796875 to 1.796875
- key_gain: bfloat16 [64], P('shard'), may hold values from 0.796875 to 1.796875
- out_weight: bfloat16 [1024, 1024], P('shard'), may hold values from -1.5 to 1.5
- feedforward_gain: bfloat16 [1024], P('shard'), may hold values from 0.5 to 1.5
- gate_weight: bfloat16 [1024, 4608], P('shard'), may hold values from -0.1875 to 0.1875
- up_weight: bfloat16 [1024, 4608], P('shard'), may hold values from -0.1875 to 0.1875
- down_weight: bfloat16 [4608, 1024], P('shard'), may hold values from -0.1875 to 0.1875
- cotangent: bfloat16 [16, 1024, 1024], P('replica', 'shard'), may hold values from -6 to 6
Outputs:
- layer_out: bfloat16 [16, 1024, 1024], P('replica', 'shard')
- input_grad: float32 [16, 1024, 1024], P('replica', 'shard')
- attention_gain_grad: float32 [1024], P('shard')
- query_weight_grad: float32 [1024, 1024], P('shard')
- key_weight_grad: float32 [1024, 512], P('shard')
- value_weight_grad: float32 [1024, 512], P('shard')
- query_gain_grad: float32 [64], P('shard')
- key_gain_grad: float32 [64], P('shard')
- out_weight_grad: float32 [1024, 1024], P('shard')
- feedforward_gain_grad: float32 [1024], P('shard')
- gate_weight_grad: float32 [1024, 4608], P('shard')
- up_weight_grad: float32 [1024, 4608], P('shard')
- down_weight_grad: float32 [4608, 1024], P('shard')
Inputs may be any that keep to these rules, and one draw needn't show every extreme that they name: `seq_lengths`: each group's 2 lengths add up to 1024, and neither exceeds 585. `token_places`: each group's row holds every place of its pack once.
All inputs are finite; a program needn't handle non-finite values.
Results may differ from a plain program's by a relative error of at most 0.035.
Values may be sent and summed in bfloat16 or wider, within the bound.
No kernel may reach another device: no remote copies, remote signals or barrier semaphores. Data moves between devices by JAX's collectives and lax.ppermute only.
A program may use at most 192 MiB of HBM per device.

v0:
```python
import jax
import jax.numpy as jnp
from jax import lax
from jax.sharding import PartitionSpec as P

HEADS = 16
KV_HEADS = 8
HD = 64


norm_eps = 1e-05
rope_base = 1000000.0


def rms_scale(values):
    return lax.rsqrt(jnp.mean(values * values, axis=-1, keepdims=True) + norm_eps)


def seq_layout(places, lengths):
    seq_ends = jnp.cumsum(lengths)
    passed = places[:, None] >= seq_ends[None, :]
    segment = jnp.sum(passed.astype(jnp.int32), axis=1)
    before = jnp.sum(jnp.where(passed, lengths[None, :], 0), axis=1)
    return (segment, places - before)


def rope_tables(positions):
    half_size = HD // 2
    frequency = rope_base ** (-2.0 * jnp.arange(half_size, dtype=jnp.float32) / HD)
    angles = positions.astype(jnp.float32)[:, None] * frequency[None, :]
    return (jnp.cos(angles), jnp.sin(angles))


def rotate(values, cosine_table, sine_table):
    half_size = values.shape[-1] // 2
    front_half = values[..., :half_size]
    back_half = values[..., half_size:]
    cosine_rows = cosine_table[:, None, :]
    sine_rows = sine_table[:, None, :]
    return jnp.concatenate(
        [
            front_half * cosine_rows - back_half * sine_rows,
            back_half * cosine_rows + front_half * sine_rows,
        ],
        axis=-1,
    )


def unrotate(values, cosine_table, sine_table):
    half_size = values.shape[-1] // 2
    front_half = values[..., :half_size]
    back_half = values[..., half_size:]
    cosine_rows = cosine_table[:, None, :]
    sine_rows = sine_table[:, None, :]
    return jnp.concatenate(
        [
            front_half * cosine_rows + back_half * sine_rows,
            back_half * cosine_rows - front_half * sine_rows,
        ],
        axis=-1,
    )


def norm_back(inputs, scale_rows, gain_vector, upstream):
    normed = inputs * scale_rows
    scaled = upstream * gain_vector
    entry_grad = scale_rows * (scaled - normed * jnp.mean(scaled * normed, axis=-1, keepdims=True))
    return (entry_grad, upstream * normed)


def matmul(left_side, right_side):
    return jnp.dot(left_side, right_side, preferred_element_type=jnp.float32)


def matmul_tn(left_side, right_side):
    return lax.dot_general(
        left_side, right_side, (((0,), (0,)), ((), ())), preferred_element_type=jnp.float32
    )


def matmul_nt(left_side, right_side):
    return lax.dot_general(
        left_side, right_side, (((1,), (1,)), ((), ())), preferred_element_type=jnp.float32
    )


def on_device(
    tokens,
    seq_lengths,
    token_places,
    attention_gain,
    query_weight,
    key_weight,
    value_weight,
    query_gain,
    key_gain,
    out_weight,
    feedforward_gain,
    gate_weight,
    up_weight,
    down_weight,
    cotangent,
):
    local_rows = tokens.shape[1]
    head_repeat = HEADS // KV_HEADS
    shard_slot = lax.axis_index("shard")
    group_places = token_places[0]
    all_segment, all_positions = seq_layout(group_places, seq_lengths[0])
    own_places = lax.dynamic_slice_in_dim(group_places, shard_slot * local_rows, local_rows)
    own_segment = lax.dynamic_slice_in_dim(all_segment, shard_slot * local_rows, local_rows)
    own_positions = lax.dynamic_slice_in_dim(all_positions, shard_slot * local_rows, local_rows)
    cosine_table, sine_table = rope_tables(own_positions)
    allowed = (own_segment[:, None] == all_segment[None, :]) & (
        group_places[None, :] <= own_places[:, None]
    )
    score_scale = HD ** (-0.5)
    gain_first, query_full, key_full, value_full, gain_query, gain_key, out_full = (
        lax.all_gather(attention_gain, "shard", axis=0, tiled=True),
        lax.all_gather(query_weight, "shard", axis=0, tiled=True),
        lax.all_gather(key_weight, "shard", axis=0, tiled=True),
        lax.all_gather(value_weight, "shard", axis=0, tiled=True),
        lax.all_gather(query_gain, "shard", axis=0, tiled=True),
        lax.all_gather(key_gain, "shard", axis=0, tiled=True),
        lax.all_gather(out_weight, "shard", axis=0, tiled=True),
    )
    gain_first_f = gain_first.astype(jnp.float32)
    gain_query_f = gain_query.astype(jnp.float32)
    gain_key_f = gain_key.astype(jnp.float32)
    inputs_f = tokens[0].astype(jnp.float32)
    first_scale = rms_scale(inputs_f)
    first_normed = (inputs_f * first_scale * gain_first_f).astype(jnp.bfloat16)
    query_pre = matmul(first_normed, query_full).reshape(local_rows, HEADS, HD)
    key_pre = matmul(first_normed, key_full).reshape(local_rows, KV_HEADS, HD)
    value_pre = matmul(first_normed, value_full)
    query_scale = rms_scale(query_pre)
    query_normed = query_pre * query_scale
    queries = rotate(query_normed * gain_query_f, cosine_table, sine_table).astype(jnp.bfloat16)
    key_scale = rms_scale(key_pre)
    key_normed = key_pre * key_scale
    key_rows = rotate(key_normed * gain_key_f, cosine_table, sine_table).astype(jnp.bfloat16)
    value_rows = value_pre.astype(jnp.bfloat16)
    group_keys, group_values = (
        lax.all_gather(key_rows.reshape(local_rows, KV_HEADS * HD), "shard", axis=0, tiled=True),
        lax.all_gather(value_rows, "shard", axis=0, tiled=True),
    )
    group_rows = group_keys.shape[0]
    query_stack = queries.reshape(local_rows, KV_HEADS, head_repeat, HD).transpose(1, 0, 2, 3)
    key_stack = group_keys.reshape(group_rows, KV_HEADS, HD).transpose(1, 0, 2)
    value_stack = group_values.reshape(group_rows, KV_HEADS, HD).transpose(1, 0, 2)

    def scores_of(query_group, key_group):
        raw_scores = (
            jnp.einsum("qrd,kd->rqk", query_group, key_group, preferred_element_type=jnp.float32)
            * score_scale
        )
        return jnp.where(allowed[None], raw_scores, -1e30)

    def forward_group(pieces):
        query_group, key_group, value_group = pieces
        scores = scores_of(query_group, key_group)
        top_score = jnp.max(scores, axis=-1, keepdims=True)
        exponent = jnp.exp(scores - top_score)
        totals = jnp.sum(exponent, axis=-1, keepdims=True)
        probabilities = exponent / totals
        mixed_group = jnp.einsum(
            "rqk,kd->qrd",
            probabilities.astype(jnp.bfloat16),
            value_group,
            preferred_element_type=jnp.float32,
        )
        return (mixed_group, top_score + jnp.log(totals))

    mixed_stack, log_totals = lax.map(forward_group, (query_stack, key_stack, value_stack))
    mixed_out = (
        mixed_stack.transpose(1, 0, 2, 3).reshape(local_rows, HEADS * HD).astype(jnp.bfloat16)
    )
    middle = inputs_f + matmul(mixed_out, out_full)
    second_scale = rms_scale(middle)
    gain_second, gate_full, up_full, down_full = (
        lax.all_gather(feedforward_gain, "shard", axis=0, tiled=True),
        lax.all_gather(gate_weight, "shard", axis=0, tiled=True),
        lax.all_gather(up_weight, "shard", axis=0, tiled=True),
        lax.all_gather(down_weight, "shard", axis=0, tiled=True),
    )
    gain_second_f = gain_second.astype(jnp.float32)
    second_normed = (middle * second_scale * gain_second_f).astype(jnp.bfloat16)
    gate_value = matmul(second_normed, gate_full)
    up_value = matmul(second_normed, up_full)
    sigmoid_gate = jax.nn.sigmoid(gate_value)
    silu_gate = gate_value * sigmoid_gate
    hidden_ffn = (silu_gate * up_value).astype(jnp.bfloat16)
    result = middle + matmul(hidden_ffn, down_full)
    gain_second, gate_full, up_full, down_full = (
        lax.all_gather(feedforward_gain, "shard", axis=0, tiled=True),
        lax.all_gather(gate_weight, "shard", axis=0, tiled=True),
        lax.all_gather(up_weight, "shard", axis=0, tiled=True),
        lax.all_gather(down_weight, "shard", axis=0, tiled=True),
    )
    gain_second_f = gain_second.astype(jnp.float32)
    upstream = cotangent[0]
    upstream_f = upstream.astype(jnp.float32)
    hidden_grad = matmul_nt(upstream, down_full).astype(jnp.bfloat16)
    down_weight_grad = matmul_tn(hidden_ffn, upstream)
    hidden_grad_f = hidden_grad.astype(jnp.float32)
    gate_grad = (
        hidden_grad_f * up_value * sigmoid_gate * (1.0 + gate_value * (1.0 - sigmoid_gate))
    ).astype(jnp.bfloat16)
    up_grad = (hidden_grad_f * silu_gate).astype(jnp.bfloat16)
    gate_weight_grad = matmul_tn(second_normed, gate_grad)
    up_weight_grad = matmul_tn(second_normed, up_grad)
    second_grad = matmul_nt(gate_grad, gate_full) + matmul_nt(up_grad, up_full)
    middle_norm_grad, second_gain_terms = norm_back(
        middle, second_scale, gain_second_f, second_grad
    )
    middle_grad = upstream_f + middle_norm_grad
    second_gain_grad = jnp.sum(second_gain_terms, axis=0)
    gain_first, query_full, key_full, value_full, gain_query, gain_key, out_full = (
        lax.all_gather(attention_gain, "shard", axis=0, tiled=True),
        lax.all_gather(query_weight, "shard", axis=0, tiled=True),
        lax.all_gather(key_weight, "shard", axis=0, tiled=True),
        lax.all_gather(value_weight, "shard", axis=0, tiled=True),
        lax.all_gather(query_gain, "shard", axis=0, tiled=True),
        lax.all_gather(key_gain, "shard", axis=0, tiled=True),
        lax.all_gather(out_weight, "shard", axis=0, tiled=True),
    )
    gain_first_f = gain_first.astype(jnp.float32)
    gain_query_f = gain_query.astype(jnp.float32)
    gain_key_f = gain_key.astype(jnp.float32)
    branch_grad = middle_grad.astype(jnp.bfloat16)
    out_weight_grad = matmul_tn(mixed_out, branch_grad)
    mixed_grad = matmul_nt(branch_grad, out_full).astype(jnp.bfloat16)
    mixed_grad_stack = mixed_grad.reshape(local_rows, KV_HEADS, head_repeat, HD).transpose(
        1, 0, 2, 3
    )

    def backward_group(pieces):
        query_group, key_group, value_group, grad_group, log_group = pieces
        scores = scores_of(query_group, key_group)
        probabilities = jnp.exp(scores - log_group)
        prob_grad = jnp.einsum(
            "qrd,kd->rqk", grad_group, value_group, preferred_element_type=jnp.float32
        )
        inner_sum = jnp.sum(probabilities * prob_grad, axis=-1, keepdims=True)
        score_grad = (probabilities * (prob_grad - inner_sum)).astype(jnp.bfloat16)
        query_part = (
            jnp.einsum("rqk,kd->qrd", score_grad, key_group, preferred_element_type=jnp.float32)
            * score_scale
        )
        key_part = (
            jnp.einsum("rqk,qrd->kd", score_grad, query_group, preferred_element_type=jnp.float32)
            * score_scale
        )
        value_part = jnp.einsum(
            "rqk,qrd->kd",
            probabilities.astype(jnp.bfloat16),
            grad_group,
            preferred_element_type=jnp.float32,
        )
        return (query_part, key_part, value_part)

    query_grad_stack, key_grad_stack, value_grad_stack = lax.map(
        backward_group, (query_stack, key_stack, value_stack, mixed_grad_stack, log_totals)
    )
    key_grad_all = key_grad_stack.transpose(1, 0, 2).reshape(group_rows, KV_HEADS * HD)
    value_grad_all = value_grad_stack.transpose(1, 0, 2).reshape(group_rows, KV_HEADS * HD)
    key_grad_own, value_grad_own = (
        lax.psum_scatter(
            key_grad_all.astype(jnp.bfloat16), "shard", scatter_dimension=0, tiled=True
        ).astype(jnp.float32),
        lax.psum_scatter(
            value_grad_all.astype(jnp.bfloat16), "shard", scatter_dimension=0, tiled=True
        ).astype(jnp.float32),
    )
    value_pre_grad = value_grad_own.astype(jnp.bfloat16)
    key_turned = unrotate(key_grad_own.reshape(local_rows, KV_HEADS, HD), cosine_table, sine_table)
    key_norm_grad, key_gain_terms = norm_back(key_pre, key_scale, gain_key_f, key_turned)
    key_pre_grad = key_norm_grad.reshape(local_rows, KV_HEADS * HD).astype(jnp.bfloat16)
    key_gain_grad = jnp.sum(key_gain_terms, axis=(0, 1))
    query_turned = unrotate(
        query_grad_stack.transpose(1, 0, 2, 3).reshape(local_rows, HEADS, HD),
        cosine_table,
        sine_table,
    )
    query_norm_grad, query_gain_terms = norm_back(
        query_pre, query_scale, gain_query_f, query_turned
    )
    query_pre_grad = query_norm_grad.reshape(local_rows, HEADS * HD).astype(jnp.bfloat16)
    query_gain_grad = jnp.sum(query_gain_terms, axis=(0, 1))
    query_weight_grad = matmul_tn(first_normed, query_pre_grad)
    key_weight_grad = matmul_tn(first_normed, key_pre_grad)
    value_weight_grad = matmul_tn(first_normed, value_pre_grad)
    first_grad = (
        matmul_nt(query_pre_grad, query_full)
        + matmul_nt(key_pre_grad, key_full)
        + matmul_nt(value_pre_grad, value_full)
    )
    input_norm_grad, first_gain_terms = norm_back(inputs_f, first_scale, gain_first_f, first_grad)
    input_grad = middle_grad + input_norm_grad
    first_gain_grad = jnp.sum(first_gain_terms, axis=0)
    (
        share_first,
        share_query,
        share_key,
        share_value,
        share_qgain,
        share_kgain,
        share_out,
        share_second,
        share_gate,
        share_up,
        share_down,
    ) = (
        lax.psum_scatter(
            first_gain_grad.astype(jnp.bfloat16), "shard", scatter_dimension=0, tiled=True
        ).astype(jnp.float32),
        lax.psum_scatter(
            query_weight_grad.astype(jnp.bfloat16), "shard", scatter_dimension=0, tiled=True
        ).astype(jnp.float32),
        lax.psum_scatter(
            key_weight_grad.astype(jnp.bfloat16), "shard", scatter_dimension=0, tiled=True
        ).astype(jnp.float32),
        lax.psum_scatter(
            value_weight_grad.astype(jnp.bfloat16), "shard", scatter_dimension=0, tiled=True
        ).astype(jnp.float32),
        lax.psum_scatter(
            query_gain_grad.astype(jnp.bfloat16), "shard", scatter_dimension=0, tiled=True
        ).astype(jnp.float32),
        lax.psum_scatter(
            key_gain_grad.astype(jnp.bfloat16), "shard", scatter_dimension=0, tiled=True
        ).astype(jnp.float32),
        lax.psum_scatter(
            out_weight_grad.astype(jnp.bfloat16), "shard", scatter_dimension=0, tiled=True
        ).astype(jnp.float32),
        lax.psum_scatter(
            second_gain_grad.astype(jnp.bfloat16), "shard", scatter_dimension=0, tiled=True
        ).astype(jnp.float32),
        lax.psum_scatter(
            gate_weight_grad.astype(jnp.bfloat16), "shard", scatter_dimension=0, tiled=True
        ).astype(jnp.float32),
        lax.psum_scatter(
            up_weight_grad.astype(jnp.bfloat16), "shard", scatter_dimension=0, tiled=True
        ).astype(jnp.float32),
        lax.psum_scatter(
            down_weight_grad.astype(jnp.bfloat16), "shard", scatter_dimension=0, tiled=True
        ).astype(jnp.float32),
    )
    (
        final_first,
        final_query,
        final_key,
        final_value,
        final_qgain,
        final_kgain,
        final_out,
        final_second,
        final_gate,
        final_up,
        final_down,
    ) = (
        lax.psum(share_first.astype(jnp.bfloat16), "replica").astype(jnp.float32),
        lax.psum(share_query.astype(jnp.bfloat16), "replica").astype(jnp.float32),
        lax.psum(share_key.astype(jnp.bfloat16), "replica").astype(jnp.float32),
        lax.psum(share_value.astype(jnp.bfloat16), "replica").astype(jnp.float32),
        lax.psum(share_qgain.astype(jnp.bfloat16), "replica").astype(jnp.float32),
        lax.psum(share_kgain.astype(jnp.bfloat16), "replica").astype(jnp.float32),
        lax.psum(share_out.astype(jnp.bfloat16), "replica").astype(jnp.float32),
        lax.psum(share_second.astype(jnp.bfloat16), "replica").astype(jnp.float32),
        lax.psum(share_gate.astype(jnp.bfloat16), "replica").astype(jnp.float32),
        lax.psum(share_up.astype(jnp.bfloat16), "replica").astype(jnp.float32),
        lax.psum(share_down.astype(jnp.bfloat16), "replica").astype(jnp.float32),
    )
    return (
        result.astype(jnp.bfloat16)[None],
        input_grad[None],
        final_first,
        final_query,
        final_key,
        final_value,
        final_qgain,
        final_kgain,
        final_out,
        final_second,
        final_gate,
        final_up,
        final_down,
    )


def solution(mesh):
    placed = (
        P("replica", "shard", None),
        P("replica", None),
        P("replica", None),
        P("shard"),
        P("shard", None),
        P("shard", None),
        P("shard", None),
        P("shard"),
        P("shard"),
        P("shard", None),
        P("shard"),
        P("shard", None),
        P("shard", None),
        P("shard", None),
        P("replica", "shard", None),
    )
    return jax.shard_map(
        on_device,
        mesh=mesh,
        in_specs=placed,
        out_specs=(
            P("replica", "shard", None),
            P("replica", "shard", None),
            P("shard"),
            P("shard", None),
            P("shard", None),
            P("shard", None),
            P("shard"),
            P("shard"),
            P("shard", None),
            P("shard"),
            P("shard", None),
            P("shard", None),
            P("shard", None),
        ),
        check_vma=False,
    )
```

profile of v0, /device:TPU:1, one launch (start us, length us, event | category | flops | bytes accessed | tf_op | source)
XLA Modules:
  0.0 1985.1 jit_solution(8155797451789885886)
XLA Ops:
  9.5 16.3 all-gather
  26.9 20.8 %all-gather.12.cloned.1.call-done = bf16[1024,512]{1,0:T(8,128)(2,1)} async-done(((bf16[128,512]{1,0:T(8,128)(2,1)}), bf16[1024,512]{1,0:T(8,128)(2,1)}) %all-gather.12.cloned.1.call-update) | async-done | bytes 1048592 | tf_op jit(solution)/shard_map/all_gather | solution.py:121
  51.9 15.1 all-reduce.9
  67.5 20.3 %all-gather.16.cloned.1.call-done = bf16[1024,512]{1,0:T(8,128)(2,1)} async-done(((bf16[128,512]{1,0:T(8,128)(2,1)}), bf16[1024,512]{1,0:T(8,128)(2,1)}) %all-gather.16.cloned.1.call-update) | async-done | bytes 1048592 | tf_op jit(solution)/shard_map/all_gather | solution.py:120
  94.2 15.1 all-gather.1
  109.4 33.4 %all-gather.20.cloned.1.call-done = bf16[1024,1024]{1,0:T(8,128)(2,1)} async-done(((bf16[128,1024]{1,0:T(8,128)(2,1)}), bf16[1024,1024]{1,0:T(8,128)(2,1)}) %all-gather.20.cloned.1.call-update) | async-done | bytes 2097168 | tf_op jit(solution)/shard_map/all_gather | solution.py:119
  146.7 35.0 %all-gather.14.cloned.1.call-done = bf16[1024,512]{1,0:T(8,128)(2,1)} async-done(((bf16[128,512]{1,0:T(8,128)(2,1)}), bf16[1024,512]{1,0:T(8,128)(2,1)}) %all-gather.14.cloned.1.call-update) | async-done | bytes 1048592 | tf_op jit(solution)/shard_map/all_gather | solution.py:144
  185.9 41.0 %all-gather.18.cloned.1.call-done = bf16[1024,512]{0,1:T(8,128)(2,1)} async-done(((bf16[128,512]{0,1:T(8,128)(2,1)}), bf16[1024,512]{0,1:T(8,128)(2,1)}) %all-gather.18.cloned.1.call-update) | async-done | bytes 1048592 | tf_op jit(solution)/shard_map/all_gather | solution.py:143
  226.9 21.4 %while.30 = (s32[]{:T(128)}, bf16[8,128,2,64]{1,3,2,0:T(8,128)(2,1)S(1)}, f32[8,2,128,1]{2,1,3,0:T(2,128)}, bf16[8,1024,64]{1,2,0:T(8,128)(2,1)S(1)}, bf16[8,102...) while((s32[]{:T(128)}, ...), condition=%wide.region_9.10_spmd.clone.clone, body=%wide.region_6.9_spmd.clone.sunk.clone | while | flops 69598976 | bytes 3787889 | solution.py:173
  248.3 35.8 %all-gather.22.cloned.1.call-done = bf16[1024,1024]{1,0:T(8,128)(2,1)} async-done(((bf16[128,1024]{1,0:T(8,128)(2,1)}), bf16[1024,1024]{1,0:T(8,128)(2,1)}) %all-gather.22.cloned.1.call-update) | async-done | bytes 2097168 | tf_op jit(solution)/shard_map/all_gather | solution.py:124
  286.4 188.5 %all-gather.24.cloned.1.call-done = bf16[1024,4608]{1,0:T(8,128)(2,1)} async-done(((bf16[128,4608]{1,0:T(8,128)(2,1)}), bf16[1024,4608]{1,0:T(8,128)(2,1)}) %all-gather.24.cloned.1.call-update) | async-done | bytes 9437200 | tf_op jit(solution)/shard_map/all_gather | solution.py:181
  474.9 6.5 fusion.87
  481.5 186.3 %all-gather.26.cloned.1.call-done = bf16[1024,4608]{1,0:T(8,128)(2,1)} async-done(((bf16[128,4608]{1,0:T(8,128)(2,1)}), bf16[1024,4608]{1,0:T(8,128)(2,1)}) %all-gather.26.cloned.1.call-update) | async-done | bytes 9437200 | tf_op jit(solution)/shard_map/all_gather | solution.py:182
  667.7 6.5 fusion.88
  674.2 186.3 %all-gather.28.cloned.1.call-done = bf16[4608,1024]{1,0:T(8,128)(2,1)} async-done(((bf16[576,1024]{1,0:T(8,128)(2,1)}), bf16[4608,1024]{1,0:T(8,128)(2,1)}) %all-gather.28.cloned.1.call-update) | async-done | bytes 9437200 | tf_op jit(solution)/shard_map/all_gather | solution.py:183
  860.6 8.7 multiply_convert_fusion.1
  869.3 7.6 fusion.89
  884.3 71.1 %while.31 = (s32[]{:T(128)}, f32[8,128,2,64]{1,3,2,0:T(8,128)}, bf16[8,1024,64]{1,2,0:T(8,128)(2,1)}, bf16[8,1024,64]{1,2,0:T(8,128)(2,1)}, bf16[8,1024,64]{1,2,...) while((s32[]{:T(128)}, f32[8,128,2,64]{1,3,2,0:T(8,128)}, ...), condition=%wide.region_14.15_spmd.clone.clone, body=%wide.region_12.14_spmd.clone.sunk.clone | while | flops 170606336 | bytes 9260169 | solution.py:261
  960.3 35.1 %reduce-scatter.28.cloned.1.call-done = bf16[128,512]{1,0:T(8,128)(2,1)} async-done(((bf16[1024,512]{1,0:T(8,128)(2,1)}), bf16[128,512]{1,0:T(8,128)(2,1)}) %reduce-scatter.28.cloned.1.call-update) | async-done | bytes 131088
  1003.9 32.8 %reduce-scatter.30.cloned.1.call-done = bf16[128,512]{1,0:T(8,128)(2,1)} async-done(((bf16[1024,512]{1,0:T(8,128)(2,1)}), bf16[128,512]{1,0:T(8,128)(2,1)}) %reduce-scatter.30.cloned.1.call-update) | async-done | bytes 131088
  1046.5 6.4 convolution_convert_fusion.2
  1053.0 6.4 convolution_convert_fusion.1
  1065.5 11.9 reduce-scatter.16.cloned.1.call-done
  1077.4 41.1 %reduce-scatter.18.cloned.1.call-done = bf16[128,512]{1,0:T(8,128)(2,1)} async-done(((bf16[1024,512]{1,0:T(8,128)(2,1)}), bf16[128,512]{1,0:T(8,128)(2,1)}) %reduce-scatter.18.cloned.1.call-update) | async-done | bytes 131088 | tf_op jit(solution)/shard_map/reduce_scatter | solution.py:322
  1118.6 56.9 %reduce-scatter.14.cloned.1.call-done = bf16[128,1024]{1,0:T(8,128)(2,1)} async-done(((bf16[1024,1024]{1,0:T(8,128)(2,1)}), bf16[128,1024]{1,0:T(8,128)(2,1)}) %reduce-scatter.14.cloned.1.call-update) | async-done | bytes 262160 | tf_op jit(solution)/shard_map/reduce_scatter | solution.py:316
  1175.5 55.0 %reduce-scatter.20.cloned.1.call-done = bf16[128,1024]{1,0:T(8,128)(2,1)} async-done(((bf16[1024,1024]{1,0:T(8,128)(2,1)}), bf16[128,1024]{1,0:T(8,128)(2,1)}) %reduce-scatter.20.cloned.1.call-update) | async-done | bytes 262160 | tf_op jit(solution)/shard_map/reduce_scatter | solution.py:331
  1230.4 193.3 %reduce-scatter.22.cloned.1.call-done = bf16[128,4608]{1,0:T(8,128)(2,1)} async-done(((bf16[1024,4608]{1,0:T(8,128)(2,1)}), bf16[128,4608]{1,0:T(8,128)(2,1)}) %reduce-scatter.22.cloned.1.call-update) | async-done | bytes 1179664 | tf_op jit(solution)/shard_map/reduce_scatter | solution.py:337
  1423.7 192.2 %reduce-scatter.24.cloned.1.call-done = bf16[128,4608]{1,0:T(8,128)(2,1)} async-done(((bf16[1024,4608]{1,0:T(8,128)(2,1)}), bf16[128,4608]{1,0:T(8,128)(2,1)}) %reduce-scatter.24.cloned.1.call-update) | async-done | bytes 1179664 | tf_op jit(solution)/shard_map/reduce_scatter | solution.py:340
  1615.9 192.2 %reduce-scatter.26.cloned.1.call-done = bf16[576,1024]{1,0:T(8,128)(2,1)} async-done(((bf16[4608,1024]{1,0:T(8,128)(2,1)}), bf16[576,1024]{1,0:T(8,128)(2,1)}) %reduce-scatter.26.cloned.1.call-update) | async-done | bytes 1179664 | tf_op jit(solution)/shard_map/reduce_scatter | solution.py:343
  1819.7 15.9 all-reduce.8
  1835.9 36.5 %all-reduce.6 = (bf16[128]{0:T(256)(128)(2,1)S(1)}, bf16[8]{0:T(256)(128)(2,1)S(1)}, bf16[8]{0:T(256)(128)(2,1)S(1)}, bf16[128]{0:T(256)(128)(2,1)S(1)}) all-reduce(bf16[128]{0:T(256)(128)(2,1)S(1)} %dynamic-slice.4, bf16[8]{0:T(256)(128)(2,1)S(1)} %dynamic-slice.6, ...), channel_id=1, replica_groups=mesh['shard'=8,'replica'=16] {'replica'}, use_global_device_ids=true, to_apply=%region_22.23 | all-reduce | flops 272 | bytes 1088 | tf_op jit(solution)/shard_map/psum | solution.py:360
  1875.5 91.1 %all-reduce.12.cloned.1.call-done = (bf16[128,1024]{1,0:T(8,128)(2,1)}, bf16[128,512]{1,0:T(8,128)(2,1)}, bf16[128,512]{1,0:T(8,128)(2,1)}, bf16[128,1024]{1,0:T...) async-done(((bf16[128,1024]{1,0:T(8,128)(2,1)}, bf16[128,512]{1,0:T(8,128)(2,1)}, bf16[128,512]{1,0:T(8,128)(2,1)}, ...) | async-done | bytes 4325392 | tf_op jit(solution)/shard_map/psum | solution.py:361
  (322 shorter events, 178.0 us)
Async XLA Ops:
  7.2 82.1 %copy-start.1 = (bf16[1,128,1024]{2,1,0:T(8,128)(2,1)S(1)}, bf16[1,128,1024]{2,1,0:T(8,128)(2,1)}, u32[]{:S(2)}) copy-start(bf16[1,128,1024]{2,1,0:T(8,128)(2,1)} %param.19) | copy-start | bytes 786436
  7.2 59.7 %copy-start.45 = (s32[1,2]{1,0:T(1,128)S(1)}, s32[1,2]{1,0:T(1,128)}, u32[]{:S(2)}) copy-start(s32[1,2]{1,0:T(1,128)} %param.20) | copy-start | bytes 28
  7.2 59.9 %copy-start.19 = (s32[1,1024]{1,0:T(1,128)S(1)}, s32[1,1024]{1,0:T(1,128)}, u32[]{:S(2)}) copy-start(s32[1,1024]{1,0:T(1,128)} %param.21) | copy-start | bytes 12292
  7.2 40.5 %all-gather.12.cloned.1.call-start = ((), (), s32[]{:S(2)}) async-start(), calls=%async_computation.9 | async-start | bytes 1179648 | tf_op jit(solution)/shard_map/all_gather | solution.py:121
  8.0 79.9 %all-gather.16.cloned.1.call-start = ((), (), s32[]{:S(2)}) async-start(), calls=%async_computation.11 | async-start | bytes 1179648 | tf_op jit(solution)/shard_map/all_gather | solution.py:120
  8.7 134.0 %all-gather.20.cloned.1.call-start = ((), (), s32[]{:S(2)}) async-start(), calls=%async_computation.13 | async-start | bytes 2359296 | tf_op jit(solution)/shard_map/all_gather | solution.py:119
  9.5 172.2 %all-gather.14.cloned.1.call-start = ((), (), s32[]{:S(2)}) async-start(), calls=%async_computation.10 | async-start | bytes 1179648 | tf_op jit(solution)/shard_map/all_gather | solution.py:144
  25.8 157.3 %copy-start.25 = (f32[8,1,128]{2,1,0:T(1,128)}, f32[8,1,128]{2,1,0:T(1,128)S(1)}, u32[]{:S(2)}) copy-start(f32[8,1,128]{2,1,0:T(1,128)S(1)} %convert_element_type.286) | copy-start | bytes 12292
  26.9 156.2 %copy-start.33 = (f32[128]{0:T(128)}, f32[128]{0:T(128)S(1)}, u32[]{:S(2)}) copy-start(f32[128]{0:T(128)S(1)} %add_rsqrt_fusion.3) | copy-start | bytes 1540
  50.1 176.8 %all-gather.18.cloned.1.call-start = ((), (), s32[]{:S(2)}) async-start(), calls=%async_computation.12 | async-start | bytes 1179648 | tf_op jit(solution)/shard_map/all_gather | solution.py:143
  67.5 118.3 %copy-start.21 = (f32[128,32]{0,1:T(8,128)}, f32[128,32]{0,1:T(8,128)S(1)}, u32[]{:S(2)}) copy-start(f32[128,32]{0,1:T(8,128)S(1)} %get-tuple-element.256) | copy-start | bytes 49156
  67.5 118.3 %copy-start.23 = (f32[128,32]{0,1:T(8,128)}, f32[128,32]{0,1:T(8,128)S(1)}, u32[]{:S(2)}) copy-start(f32[128,32]{0,1:T(8,128)S(1)} %get-tuple-element.257) | copy-start | bytes 49156
  91.2 192.9 %all-gather.22.cloned.1.call-start = ((), (), s32[]{:S(2)}) async-start(), calls=%async_computation.14 | async-start | bytes 2359296 | tf_op jit(solution)/shard_map/all_gather | solution.py:124
  91.8 383.1 %all-gather.24.cloned.1.call-start = ((), (), s32[]{:S(2)}) async-start(), calls=%async_computation.15 | async-start | bytes 10616832 | tf_op jit(solution)/shard_map/all_gather | solution.py:181
  92.6 575.2 %all-gather.26.cloned.1.call-start = ((), (), s32[]{:S(2)}) async-start(), calls=%async_computation.16 | async-start | bytes 10616832 | tf_op jit(solution)/shard_map/all_gather | solution.py:182
  93.3 767.2 %all-gather.28.cloned.1.call-start = ((), (), s32[]{:S(2)}) async-start(), calls=%async_computation.17 | async-start | bytes 10616832 | tf_op jit(solution)/shard_map/all_gather | solution.py:183
  94.0 901.4 %reduce-scatter.28.cloned.1.call-start = ((), (), s32[]{:S(2)}) async-start(), calls=%async_computation.25 | async-start | bytes 1179648
  94.1 91.5 %copy-start.37 = (f32[64]{0:T(128)}, f32[64]{0:T(128)S(1)}, u32[]{:S(2)}) copy-start(f32[64]{0:T(128)S(1)} %convert_element_type.238) | copy-start | bytes 772
  248.3 233.1 %copy-start.8 = (bf16[8,128,2,64]{1,3,2,0:T(8,128)(2,1)}, bf16[8,128,2,64]{1,3,2,0:T(8,128)(2,1)S(1)}, u32[]{:S(2)}) copy-start(bf16[8,128,2,64]{1,3,2,0:T(8,128)(2,1)S(1)} %get-tuple-element.105) | copy-start | bytes 786436
  248.3 233.1 %copy-start.10 = (bf16[8,128,2,64]{1,3,2,0:T(8,128)(2,1)}, bf16[8,128,2,64]{1,3,2,0:T(8,128)(2,1)S(1)}, u32[]{:S(2)}) copy-start(bf16[8,128,2,64]{1,3,2,0:T(8,128)(2,1)S(1)} %get-tuple-element.599) | copy-start | bytes 786436
  248.3 233.1 %copy-start.31 = (s32[128]{0:T(128)}, s32[128]{0:T(128)S(1)}, u32[]{:S(2)}) copy-start(s32[128]{0:T(128)S(1)} %get-tuple-element.647) | copy-start | bytes 1540
  286.3 195.2 %copy-start.40 = (f32[128]{0:T(128)}, f32[128]{0:T(128)S(1)}, u32[]{:S(2)}) copy-start(f32[128]{0:T(128)S(1)} %add_rsqrt_fusion.2) | copy-start | bytes 1540
  481.4 379.1 %copy-start.16 = (bf16[1,128,1024]{2,1,0:T(8,128)(2,1)S(1)}, bf16[1,128,1024]{2,1,0:T(8,128)(2,1)}, u32[]{:S(2)}) copy-start(bf16[1,128,1024]{2,1,0:T(8,128)(2,1)} %param.33) | copy-start | bytes 786436
  957.7 79.1 %reduce-scatter.30.cloned.1.call-start = ((), (), s32[]{:S(2)}) async-start(), calls=%async_computation.26 | async-start | bytes 1179648
  960.1 117.4 %reduce-scatter.16.cloned.1.call-start = ((), (), s32[]{:S(2)}) async-start(), calls=%async_computation.19 | async-start | bytes 1179648 | tf_op jit(solution)/shard_map/reduce_scatter | solution.py:319
  1003.9 114.7 %reduce-scatter.18.cloned.1.call-start = ((), (), s32[]{:S(2)}) async-start(), calls=%async_computation.20 | async-start | bytes 1179648 | tf_op jit(solution)/shard_map/reduce_scatter | solution.py:322
  1039.3 136.2 %reduce-scatter.14.cloned.1.call-start = ((), (), s32[]{:S(2)}) async-start(), calls=%async_computation.18 | async-start | bytes 2359296 | tf_op jit(solution)/shard_map/reduce_scatter | solution.py:316
  1044.4 186.0 %reduce-scatter.20.cloned.1.call-start = ((), (), s32[]{:S(2)}) async-start(), calls=%async_computation.21 | async-start | bytes 2359296 | tf_op jit(solution)/shard_map/reduce_scatter | solution.py:331
  1046.5 377.2 %reduce-scatter.22.cloned.1.call-start = ((), (), s32[]{:S(2)}) async-start(), calls=%async_computation.22 | async-start | bytes 10616832 | tf_op jit(solution)/shard_map/reduce_scatter | solution.py:337
  1052.9 563.0 %reduce-scatter.24.cloned.1.call-start = ((), (), s32[]{:S(2)}) async-start(), calls=%async_computation.23 | async-start | bytes 10616832 | tf_op jit(solution)/shard_map/reduce_scatter | solution.py:340
  1059.4 748.8 %reduce-scatter.26.cloned.1.call-start = ((), (), s32[]{:S(2)}) async-start(), calls=%async_computation.24 | async-start | bytes 10616832 | tf_op jit(solution)/shard_map/reduce_scatter | solution.py:343
  1065.4 901.1 %all-reduce.12.cloned.1.call-start = ((), (), s32[]{:S(2)}) async-start(), calls=%async_computation.27 | async-start | bytes 8650752 | tf_op jit(solution)/shard_map/psum | solution.py:361
  (35 other events, 555.9 us)
Sparse Core Ops, SparseCore 0:
  9.7 37.9 all-gather.11
  49.3 38.4 all-gather.15
  89.5 53.1 all-gather.19
  144.8 36.8 all-gather.13
  183.7 43.1 all-gather.17
  228.4 55.6 all-gather.21
  285.8 189.1 all-gather.23
  476.6 191.1 all-gather.25
  669.4 191.1 all-gather.27
  957.8 37.5 reduce-scatter.27
  998.4 38.3 reduce-scatter.29
  1039.0 38.3 reduce-scatter.15
  1079.8 38.7 reduce-scatter.17
  1121.4 54.0 reduce-scatter.13
  1178.3 52.0 reduce-scatter.19
  1232.7 190.9 reduce-scatter.21
  1426.0 189.9 reduce-scatter.23
  1618.2 189.9 reduce-scatter.25
  1811.3 155.2 all-reduce.11
where the time goes:
time: 1990 us
  waiting for transfers between devices  1650 us (83%)
  matrix products  153 us (8%)
  blocking collectives  98.9 us (5%)
  other arithmetic  36.3 us (2%)
  local copies, waits for them, and re-layouts  24.5 us (1%)
    reduce_scatter x1, waiting for transfers between devices, on_device(): lax.psum_scatter(gate_weight_grad.astype(jnp.bfloat16), 'shard', scatter_...  193 us
    reduce_scatter x1, waiting for transfers between devices, on_device(): lax.psum_scatter(down_weight_grad.astype(jnp.bfloat16), 'shard', scatter_...  192 us
    reduce_scatter x1, waiting for transfers between devices, on_device(): lax.psum_scatter(up_weight_grad.astype(jnp.bfloat16), 'shard', scatter_di...  192 us
    all_gather x1, waiting for transfers between devices, on_device(): lax.all_gather(gate_weight, 'shard', axis=0, tiled=True)  189 us
    all_gather x1, waiting for transfers between devices, on_device(): lax.all_gather(down_weight, 'shard', axis=0, tiled=True)  186 us
    all_gather x1, waiting for transfers between devices, on_device(): lax.all_gather(up_weight, 'shard', axis=0, tiled=True)  186 us
    psum x1, waiting for transfers between devices, on_device(): lax.psum(share_query.astype(jnp.bfloat16), 'replica').astype(jnp.float32)  91.1 us
    unnamed x21, waiting for transfers between devices  72.8 us
  transfers between devices with their start and end apart: 19, of which 19 were waited for; matrix products, arithmetic and copies ran while one was open for 5% of the time, Pallas kernels for 0%

commit v1 on v0

v1 whole, which is shorter than its diff:
```python
import jax
import jax.numpy as jnp
from jax import lax
from jax.sharding import PartitionSpec as P

HEADS = 16
KV_HEADS = 8
HD = 64
AXES = ("shard", "replica")

norm_eps = 1e-05
rope_base = 1000000.0
bf16 = jnp.bfloat16
f32 = jnp.float32


def place(x, y, z, core):
    return ((x % 4) * 2 + (z % 4) % 2) * 16 + ((y % 4) * 2 + (z % 4) // 2) * 2 + core % 2


def pairs(move, keep=lambda x, y, z, c: True):
    found = []
    for x in range(4):
        for y in range(4):
            for z in range(4):
                for c in range(2):
                    if keep(x, y, z, c):
                        found.append((place(x, y, z, c), place(*move(x, y, z, c))))
    return found


def home(x, y, z, c):
    return c == z % 2


x_up = pairs(lambda x, y, z, c: (x + 1, y, z, c))
x_down = pairs(lambda x, y, z, c: (x - 1, y, z, c))
x_far = pairs(lambda x, y, z, c: (x + 2, y, z, c))
y_up = pairs(lambda x, y, z, c: (x, y + 1, z, c))
y_down = pairs(lambda x, y, z, c: (x, y - 1, z, c))
y_far = pairs(lambda x, y, z, c: (x, y + 2, z, c))
z_up = pairs(lambda x, y, z, c: (x, y, z + 1, c))
z_down = pairs(lambda x, y, z, c: (x, y, z - 1, c))
z_far = pairs(lambda x, y, z, c: (x, y, z + 2, c))
z_up_home = pairs(lambda x, y, z, c: (x, y, z + 1, c), home)
z_down_home = pairs(lambda x, y, z, c: (x, y, z - 1, c), home)
other_core = pairs(lambda x, y, z, c: (x, y, z, 1 - c))
from_home = pairs(lambda x, y, z, c: (x, y, z, 1 - c), home)
regroup = pairs(lambda x, y, z, c: (x, y, (z // 2) * 2 + c, z % 2))


def send(values, moves):
    return lax.ppermute(values, AXES, moves)


def cat(pieces, axis=0):
    return jnp.concatenate(pieces, axis=axis)


def pick(values, index, axis):
    return lax.dynamic_index_in_dim(values, index, axis, keepdims=False)


def unroll(values, index, axis):
    doubled = cat([values, values], axis)
    return lax.dynamic_slice_in_dim(doubled, (4 - index) % 4, 4, axis)


def gather_group(block):
    near = [send(block, x_down), send(block, x_far), send(block, x_up)]
    mine = cat([block] + near)
    return cat([mine, send(mine, other_core)])


def scatter_group(partial):
    rows = partial.shape[0] // 8
    blocks = partial.reshape(8, rows, partial.shape[1])
    got = send(blocks[4:].astype(bf16), other_core)
    summed = blocks[:4] + got.astype(f32)
    low = summed.astype(bf16)
    return (
        summed[0]
        + send(low[1], x_up).astype(f32)
        + send(low[2], x_far).astype(f32)
        + send(low[3], x_down).astype(f32)
    )


def spread_columns(columns, x, z_low):
    near = [pick(columns, (x + step) % 4, 1) for step in range(4)]
    got = jnp.stack([near[0], send(near[3], x_down), send(near[2], x_far), send(near[1], x_up)])
    across = cat([send(got[:2], z_up), send(got[2:], z_down)])
    even = jnp.where(z_low == 0, got, across)
    odd = jnp.where(z_low == 0, across, got)
    ordered = unroll(jnp.stack([even, odd], axis=1), x, 0)
    return ordered.reshape(1024, columns.shape[2])


def reduce_ring(pieces, up, down, far):
    return (
        pieces[0]
        + send(pieces[1].astype(bf16), up).astype(f32)
        + send(pieces[2].astype(bf16), far).astype(f32)
        + send(pieces[3].astype(bf16), down).astype(f32)
    )


def reduce_ring_wide(pieces, up, down):
    half = pieces[0].shape[0] // 2
    low = pieces[2].astype(bf16)
    to_up = send(low[:half], up).astype(f32)
    to_down = send(low[half:], down).astype(f32)
    first = cat([pieces[1][:half] + to_up, pieces[1][half:]])
    third = cat([pieces[3][:half], pieces[3][half:] + to_down])
    return (
        pieces[0]
        + send(first.astype(bf16), up).astype(f32)
        + send(third.astype(bf16), down).astype(f32)
    )


def gather_ring(block, up, down, far):
    return jnp.stack([block, send(block, down), send(block, far), send(block, up)])


def gather_ring_wide(block, up, down):
    half = block.shape[0] // 2
    after, before = send(block, down), send(block, up)
    across = cat([send(after[:half], down), send(before[half:], up)])
    return jnp.stack([block, after, across, before])


def reduce_weights(by_row, by_block, where):
    x, y, z, core, z_low = where
    width, block_width = by_row.shape[1], by_block.shape[1]
    grid = cat([by_row, by_block], 1).reshape(8, 4, 4, 8, width + block_width)
    wide = width > 512
    pieces = [pick(grid, (y + step) % 4, 1) for step in range(4)]
    if wide:
        rows = reduce_ring_wide(pieces, y_up, y_down)
    else:
        rows = reduce_ring(pieces, y_up, y_down, y_far)
    rows = reduce_ring([pick(rows, (z + step) % 4, 1) for step in range(4)], z_up, z_down, z_far)
    rows = rows.astype(bf16)
    own = rows[..., :width].reshape(4, 2, 8, width)
    near = [pick(own, (x + step) % 4, 0) for step in range(4)]
    got = jnp.stack([near[0], send(near[3], x_down), send(near[2], x_far), send(near[1], x_up)])
    flat = rows[..., width:].reshape(32, 2 * block_width)
    same = cat([pick(got, z_low, 1).reshape(32, width), flat], 1)
    odd = cat([pick(got, 1 - z_low, 1).reshape(32, width), flat], 1)
    stacked = jnp.stack([same, send(odd, z_down), send(same, z_far), send(odd, z_up)])
    stacked = stacked.reshape(128, width + 2 * block_width)
    if wide:
        stacked = gather_ring_wide(stacked, y_up, y_down)
    else:
        stacked = gather_ring(stacked, y_up, y_down, y_far)
    stacked = stacked.reshape(4, 4, 32, width + 2 * block_width)
    stacked = unroll(unroll(stacked, y, 0), z, 1)
    row_part, block_part = stacked[..., :width], stacked[..., width:]
    row_other = send(row_part, other_core)
    block_other = send(block_part, from_home)
    block_part = jnp.where(core == z_low, block_part, block_other)
    first = jnp.where(core == 0, row_part, row_other)
    second = jnp.where(core == 0, row_other, row_part)
    both = jnp.stack([first, second], axis=2).reshape(4, 4, 2, 4, 8, width)
    both = unroll(both, x, 3)
    by_row_out = both.transpose(0, 1, 4, 3, 2, 5).reshape(128, 8, width)
    by_block_out = block_part.reshape(4, 4, 8, 8, block_width)
    by_block_out = by_block_out.transpose(2, 0, 1, 3, 4).reshape(1024, block_width)
    return by_row_out, by_block_out


def rms_scale(values):
    return lax.rsqrt(jnp.mean(values * values, axis=-1, keepdims=True) + norm_eps)


def rope_tables(positions):
    half_size = HD // 2
    frequency = rope_base ** (-2.0 * jnp.arange(half_size, dtype=f32) / HD)
    angles = positions.astype(f32)[:, None] * frequency[None, :]
    return (jnp.cos(angles), jnp.sin(angles))


def rotate(values, cosine_table, sine_table):
    half_size = values.shape[-1] // 2
    front, back = values[..., :half_size], values[..., half_size:]
    cosine, sine = cosine_table[:, None, :], sine_table[:, None, :]
    return cat([front * cosine - back * sine, back * cosine + front * sine], -1)


def unrotate(values, cosine_table, sine_table):
    half_size = values.shape[-1] // 2
    front, back = values[..., :half_size], values[..., half_size:]
    cosine, sine = cosine_table[:, None, :], sine_table[:, None, :]
    return cat([front * cosine + back * sine, back * cosine - front * sine], -1)


def norm_back(inputs, scale_rows, gain_vector, upstream):
    normed = inputs * scale_rows
    scaled = upstream * gain_vector
    entry_grad = scale_rows * (scaled - normed * jnp.mean(scaled * normed, axis=-1, keepdims=True))
    return (entry_grad, upstream * normed)


def matmul(left_side, right_side):
    return jnp.dot(left_side, right_side, preferred_element_type=f32)


def matmul_tn(left_side, right_side):
    return lax.dot_general(
        left_side, right_side, (((0,), (0,)), ((), ())), preferred_element_type=f32
    )


def matmul_nt(left_side, right_side):
    return lax.dot_general(
        left_side, right_side, (((1,), (1,)), ((), ())), preferred_element_type=f32
    )


def attend(queries, keys, values, allowed):
    scores = jnp.einsum("qhd,kd->hqk", queries, keys, preferred_element_type=f32) * HD**-0.5
    scores = jnp.where(allowed[None], scores, -1e30)
    top = jnp.max(scores, axis=-1, keepdims=True)
    exponent = jnp.exp(scores - top)
    totals = jnp.sum(exponent, axis=-1, keepdims=True)
    probs = exponent / totals
    mixed = jnp.einsum("hqk,kd->qhd", probs.astype(bf16), values, preferred_element_type=f32)
    return mixed, top + jnp.log(totals)


def attend_back(queries, keys, values, allowed, logs, mixed_grad):
    scores = jnp.einsum("qhd,kd->hqk", queries, keys, preferred_element_type=f32) * HD**-0.5
    scores = jnp.where(allowed[None], scores, -1e30)
    probs = jnp.exp(scores - logs)
    prob_grad = jnp.einsum("qhd,kd->hqk", mixed_grad, values, preferred_element_type=f32)
    inner = jnp.sum(probs * prob_grad, axis=-1, keepdims=True)
    score_grad = (probs * (prob_grad - inner)).astype(bf16)
    scale = HD**-0.5
    query_grad = jnp.einsum("hqk,kd->qhd", score_grad, keys, preferred_element_type=f32) * scale
    key_grad = jnp.einsum("hqk,qhd->kd", score_grad, queries, preferred_element_type=f32) * scale
    value_grad = jnp.einsum(
        "hqk,qhd->kd", probs.astype(bf16), mixed_grad, preferred_element_type=f32
    )
    return query_grad, key_grad, value_grad


def on_device(
    tokens,
    seq_lengths,
    token_places,
    attention_gain,
    query_weight,
    key_weight,
    value_weight,
    query_gain,
    key_gain,
    out_weight,
    feedforward_gain,
    gate_weight,
    up_weight,
    down_weight,
    cotangent,
):
    shard, replica = lax.axis_index("shard"), lax.axis_index("replica")
    x, z_low = shard // 2, shard % 2
    y, z, core = replica // 4, (replica // 2) % 2 * 2 + z_low, replica % 2
    where = (x, y, z, core, z_low)

    own_places = lax.dynamic_slice_in_dim(token_places[0], shard * 128, 128)
    first_length = seq_lengths[0, :1]
    notes = cat(
        [
            attention_gain,
            feedforward_gain,
            query_gain,
            key_gain,
            (first_length // 32).astype(bf16),
            (first_length % 32).astype(bf16),
            jnp.zeros((110,), bf16),
            (own_places // 32).astype(bf16),
            (own_places % 32).astype(bf16),
            jnp.zeros((384,), bf16),
        ]
    )
    notes = jnp.broadcast_to(notes[None], (16, 1024))
    packed = send(cat([tokens[0], notes]), regroup)
    gathered = gather_group(packed).reshape(8, 144, 1024)
    inputs_all = gathered[:, :128].reshape(1024, 1024)
    notes_all = gathered[:, 128]
    inputs = packed[:128].astype(f32)

    both = jnp.concatenate(
        [
            query_weight.reshape(128, 4, 2, 128),
            key_weight.reshape(128, 4, 2, 64),
            value_weight.reshape(128, 4, 2, 64),
        ],
        axis=3,
    )
    attention_slice = spread_columns(pick(both, core, 2), x, z_low)
    rows_held = cat([out_weight, down_weight])
    rows_got = cat([send(rows_held[:352], z_up_home), send(rows_held[352:], z_down_home)])
    rows_slot = jnp.where(core == z_low, rows_held, rows_got)
    out_slot, down_slot = rows_slot[:128], rows_slot[128:]
    both = jnp.concatenate(
        [gate_weight.reshape(128, 4, 2, 576), up_weight.reshape(128, 4, 2, 576)], axis=3
    )
    feed_slice = spread_columns(pick(both, core, 2), x, z_low)
    upstream_own = send(cotangent[0], regroup)
    upstream = gather_group(upstream_own)

    gains = notes_all[:, :384].reshape(2, 4, 384)
    gains = unroll(jnp.where(core == 0, gains, gains[::-1]), x, 1).transpose(1, 0, 2)
    gain_first = gains[..., :128].reshape(1024).astype(f32)
    gain_second = gains[..., 128:256].reshape(1024).astype(f32)
    gain_query = gains[..., 256:264].reshape(64).astype(f32)
    gain_key = gains[..., 264:272].reshape(64).astype(f32)
    length = (notes_all[0, 272].astype(f32) * 32 + notes_all[0, 273].astype(f32)).astype(jnp.int32)
    places = notes_all[:, 384:512].astype(f32) * 32 + notes_all[:, 512:640].astype(f32)
    places = places.reshape(1024).astype(jnp.int32)
    segment = (places >= length).astype(jnp.int32)
    cosine, sine = rope_tables(places - segment * length)
    allowed = (segment[:, None] == segment[None, :]) & (places[None, :] <= places[:, None])

    inputs_all = inputs_all.astype(f32)
    first_scale = rms_scale(inputs_all)
    first_normed = (inputs_all * first_scale * gain_first).astype(bf16)
    pre = matmul(first_normed, attention_slice)
    query_pre = pre[:, :128].reshape(1024, 2, HD)
    key_pre = pre[:, 128:192].reshape(1024, 1, HD)
    values = pre[:, 192:].astype(bf16)
    query_scale, key_scale = rms_scale(query_pre), rms_scale(key_pre)
    queries = rotate(query_pre * query_scale * gain_query, cosine, sine).astype(bf16)
    keys = rotate(key_pre * key_scale * gain_key, cosine, sine).astype(bf16)[:, 0]
    mixed, logs = attend(queries, keys, values, allowed)
    mixed = mixed.astype(bf16).reshape(1024, 128)
    middle = inputs + scatter_group(matmul(mixed, out_slot))

    second_scale = rms_scale(middle)
    second_normed = gather_group((middle * second_scale * gain_second).astype(bf16))
    pre = matmul(second_normed, feed_slice)
    gate, up = pre[:, :576], pre[:, 576:]
    sigmoid = jax.nn.sigmoid(gate)
    silu = gate * sigmoid
    hidden = (silu * up).astype(bf16)
    hidden_grad = matmul_nt(upstream, down_slot).astype(bf16).astype(f32)
    gate_grad = (hidden_grad * up * sigmoid * (1.0 + gate * (1.0 - sigmoid))).astype(bf16)
    up_grad = (hidden_grad * silu).astype(bf16)
    pre_grad = cat([gate_grad, up_grad], 1)
    second_grad = scatter_group(matmul_nt(pre_grad, feed_slice))
    result = middle + scatter_group(matmul(hidden, down_slot))
    feed_weight_grad = matmul_tn(second_normed, pre_grad)
    down_weight_grad = matmul_tn(upstream, hidden)
    feed_sum, down_sum = reduce_weights(feed_weight_grad, down_weight_grad, where)

    middle_norm_grad, second_gain_terms = norm_back(middle, second_scale, gain_second, second_grad)
    middle_grad = upstream_own.astype(f32) + middle_norm_grad
    second_gain_grad = jnp.sum(second_gain_terms, axis=0)
    branch_grad = gather_group(middle_grad.astype(bf16))
    mixed_grad = matmul_nt(branch_grad, out_slot).astype(bf16)
    out_weight_grad = matmul_tn(branch_grad, mixed)
    query_grad, key_grad, value_grad = attend_back(
        queries, keys, values, allowed, logs, mixed_grad.reshape(1024, 2, HD)
    )
    key_turned = unrotate(key_grad[:, None], cosine, sine)
    key_pre_grad, key_terms = norm_back(key_pre, key_scale, gain_key, key_turned)
    query_turned = unrotate(query_grad, cosine, sine)
    query_pre_grad, query_terms = norm_back(query_pre, query_scale, gain_query, query_turned)
    pre_grad = cat(
        [query_pre_grad.reshape(1024, 128), key_pre_grad.reshape(1024, HD), value_grad], 1
    ).astype(bf16)
    first_partial = matmul_nt(pre_grad, attention_slice)
    first_grad = scatter_group(first_partial)
    attention_weight_grad = matmul_tn(first_normed, pre_grad)
    first_gain_grad = jnp.sum(first_partial * (inputs_all * first_scale), axis=0)
    small = jnp.stack([jnp.sum(query_terms, axis=(0, 1)), jnp.sum(key_terms, axis=(0, 1))], 1)
    small = jnp.pad(small.reshape(8, 8, 2), ((0, 0), (0, 120), (0, 0))).reshape(1024, 2)
    extra = cat([first_gain_grad[:, None], second_gain_grad[:, None], small], 1)
    extra = jnp.pad(extra, ((0, 0), (0, 124)))
    attention_sum, out_sum = reduce_weights(
        cat([attention_weight_grad, extra], 1), out_weight_grad, where
    )
    own_scale = rms_scale(inputs)
    input_norm_grad, _ = norm_back(inputs, own_scale, gain_first, first_grad)
    input_grad = middle_grad + input_norm_grad

    attention_sum = attention_sum.astype(f32)
    gain_sums = jnp.sum(attention_sum[:, :, 256:260], axis=1)
    feed_sum = feed_sum.astype(f32)
    return (
        send(result.astype(bf16), regroup)[None],
        send(input_grad.astype(bf16), regroup).astype(f32)[None],
        gain_sums[:, 0],
        attention_sum[:, :, :128].reshape(128, 1024),
        attention_sum[:, :, 128:192].reshape(128, 512),
        attention_sum[:, :, 192:256].reshape(128, 512),
        gain_sums[:8, 2],
        gain_sums[:8, 3],
        out_sum.T.astype(f32),
        gain_sums[:, 1],
        feed_sum[:, :, :576].reshape(128, 4608),
        feed_sum[:, :, 576:].reshape(128, 4608),
        down_sum.T.astype(f32),
    )


def solution(mesh):
    placed = (
        P("replica", "shard", None),
        P("replica", None),
        P("replica", None),
        P("shard"),
        P("shard", None),
        P("shard", None),
        P("shard", None),
        P("shard"),
        P("shard"),
        P("shard", None),
        P("shard"),
        P("shard", None),
        P("shard", None),
        P("shard", None),
        P("replica", "shard", None),
    )
    return jax.shard_map(
        on_device,
        mesh=mesh,
        in_specs=placed,
        out_specs=(
            P("replica", "shard", None),
            P("replica", "shard", None),
            P("shard"),
            P("shard", None),
            P("shard", None),
            P("shard", None),
            P("shard"),
            P("shard"),
            P("shard", None),
            P("shard"),
            P("shard", None),
            P("shard", None),
            P("shard", None),
        ),
        check_vma=False,
    )
```

time: 1990 us -> 488 us (0.25)
  waiting for transfers between devices: 1650 us -> 123 us
  starting transfers between devices: 0.98 us -> 131 us
  matrix products: 153 us -> 39.2 us
  blocking collectives: 98.9 us -> 0 us
  local copies, waits for them, and re-layouts: 24.5 us -> 109 us
  other arithmetic: 36.3 us -> 71.2 us
    all_gather x9 -> x0, waiting for transfers between devices: 747 us -> none  [the longest x1 189 us: on_device(): lax.all_gather(gate_weight, 'shard', axis=0, tiled=True)]
    reduce_scatter x7 -> x0, waiting for transfers between devices: 743 us -> none  [the longest x1 193 us: on_device(): lax.psum_scatter(gate_weight_grad.astype(jnp.bfloat16), 'shard', scatter_...]
    ppermute x0 -> x84, starting transfers between devices: none -> 131 us  [send(): return lax.ppermute(values, AXES, moves)]
    ppermute x0 -> x84, waiting for transfers between devices: none -> 123 us  [send(): return lax.ppermute(values, AXES, moves)]
    psum x1 -> x0, waiting for transfers between devices: 91.1 us -> none  [on_device(): lax.psum(share_query.astype(jnp.bfloat16), 'replica').astype(jnp.float32)]
    dot_general x63 -> x10, matrix products: 101 us -> 18.3 us  [the longest x4 8.94 us: matmul(): return jnp.dot(left_side, right_side, preferred_element_type=f32)]
    unnamed x21 -> x0, waiting for transfers between devices: 72.8 us -> none
    psum x1 -> x0, blocking collectives: 36.5 us -> none  [on_device(): lax.psum(share_first.astype(jnp.bfloat16), 'replica').astype(jnp.float32)]
  transfers between devices with their start and end apart: 19 -> 84, of which waited for: 19 -> 34; matrix products, arithmetic and copies ran while one was open for 5% -> 36% of each run, Pallas kernels for 0% -> 0%
where the time goes in v1:
time: 488 us; the launch traced here: 481 us
  starting transfers between devices  131 us (27%)
  waiting for transfers between devices  123 us (25%)
  local copies, waits for them, and re-layouts  109 us (22%)
  other arithmetic  71.2 us (15%)
  matrix products  39.2 us (8%)
  between operations  7.17 us (1%)
    ppermute x84, starting transfers between devices, send(): return lax.ppermute(values, AXES, moves)  131 us
    ppermute x84, waiting for transfers between devices, send(): return lax.ppermute(values, AXES, moves)  123 us
    unnamed x213, local copies, waits for them, and re-layouts  46.7 us
    concatenate x17, other arithmetic, cat(): return jnp.concatenate(pieces, axis=axis)  14.6 us
    dot_general x4, matrix products, matmul_nt(): lax.dot_general(left_side, right_side, (((1,), (1,)), ((), ())), preferre...  12.5 us
  transfers between devices with their start and end apart: 84, of which 34 were waited for; matrix products, arithmetic and copies ran while one was open for 36% of the time, Pallas kernels for 0%

profile of v1, /device:TPU:1, one launch (start us, length us, event | category | flops | bytes accessed | tf_op | source)
XLA Modules:
  0.0 481.2 jit_solution(10088845660587777749)
XLA Ops:
  8.5 4.9 %collective-permute-start = (bf16[144,1024]{1,0:T(8,128)(2,1)S(1)}, bf16[144,1024]{1,0:T(8,128)(2,1)S(1)}, u32[]{:S(2)}, u32[]{:S(2)}) collective-permute-start(bf16[144,1024]{1,0:T(8,128)(2,1)S(1)} %pad_maximum_fusion.20), channel_id=1, source_target_pairs={{0,0},{1,16},{16,1},{17,17},{2,2},{3,18},{18,3},{19,19},{4,4},{5,2... | collective-permute-start | bytes 884744 | tf_op jit(solution)/shard_map/ppermute | solution.py:53
  21.4 3.5 collective-permute-start.2
  26.3 3.3 collective-permute-start.30
  29.7 8.6 %collective-permute-done.5 = bf16[128,256]{1,0:T(8,128)(2,1)S(1)} collective-permute-done((bf16[128,256]{1,0:T(8,128)(2,1)S(1)}, bf16[128,256]{1,0:T(8,128)(2,1)S(1)}, u32[]{:S(2)}, u32[]{:S(2)}) %collective-permute-start.5) | collective-permute-done | bytes 65568 | tf_op jit(solution)/shard_map/ppermute | solution.py:53
  57.8 10.7 %collective-permute-done.10 = bf16[352,1024]{1,0:T(8,128)(2,1)S(1)} collective-permute-done((bf16[352,1024]{1,0:T(8,128)(2,1)}, bf16[352,1024]{1,0:T(8,128)(2,1)S(1)}, u32[]{:S(2)}, u32[]{:S(2)}) %collective-permute-start.10) | collective-permute-done | bytes 720928 | tf_op jit(solution)/shard_map/ppermute | solution.py:53
  112.4 4.1 collective-permute-done.20
  116.5 3.3 collective-permute-start.31
  123.1 7.8 %collective-permute-done.31 = bf16[128,1024]{1,0:T(8,128)(2,1)S(1)} collective-permute-done((bf16[128,1024]{1,0:T(8,128)(2,1)}, bf16[128,1024]{1,0:T(8,128)(2,1)S(1)}, u32[]{:S(2)}, u32[]{:S(2)}) %collective-permute-start.31) | collective-permute-done | bytes 262176 | tf_op jit(solution)/shard_map/ppermute | solution.py:53
  134.5 3.5 collective-permute-start.15
  159.1 5.7 %collective-permute-done.17 = bf16[128,1024]{1,0:T(8,128)(2,1)S(1)} collective-permute-done((bf16[128,1024]{1,0:T(8,128)(2,1)S(1)}, bf16[128,1024]{1,0:T(8,128)(2,1)S(1)}, u32[]{:S(2)}, u32[]{:S(2)}) %collective-permute-start.17) | collective-permute-done | bytes 262176 | tf_op jit(solution)/shard_map/ppermute | solution.py:53
  183.5 4.6 fusion.158
  198.2 3.3 fusion.159
  212.3 8.8 %collective-permute-done.67 = bf16[4,4,8,1728]{3,2,1,0:T(8,128)(2,1)S(1)} collective-permute-done((bf16[4,4,8,1728]{3,2,1,0:T(8,128)(2,1)S(1)}, bf16[4,4,8,1728]{3,2,1,0:T(8,128)(2,1)S(1)}, u32[]{:S(2)}, u32[]{:S(2)}) %collective-permute-start.67) | collective-permute-done | bytes 442400 | tf_op jit(solution)/shard_map/ppermute | solution.py:53
  221.3 3.1 collective-permute-start.68
  234.4 6.0 %collective-permute-done.37 = bf16[128,1024]{1,0:T(8,128)(2,1)S(1)} collective-permute-done((bf16[128,1024]{1,0:T(8,128)(2,1)S(1)}, bf16[128,1024]{1,0:T(8,128)(2,1)S(1)}, u32[]{:S(2)}, u32[]{:S(2)}) %collective-permute-start.37) | collective-permute-done | bytes 262176 | tf_op jit(solution)/shard_map/ppermute | solution.py:53
  242.5 3.4 collective-permute-done.66
  249.1 3.4 collective-permute-done.69
  256.6 3.3 collective-permute-start.73
  280.6 6.0 %collective-permute-start.42 = (bf16[512,1024]{1,0:T(8,128)(2,1)S(1)}, bf16[512,1024]{1,0:T(8,128)(2,1)S(1)}, u32[]{:S(2)}, u32[]{:S(2)}) collective-permute-start(bf16[512,1024]{1,0:T(8,128)(2,1)S(1)} %pad_maximum_fusion.10), channel_id=1, source_target_pairs={{0,1},{1,0},{16,17},{17,16},{2,3},{3,2},{18,19},{19,18},{4,5},{5,4... | collective-permute-start | bytes 3145736 | tf_op jit(solution)/shard_map/ppermute | solution.py:53
  291.5 11.5 %collective-permute-done.80 = bf16[128,2304]{1,0:T(8,128)(2,1)S(1)} collective-permute-done((bf16[128,2304]{1,0:T(8,128)(2,1)S(1)}, bf16[128,2304]{1,0:T(8,128)(2,1)S(1)}, u32[]{:S(2)}, u32[]{:S(2)}) %collective-permute-start.80) | collective-permute-done | bytes 589856 | tf_op jit(solution)/shard_map/ppermute | solution.py:53
  306.1 5.9 %collective-permute-done.81 = bf16[64,2304]{1,0:T(8,128)(2,1)S(1)} collective-permute-done((bf16[64,2304]{1,0:T(8,128)(2,1)S(1)}, bf16[64,2304]{1,0:T(8,128)(2,1)S(1)}, u32[]{:S(2)}, u32[]{:S(2)}) %collective-permute-start.81) | collective-permute-done | bytes 294944 | tf_op jit(solution)/shard_map/ppermute | solution.py:53
  337.3 4.5 multiply_convert_fusion
  353.7 6.5 %collective-permute-done.49 = bf16[8,4,8,512]{3,2,1,0:T(8,128)(2,1)S(1)} collective-permute-done((bf16[8,4,8,512]{3,2,1,0:T(8,128)(2,1)S(1)}, bf16[8,4,8,512]{3,2,1,0:T(8,128)(2,1)S(1)}, u32[]{:S(2)}, u32[]{:S(2)}) %collective-permute-start.49) | collective-permute-done | bytes 262176 | tf_op jit(solution)/shard_map/ppermute | solution.py:53
  386.6 4.0 collective-permute-done.61
  393.9 10.5 %collective-permute-start.63 = (bf16[4,4,32,384]{3,2,1,0:T(8,128)(2,1)}, bf16[4,4,32,384]{3,2,1,0:T(8,128)(2,1)}, u32[]{:S(2)}, u32[]{:S(2)}) collective-permute-start(bf16[4,4,32,384]{3,2,1,0:T(8,128)(2,1)} %slice.433), channel_id=1, source_target_pairs={{0,1},{1,0},{16,17},{17,16},{2,3},{3,2},{18,19},{19,18},{4,5},{5,4... | collective-permute-start | bytes 1179656 | tf_op jit(solution)/shard_map/ppermute | solution.py:53
  433.0 3.4 select_bitcast_fusion
  444.6 5.3 %collective-permute-done.27 = bf16[128,1024]{1,0:T(8,128)(2,1)S(1)} collective-permute-done((bf16[128,1024]{1,0:T(8,128)(2,1)S(1)}, bf16[128,1024]{1,0:T(8,128)(2,1)S(1)}, u32[]{:S(2)}, u32[]{:S(2)}) %collective-permute-start.27) | collective-permute-done | bytes 262176 | tf_op jit(solution)/shard_map/ppermute | solution.py:53
  457.3 3.1 fusion.152
  464.5 3.2 copy.288
  467.7 3.2 copy.295
  472.7 3.6 copy.290
  476.3 3.1 copy.297
  (556 shorter events, 308.7 us)
Async XLA Ops:
  21.4 18.2 %collective-permute-start.3 = (bf16[144,1024]{1,0:T(8,128)(2,1)S(1)}, bf16[144,1024]{1,0:T(8,128)(2,1)S(1)}, u32[]{:S(2)}, u32[]{:S(2)}) collective-permute-start(bf16[144,1024]{1,0:T(8,128)(2,1)S(1)} %collective-permute-done), channel_id=1, source_target_pairs={{0,32},{1,33},{16,48},{17,49},{2,34},{3,35},{18,50},{19,51},{4,36}... | collective-permute-start | bytes 884744 | tf_op jit(solution)/shard_map/ppermute | solution.py:53
  21.4 21.2 %collective-permute-start.2 = (bf16[144,1024]{1,0:T(8,128)(2,1)S(1)}, bf16[144,1024]{1,0:T(8,128)(2,1)S(1)}, u32[]{:S(2)}, u32[]{:S(2)}) collective-permute-start(bf16[144,1024]{1,0:T(8,128)(2,1)S(1)} %collective-permute-done), channel_id=1, source_target_pairs={{0,64},{1,65},{16,80},{17,81},{2,66},{3,67},{18,82},{19,83},{4,68}... | collective-permute-start | bytes 884744 | tf_op jit(solution)/shard_map/ppermute | solution.py:53
  25.0 20.1 %collective-permute-start.1 = (bf16[144,1024]{1,0:T(8,128)(2,1)S(1)}, bf16[144,1024]{1,0:T(8,128)(2,1)S(1)}, u32[]{:S(2)}, u32[]{:S(2)}) collective-permute-start(bf16[144,1024]{1,0:T(8,128)(2,1)S(1)} %collective-permute-done), channel_id=1, source_target_pairs={{0,96},{1,97},{16,112},{17,113},{2,98},{3,99},{18,114},{19,115},{4... | collective-permute-start | bytes 884744 | tf_op jit(solution)/shard_map/ppermute | solution.py:53
  26.3 83.3 %collective-permute-start.30 = (bf16[128,1024]{1,0:T(8,128)(2,1)}, bf16[128,1024]{1,0:T(8,128)(2,1)}, u32[]{:S(2)}, u32[]{:S(2)}) collective-permute-start(bf16[128,1024]{1,0:T(8,128)(2,1)} %bitcast.561), channel_id=1, source_target_pairs={{0,0},{1,16},{16,1},{17,17},{2,2},{3,18},{18,3},{19,19},{4,4},{5,2... | collective-permute-start | bytes 786440 | tf_op jit(solution)/shard_map/ppermute | solution.py:53
  38.3 19.5 %collective-permute-start.11 = (bf16[352,1024]{1,0:T(8,128)(2,1)}, bf16[352,1024]{1,0:T(8,128)(2,1)}, u32[]{:S(2)}, u32[]{:S(2)}) collective-permute-start(bf16[352,1024]{1,0:T(8,128)(2,1)} %slice.309), channel_id=1, source_target_pairs={{0,18},{17,1},{2,16},{19,3},{4,22},{21,5},{6,20},{23,7},{8,26},{25... | collective-permute-start | bytes 2162696 | tf_op jit(solution)/shard_map/ppermute | solution.py:53
  46.2 25.2 %collective-permute-start.4 = (bf16[576,1024]{1,0:T(8,128)(2,1)}, bf16[576,1024]{1,0:T(8,128)(2,1)}, u32[]{:S(2)}, u32[]{:S(2)}) collective-permute-start(bf16[576,1024]{1,0:T(8,128)(2,1)} %pad_maximum_fusion.5), channel_id=1, source_target_pairs={{0,1},{1,0},{16,17},{17,16},{2,3},{3,2},{18,19},{19,18},{4,5},{5,4... | collective-permute-start | bytes 3538952 | tf_op jit(solution)/shard_map/ppermute | solution.py:53
  96.8 34.2 %collective-permute-start.12 = (bf16[4,128,1024]{2,1,0:T(8,128)(2,1)}, bf16[4,128,1024]{2,1,0:T(8,128)(2,1)}, u32[]{:S(2)}, u32[]{:S(2)}) collective-permute-start(bf16[4,128,1024]{2,1,0:T(8,128)(2,1)} %bitcast.36), channel_id=1, source_target_pairs={{0,1},{1,0},{16,17},{17,16},{2,3},{3,2},{18,19},{19,18},{4,5},{5,4... | collective-permute-start | bytes 3145736 | tf_op jit(solution)/shard_map/ppermute | solution.py:53
  100.7 15.8 %collective-permute-start.20 = (bf16[128,1152]{1,0:T(8,128)(2,1)}, bf16[128,1152]{1,0:T(8,128)(2,1)}, u32[]{:S(2)}, u32[]{:S(2)}) collective-permute-start(bf16[128,1152]{1,0:T(8,128)(2,1)} %bitcast.520), channel_id=1, source_target_pairs={{0,96},{1,97},{16,112},{17,113},{2,98},{3,99},{18,114},{19,115},{4... | collective-permute-start | bytes 884744 | tf_op jit(solution)/shard_map/ppermute | solution.py:53
  104.9 16.1 %collective-permute-start.21 = (bf16[128,1152]{1,0:T(8,128)(2,1)}, bf16[128,1152]{1,0:T(8,128)(2,1)}, u32[]{:S(2)}, u32[]{:S(2)}) collective-permute-start(bf16[128,1152]{1,0:T(8,128)(2,1)} %bitcast.519), channel_id=1, source_target_pairs={{0,64},{1,65},{16,80},{17,81},{2,66},{3,67},{18,82},{19,83},{4,68}... | collective-permute-start | bytes 884744 | tf_op jit(solution)/shard_map/ppermute | solution.py:53
  109.6 29.6 %collective-permute-start.33 = (bf16[128,1024]{1,0:T(8,128)(2,1)}, bf16[128,1024]{1,0:T(8,128)(2,1)S(1)}, u32[]{:S(2)}, u32[]{:S(2)}) collective-permute-start(bf16[128,1024]{1,0:T(8,128)(2,1)} %collective-permute-done.30), channel_id=1, source_target_pairs={{0,32},{1,33},{16,48},{17,49},{2,34},{3,35},{18,50},{19,51},{4,36}... | collective-permute-start | bytes 786440 | tf_op jit(solution)/shard_map/ppermute | solution.py:53
  121.0 17.0 %collective-permute-start.32 = (bf16[128,1024]{1,0:T(8,128)(2,1)}, bf16[128,1024]{1,0:T(8,128)(2,1)S(1)}, u32[]{:S(2)}, u32[]{:S(2)}) collective-permute-start(bf16[128,1024]{1,0:T(8,128)(2,1)} %collective-permute-done.30), channel_id=1, source_target_pairs={{0,64},{1,65},{16,80},{17,81},{2,66},{3,67},{18,82},{19,83},{4,68}... | collective-permute-start | bytes 786440 | tf_op jit(solution)/shard_map/ppermute | solution.py:53
  122.0 33.0 %collective-permute-start.23 = (bf16[2,128,1152]{2,1,0:T(8,128)(2,1)S(1)}, bf16[2,128,1152]{2,1,0:T(8,128)(2,1)S(1)}, u32[]{:S(2)}, u32[]{:S(2)}) collective-permute-start(bf16[2,128,1152]{2,1,0:T(8,128)(2,1)S(1)} %pad_maximum_fusion.13), channel_id=1, source_target_pairs={{0,16},{1,17},{16,2},{17,3},{2,18},{3,19},{18,0},{19,1},{4,20},{5,... | collective-permute-start | bytes 1769480 | tf_op jit(solution)/shard_map/ppermute | solution.py:53
  139.2 16.1 %collective-permute-start.24 = (bf16[2,128,1152]{2,1,0:T(8,128)(2,1)S(1)}, bf16[2,128,1152]{2,1,0:T(8,128)(2,1)S(1)}, u32[]{:S(2)}, u32[]{:S(2)}) collective-permute-start(bf16[2,128,1152]{2,1,0:T(8,128)(2,1)S(1)} %pad_maximum_fusion.14), channel_id=1, source_target_pairs={{0,18},{1,19},{16,0},{17,1},{2,16},{3,17},{18,2},{19,3},{4,22},{5,... | collective-permute-start | bytes 1769480 | tf_op jit(solution)/shard_map/ppermute | solution.py:53
  143.3 28.8 %collective-permute-start.34 = (bf16[512,1024]{1,0:T(8,128)(2,1)S(1)}, bf16[512,1024]{1,0:T(8,128)(2,1)S(1)}, u32[]{:S(2)}, u32[]{:S(2)}) collective-permute-start(bf16[512,1024]{1,0:T(8,128)(2,1)S(1)} %pad_maximum_fusion.9), channel_id=1, source_target_pairs={{0,1},{1,0},{16,17},{17,16},{2,3},{3,2},{18,19},{19,18},{4,5},{5,4... | collective-permute-start | bytes 3145736 | tf_op jit(solution)/shard_map/ppermute | solution.py:53
  205.6 19.0 %collective-permute-start.35 = (bf16[4,128,1024]{2,1,0:T(8,128)(2,1)}, bf16[4,128,1024]{2,1,0:T(8,128)(2,1)}, u32[]{:S(2)}, u32[]{:S(2)}) collective-permute-start(bf16[4,128,1024]{2,1,0:T(8,128)(2,1)} %bitcast.67), channel_id=1, source_target_pairs={{0,1},{1,0},{16,17},{17,16},{2,3},{3,2},{18,19},{19,18},{4,5},{5,4... | collective-permute-start | bytes 3145736 | tf_op jit(solution)/shard_map/ppermute | solution.py:53
  208.5 16.0 %collective-permute-start.65 = (bf16[4,4,8,1728]{3,2,1,0:T(8,128)(2,1)S(1)}, bf16[4,4,8,1728]{3,2,1,0:T(8,128)(2,1)S(1)}, u32[]{:S(2)}, u32[]{:S(2)}) collective-permute-start(bf16[4,4,8,1728]{3,2,1,0:T(8,128)(2,1)S(1)} %get-tuple-element.147), channel_id=1, source_target_pairs={{0,4},{1,5},{16,20},{17,21},{2,6},{3,7},{18,22},{19,23},{4,8},{5,9... | collective-permute-start | bytes 1327112 | tf_op jit(solution)/shard_map/ppermute | solution.py:53
  211.3 18.1 %collective-permute-start.25 = (bf16[4,128,1024]{2,1,0:T(8,128)(2,1)S(1)}, bf16[4,128,1024]{2,1,0:T(8,128)(2,1)S(1)}, u32[]{:S(2)}, u32[]{:S(2)}) collective-permute-start(bf16[4,128,1024]{2,1,0:T(8,128)(2,1)S(1)} %bitcast.490), channel_id=1, source_target_pairs={{0,1},{1,0},{16,17},{17,16},{2,3},{3,2},{18,19},{19,18},{4,5},{5,4... | collective-permute-start | bytes 3145736 | tf_op jit(solution)/shard_map/ppermute | solution.py:53
  221.3 21.2 %collective-permute-start.68 = (bf16[8,4,8,1728]{3,2,1,0:T(8,128)(2,1)S(1)}, bf16[8,4,8,1728]{3,2,1,0:T(8,128)(2,1)S(1)}, u32[]{:S(2)}, u32[]{:S(2)}) collective-permute-start(bf16[8,4,8,1728]{3,2,1,0:T(8,128)(2,1)S(1)} %pad_maximum_fusion.12), channel_id=1, source_target_pairs={{0,12},{1,13},{16,28},{17,29},{2,14},{3,15},{18,30},{19,31},{4,0},... | collective-permute-start | bytes 2654216 | tf_op jit(solution)/shard_map/ppermute | solution.py:53
  224.6 21.3 %collective-permute-start.66 = (bf16[8,4,8,1728]{3,2,1,0:T(8,128)(2,1)S(1)}, bf16[8,4,8,1728]{3,2,1,0:T(8,128)(2,1)S(1)}, u32[]{:S(2)}, u32[]{:S(2)}) collective-permute-start(bf16[8,4,8,1728]{3,2,1,0:T(8,128)(2,1)S(1)} %pad_maximum_fusion.11), channel_id=1, source_target_pairs={{0,4},{1,5},{16,20},{17,21},{2,6},{3,7},{18,22},{19,23},{4,8},{5,9... | collective-permute-start | bytes 2654216 | tf_op jit(solution)/shard_map/ppermute | solution.py:53
  269.8 16.9 %collective-permute-start.77 = (bf16[32,2304]{1,0:T(8,128)(2,1)S(1)}, bf16[32,2304]{1,0:T(8,128)(2,1)S(1)}, u32[]{:S(2)}, u32[]{:S(2)}) collective-permute-start(bf16[32,2304]{1,0:T(8,128)(2,1)S(1)} %get-tuple-element.179), channel_id=1, source_target_pairs={{0,16},{1,17},{16,2},{17,3},{2,18},{3,19},{18,0},{19,1},{4,20},{5,... | collective-permute-start | bytes 442376 | tf_op jit(solution)/shard_map/ppermute | solution.py:53
  276.7 167.8 %collective-permute-start.26 = (bf16[128,1024]{1,0:T(8,128)(2,1)}, bf16[128,1024]{1,0:T(8,128)(2,1)}, u32[]{:S(2)}, u32[]{:S(2)}) collective-permute-start(bf16[128,1024]{1,0:T(8,128)(2,1)} %get-tuple-element.141), channel_id=1, source_target_pairs={{0,32},{1,33},{16,48},{17,49},{2,34},{3,35},{18,50},{19,51},{4,36}... | collective-permute-start | bytes 786440 | tf_op jit(solution)/shard_map/ppermute | solution.py:53
  277.2 167.4 %collective-permute-start.28 = (bf16[128,1024]{1,0:T(8,128)(2,1)}, bf16[128,1024]{1,0:T(8,128)(2,1)}, u32[]{:S(2)}, u32[]{:S(2)}) collective-permute-start(bf16[128,1024]{1,0:T(8,128)(2,1)} %get-tuple-element.142), channel_id=1, source_target_pairs={{0,96},{1,97},{16,112},{17,113},{2,98},{3,99},{18,114},{19,115},{4... | collective-permute-start | bytes 786440 | tf_op jit(solution)/shard_map/ppermute | solution.py:53
  280.6 32.5 %collective-permute-start.42 = (bf16[512,1024]{1,0:T(8,128)(2,1)S(1)}, bf16[512,1024]{1,0:T(8,128)(2,1)S(1)}, u32[]{:S(2)}, u32[]{:S(2)}) collective-permute-start(bf16[512,1024]{1,0:T(8,128)(2,1)S(1)} %pad_maximum_fusion.10), channel_id=1, source_target_pairs={{0,1},{1,0},{16,17},{17,16},{2,3},{3,2},{18,19},{19,18},{4,5},{5,4... | collective-permute-start | bytes 3145736 | tf_op jit(solution)/shard_map/ppermute | solution.py:53
  286.7 16.2 %collective-permute-start.80 = (bf16[128,2304]{1,0:T(8,128)(2,1)S(1)}, bf16[128,2304]{1,0:T(8,128)(2,1)S(1)}, u32[]{:S(2)}, u32[]{:S(2)}) collective-permute-start(bf16[128,2304]{1,0:T(8,128)(2,1)S(1)} %bitcast.502), channel_id=1, source_target_pairs={{0,4},{1,5},{16,20},{17,21},{2,6},{3,7},{18,22},{19,23},{4,8},{5,9... | collective-permute-start | bytes 1769480 | tf_op jit(solution)/shard_map/ppermute | solution.py:53
  286.8 16.3 %collective-permute-start.78 = (bf16[128,2304]{1,0:T(8,128)(2,1)S(1)}, bf16[128,2304]{1,0:T(8,128)(2,1)S(1)}, u32[]{:S(2)}, u32[]{:S(2)}) collective-permute-start(bf16[128,2304]{1,0:T(8,128)(2,1)S(1)} %bitcast.503), channel_id=1, source_target_pairs={{0,12},{1,13},{16,28},{17,29},{2,14},{3,15},{18,30},{19,31},{4,0},... | collective-permute-start | bytes 1769480 | tf_op jit(solution)/shard_map/ppermute | solution.py:53
  392.4 17.7 %collective-permute-start.64 = (bf16[4,4,32,256]{3,2,1,0:T(8,128)(2,1)S(1)}, bf16[4,4,32,256]{3,2,1,0:T(8,128)(2,1)S(1)}, u32[]{:S(2)}, u32[]{:S(2)}) collective-permute-start(bf16[4,4,32,256]{3,2,1,0:T(8,128)(2,1)S(1)} %slice.441), channel_id=1, source_target_pairs={{0,1},{17,16},{2,3},{19,18},{4,5},{21,20},{6,7},{23,22},{8,9},{25,... | collective-permute-start | bytes 786440 | tf_op jit(solution)/shard_map/ppermute | solution.py:53
  393.9 21.3 %collective-permute-start.63 = (bf16[4,4,32,384]{3,2,1,0:T(8,128)(2,1)}, bf16[4,4,32,384]{3,2,1,0:T(8,128)(2,1)}, u32[]{:S(2)}, u32[]{:S(2)}) collective-permute-start(bf16[4,4,32,384]{3,2,1,0:T(8,128)(2,1)} %slice.433), channel_id=1, source_target_pairs={{0,1},{1,0},{16,17},{17,16},{2,3},{3,2},{18,19},{19,18},{4,5},{5,4... | collective-permute-start | bytes 1179656 | tf_op jit(solution)/shard_map/ppermute | solution.py:53
  406.1 23.7 %collective-permute-start.83 = (bf16[4,4,32,1152]{3,2,1,0:T(8,128)(2,1)}, bf16[4,4,32,1152]{3,2,1,0:T(8,128)(2,1)}, u32[]{:S(2)}, u32[]{:S(2)}) collective-permute-start(bf16[4,4,32,1152]{3,2,1,0:T(8,128)(2,1)} %get-tuple-element.115), channel_id=1, source_target_pairs={{0,1},{17,16},{2,3},{19,18},{4,5},{21,20},{6,7},{23,22},{8,9},{25,... | collective-permute-start | bytes 3538952 | tf_op jit(solution)/shard_map/ppermute | solution.py:53
  410.0 17.4 %collective-permute-start.43 = (bf16[4,128,1024]{2,1,0:T(8,128)(2,1)}, bf16[4,128,1024]{2,1,0:T(8,128)(2,1)}, u32[]{:S(2)}, u32[]{:S(2)}) collective-permute-start(bf16[4,128,1024]{2,1,0:T(8,128)(2,1)} %bitcast.84), channel_id=1, source_target_pairs={{0,1},{1,0},{16,17},{17,16},{2,3},{3,2},{18,19},{19,18},{4,5},{5,4... | collective-permute-start | bytes 3145736 | tf_op jit(solution)/shard_map/ppermute | solution.py:53
  415.2 17.4 %collective-permute-start.82 = (bf16[4,4,32,1152]{3,2,1,0:T(8,128)(2,1)}, bf16[4,4,32,1152]{3,2,1,0:T(8,128)(2,1)}, u32[]{:S(2)}, u32[]{:S(2)}) collective-permute-start(bf16[4,4,32,1152]{3,2,1,0:T(8,128)(2,1)} %get-tuple-element.116), channel_id=1, source_target_pairs={{0,1},{1,0},{16,17},{17,16},{2,3},{3,2},{18,19},{19,18},{4,5},{5,4... | collective-permute-start | bytes 3538952 | tf_op jit(solution)/shard_map/ppermute | solution.py:53
  451.7 27.7 %collective-permute-start.47 = (bf16[128,1024]{1,0:T(8,128)(2,1)S(1)}, bf16[128,1024]{1,0:T(8,128)(2,1)S(1)}, u32[]{:S(2)}, u32[]{:S(2)}) collective-permute-start(bf16[128,1024]{1,0:T(8,128)(2,1)S(1)} %get-tuple-element.156), channel_id=1, source_target_pairs={{0,0},{1,16},{16,1},{17,17},{2,2},{3,18},{18,3},{19,19},{4,4},{5,2... | collective-permute-start | bytes 786440 | tf_op jit(solution)/shard_map/ppermute | solution.py:53
  454.6 24.8 %collective-permute-start.29 = (bf16[128,1024]{1,0:T(8,128)(2,1)S(1)}, bf16[128,1024]{1,0:T(8,128)(2,1)S(1)}, u32[]{:S(2)}, u32[]{:S(2)}) collective-permute-start(bf16[128,1024]{1,0:T(8,128)(2,1)S(1)} %get-tuple-element.157), channel_id=1, source_target_pairs={{0,0},{1,16},{16,1},{17,17},{2,2},{3,18},{18,3},{19,19},{4,4},{5,2... | collective-permute-start | bytes 786440 | tf_op jit(solution)/shard_map/ppermute | solution.py:53
  (140 other events, 1076.5 us)

commit v2 on v1

v2 whole, which is shorter than its diff:
```python
import jax
import jax.numpy as jnp
from jax import lax
from jax.experimental import pallas as pl
from jax.experimental.pallas import tpu as pltpu
from jax.sharding import PartitionSpec as P

HEADS = 16
KV_HEADS = 8
HD = 64
AXES = ("shard", "replica")

norm_eps = 1e-05
rope_base = 1000000.0
bf16 = jnp.bfloat16
f32 = jnp.float32


def place(x, y, z, core):
    return ((x % 4) * 2 + (z % 4) % 2) * 16 + ((y % 4) * 2 + (z % 4) // 2) * 2 + core % 2


def pairs(move, keep=lambda x, y, z, c: True):
    found = []
    for x in range(4):
        for y in range(4):
            for z in range(4):
                for c in range(2):
                    if keep(x, y, z, c):
                        found.append((place(x, y, z, c), place(*move(x, y, z, c))))
    return found


def home(x, y, z, c):
    return c == z % 2


x_up = pairs(lambda x, y, z, c: (x + 1, y, z, c))
x_down = pairs(lambda x, y, z, c: (x - 1, y, z, c))
x_far = pairs(lambda x, y, z, c: (x + 2, y, z, c))
y_up = pairs(lambda x, y, z, c: (x, y + 1, z, c))
y_down = pairs(lambda x, y, z, c: (x, y - 1, z, c))
y_far = pairs(lambda x, y, z, c: (x, y + 2, z, c))
z_up = pairs(lambda x, y, z, c: (x, y, z + 1, c))
z_down = pairs(lambda x, y, z, c: (x, y, z - 1, c))
z_far = pairs(lambda x, y, z, c: (x, y, z + 2, c))
z_up_home = pairs(lambda x, y, z, c: (x, y, z + 1, c), home)
z_down_home = pairs(lambda x, y, z, c: (x, y, z - 1, c), home)
other_core = pairs(lambda x, y, z, c: (x, y, z, 1 - c))
from_home = pairs(lambda x, y, z, c: (x, y, z, 1 - c), home)
regroup = pairs(lambda x, y, z, c: (x, y, (z // 2) * 2 + c, z % 2))


def send(values, moves):
    return lax.ppermute(values, AXES, moves)


def cat(pieces, axis=0):
    return jnp.concatenate(pieces, axis=axis)


def pick(values, index, axis):
    return lax.dynamic_index_in_dim(values, index, axis, keepdims=False)


def unroll(values, index, axis):
    doubled = cat([values, values], axis)
    return lax.dynamic_slice_in_dim(doubled, (4 - index) % 4, 4, axis)


x_rings = [
    [place(x, y, z, core) for x in range(4)] for core in range(2) for y in range(4) for z in range(4)
]
planes = [
    [place(x, y, z, core) for y in range(4) for z in range(4)] for x in range(4) for core in range(2)
]
x_groups = [
    [place(x, y, z, core) for x in range(4) for core in range(2)]
    for y in range(4)
    for z in range(4)
]


def join(*values):
    return lax.optimization_barrier(values)


def exchange(values, groups):
    return lax.all_to_all(values, AXES, 0, 0, axis_index_groups=groups)


def gather_half(block):
    return exchange(jnp.broadcast_to(block[None], (4, *block.shape)), x_rings)


def scatter_sums(own, got):
    summed = (own + got.astype(f32)).astype(bf16).reshape(4, 128, own.shape[1])
    return exchange(summed, x_rings)


def add_up(parts):
    return jnp.sum(parts.astype(f32), axis=0)


def units(values, rows, columns):
    height, width = values.shape
    return values.reshape(rows, height // rows // 8, 8, columns, width // columns // 128, 128)


def rows_for_planes(by_row):
    grid = by_row.astype(bf16).reshape(8, 4, 4, 8, by_row.shape[1] // 128, 128)
    return grid.transpose(1, 2, 0, 4, 3, 5)


def block_for_planes(by_block):
    return units(by_block.astype(bf16), 4, 4).transpose(0, 3, 1, 4, 2, 5)


def exchange_rows(by_row):
    return exchange(by_row.reshape(4, 2, *by_row.shape[1:]), x_rings)


def return_planes(got, by_block):
    both = [cat([got[:, parity].reshape(-1, 128), by_block.reshape(-1, 128)]) for parity in range(2)]
    return exchange(jnp.stack(both * 8), planes)


def exchange_x(by_row, x):
    own = by_row.reshape(4, 2, *by_row.shape[1:])
    near = [pick(own, (x + step) % 4, 0) for step in range(4)]
    return jnp.stack([near[0]] + send_x(*near[1:])[::-1])


def send_ring(pieces, up, down, far):
    low = [piece.astype(bf16) for piece in pieces[1:]]
    return [send(low[0], up), send(low[1], far), send(low[2], down)]


def gather_z(got, by_block, z_low):
    same = cat([pick(got, z_low, 1).reshape(-1, 128), by_block.reshape(-1, 128)])
    odd = cat([pick(got, 1 - z_low, 1).reshape(-1, 128), by_block.reshape(-1, 128)])
    return jnp.stack([same, send(odd, z_down), send(same, z_far), send(odd, z_up)])


def gather_y(block):
    return jnp.stack([block, send(block, y_down), send(block, y_far), send(block, y_up)])


def send_x(first, second, third):
    return [send(first, x_up), send(second, x_far), send(third, x_down)]


def gather_x(block):
    return [block, send(block, x_down), send(block, x_far), send(block, x_up)]


def quarter(values, step):
    return values[step * 128 : (step + 1) * 128]


def scatter_parts(own, got):
    sums = [quarter(own, step) + quarter(got, step).astype(f32) for step in range(4)]
    return sums[0], [part.astype(bf16) for part in sums[1:]]


def turn_back(rows, x):
    blocks = rows.reshape(4, 128, rows.shape[1])
    return lax.dynamic_slice_in_dim(cat([blocks, blocks]), x, 4, 0).reshape(rows.shape)


def whole(count):
    return [pl.BlockSpec(memory_space=pltpu.VMEM)] * count


def spot(values):
    return jnp.stack(values).astype(jnp.int32)


def call(kernel, scalars, arrays, outs, scratch=(), limit=40, flops=0):
    size = sum(a.size * a.dtype.itemsize for a in arrays)
    return pl.pallas_call(
        kernel,
        out_shape=[jax.ShapeDtypeStruct(shape, kind) for shape, kind in outs],
        in_specs=[pl.BlockSpec(memory_space=pltpu.SMEM)] + whole(len(arrays)),
        out_specs=whole(len(outs)),
        scratch_shapes=list(scratch),
        compiler_params=pltpu.CompilerParams(vmem_limit_bytes=limit * 2**20),
        cost_estimate=pl.CostEstimate(flops=flops, bytes_accessed=size, transcendentals=0),
    )(scalars, *arrays)


def rms_scale(values):
    return lax.rsqrt(jnp.mean(values * values, axis=-1, keepdims=True) + norm_eps)


def norm_back(inputs, scale_rows, gain_vector, upstream):
    normed = inputs * scale_rows
    scaled = upstream * gain_vector
    entry_grad = scale_rows * (scaled - normed * jnp.mean(scaled * normed, axis=-1, keepdims=True))
    return (entry_grad, upstream * normed)


def matmul(left_side, right_side):
    return jnp.dot(left_side, right_side, preferred_element_type=f32)


def matmul_tn(left_side, right_side):
    return lax.dot_general(
        left_side, right_side, (((0,), (0,)), ((), ())), preferred_element_type=f32
    )


def matmul_nt(left_side, right_side):
    return lax.dot_general(
        left_side, right_side, (((1,), (1,)), ((), ())), preferred_element_type=f32
    )


def columns_kernel(spot_ref, q_ref, k_ref, v_ref, gate_ref, up_ref, packed_ref, out_ref, feed_ref):
    core = spot_ref[0]
    for at in range(4):
        out_ref[at, :, :1024] = packed_ref[...]
        out_ref[at, 128:, 1024:] = jnp.zeros((16, 256), bf16)
        out_ref[at, :128, 1024:1152] = jnp.where(
            core == 0,
            q_ref[:, at * 256 : at * 256 + 128],
            q_ref[:, at * 256 + 128 : at * 256 + 256],
        )
        for ref, low in ((k_ref, 1152), (v_ref, 1216)):
            pair = ref[:, at * 128 : at * 128 + 128]
            out_ref[at, :128, low : low + 64] = jnp.where(core == 0, pair[:, :64], pair[:, 64:])
        for row, ref in enumerate((gate_ref, up_ref)):
            some = ref[:, at * 1152 : at * 1152 + 1152]
            feed_ref[at, :, row * 576 : row * 576 + 576] = jnp.where(
                core == 0, some[:, :576], some[:, 576:]
            )


def pick_columns(query_weight, key_weight, value_weight, gate_weight, up_weight, packed, core):
    outs = [((4, 144, 1280), bf16), ((4, 128, 1152), bf16)]
    arrays = (query_weight, key_weight, value_weight, gate_weight, up_weight, packed)
    return call(columns_kernel, spot([core]), arrays, outs, limit=16)


def pack_kernel(tokens_ref, first_ref, second_ref, small_ref, out_ref):
    out_ref[:128, :] = tokens_ref[...]
    out_ref[128:, :] = jnp.zeros((16, 1024), bf16)
    for step, ref in enumerate((first_ref, second_ref, small_ref)):
        row = jnp.broadcast_to(ref[...].astype(f32), (16, 128)).astype(bf16)
        out_ref[128:, step * 128 : step * 128 + 128] = row


def pack(*arrays):
    return pl.pallas_call(
        pack_kernel, out_shape=jax.ShapeDtypeStruct((144, 1024), bf16)
    )(*arrays)


def lanes(width):
    return lax.broadcasted_iota(jnp.int32, (1, width), 1)


def swap_halves(values):
    first = lanes(256) % 64 < 32
    return jnp.where(first, pltpu.roll(values, 224, 1), pltpu.roll(values, 32, 1))


def head_means(values):
    lane = lanes(256)
    found = jnp.zeros_like(values)
    for head in range(3):
        inside = (lane >= head * 64) & (lane < head * 64 + 64)
        mean = jnp.sum(jnp.where(inside, values, 0.0), axis=1, keepdims=True) * (1.0 / 64)
        found = jnp.where(inside, mean, found)
    return found


def twice(values):
    return jnp.concatenate([values, values], axis=1)


def attend_kernel(
    spot_ref,
    half_ref,
    far_ref,
    across_ref,
    gain_ref,
    cosine_ref,
    sine_ref,
    place_ref,
    place_row_ref,
    start_row_ref,
    weight_ref,
    normed_ref,
    qkv_ref,
    head_ref,
    scale_ref,
    mixed_ref,
    logs_ref,
    gains_ref,
    turned_ref,
):
    z_low, core = spot_ref[0], spot_ref[1]
    for at in range(4):
        for piece, parity in ((half_ref[at, :128, 1024:], z_low), (across_ref[at], 1 - z_low)):
            weight_ref[pl.ds(pl.multiple_of((at * 2 + parity) * 128, 128), 128), :] = piece
        for ref, slot in ((half_ref, at * 2 + core), (far_ref, at * 2 + 1 - core)):
            to = pl.ds(pl.multiple_of(slot * 128, 128), 128)
            gains_ref[:8, to] = ref[at, 128:, :128].astype(f32)[:8]
            gains_ref[8:, to] = ref[at, 128:, 128:256].astype(f32)[:8]
    gain = gain_ref[...]
    lane = lanes(256)
    for block in range(8):
        ref = half_ref if block < 4 else far_ref
        rows = slice(block * 128, block * 128 + 128)
        inputs = ref[block % 4, :128, :1024].astype(f32)
        scale = lax.rsqrt(jnp.mean(inputs * inputs, axis=1, keepdims=True) + norm_eps)
        normed = (inputs * scale * gains_ref[0:1, :]).astype(bf16)
        normed_ref[rows, :] = normed
        pre = matmul(normed, weight_ref[...])
        scales = lax.rsqrt(head_means(pre * pre) + norm_eps)
        heads = pre * scales
        head_ref[rows, :] = heads
        scale_ref[rows, :] = scales
        gained = heads * gain
        turned = gained * twice(cosine_ref[rows, :]) + swap_halves(gained) * twice(sine_ref[rows, :])
        qkv_ref[rows, :] = jnp.where(lane < 192, turned, pre).astype(bf16)
        turned_ref[:, rows] = jnp.where(lane < 192, turned, pre)[:, 128:].T.astype(bf16)

    keys = qkv_ref[:, 128:192]
    values = turned_ref[64:, :]
    place = place_ref[...]
    for part in range(4):
        rows = slice(part * 256, part * 256 + 256)
        allowed = (place <= place_row_ref[:, rows]) & (place >= start_row_ref[:, rows])
        for head in range(2):
            columns = slice(head * 64, head * 64 + 64)
            scores = matmul_nt(keys, qkv_ref[rows, columns]) * HD**-0.5
            scores = jnp.where(allowed, scores, -1e30)
            top = jnp.max(scores, axis=0, keepdims=True)
            exponent = jnp.exp(scores - top)
            total = jnp.sum(exponent, axis=0, keepdims=True)
            probs = (exponent * (1.0 / total)).astype(bf16)
            mixed_ref[rows, columns] = matmul(values, probs).T.astype(bf16)
            logs_ref[head : head + 1, rows] = top + jnp.log(total)


def attend(half, far, across, gain, tables, where):
    outs = [
        ((1024, 256), bf16),
        ((1024, 1024), bf16),
        ((1024, 256), bf16),
        ((1024, 256), f32),
        ((1024, 256), f32),
        ((1024, 128), bf16),
        ((8, 1024), f32),
        ((16, 1024), f32),
    ]
    arrays = (half, far, across, gain, *tables)
    scratch = [pltpu.VMEM((128, 1024), bf16)]
    scalars = spot([where[4], where[3]])
    return call(attend_kernel, scalars, arrays, outs, scratch, 44, 2 * 1024**3)


def attend_back_kernel(
    spot_ref,
    near_ref,
    far_ref,
    out_weight_ref,
    weight_ref,
    normed_ref,
    qkv_ref,
    head_ref,
    scale_ref,
    mixed_ref,
    logs_ref,
    gain_ref,
    cosine_ref,
    sine_ref,
    place_ref,
    place_row_ref,
    start_row_ref,
    other_ref,
    own_ref,
    pre_grad_ref,
    out_grad_ref,
    sums_ref,
    first_ref,
    branch_ref,
    mixed_grad_ref,
    grad_ref,
    turned_ref,
):
    x = spot_ref[0]
    for step in range(4):
        to = pl.multiple_of(((x + step) % 4) * 128, 128)
        piece = slice(step * 128, step * 128 + 128)
        branch_ref[pl.ds(to, 128), :] = near_ref[piece, :]
        branch_ref[pl.ds(to + 512, 128), :] = far_ref[piece, :]
    mixed_grad_ref[...] = matmul_nt(branch_ref[...], out_weight_ref[...]).astype(bf16)
    keys, values = qkv_ref[:, 128:192], qkv_ref[:, 192:]
    turned_ref[...] = qkv_ref[:, 128:].astype(f32).T.astype(bf16)
    keys_turned = turned_ref[:64, :]
    place = place_ref[...]
    grad_ref[:, 128:] = jnp.zeros((1024, 128), f32)
    for part in range(4):
        rows = slice(part * 256, part * 256 + 256)
        allowed = (place <= place_row_ref[:, rows]) & (place >= start_row_ref[:, rows])
        for head in range(2):
            columns = slice(head * 64, head * 64 + 64)
            queries, upstream = qkv_ref[rows, columns], mixed_grad_ref[rows, columns]
            scores = matmul_nt(keys, queries) * HD**-0.5
            probs = jnp.where(allowed, jnp.exp(scores - logs_ref[head : head + 1, rows]), 0.0)
            prob_grad = matmul_nt(values, upstream)
            inner = jnp.sum(probs * prob_grad, axis=0, keepdims=True)
            score_grad = (probs * (prob_grad - inner)).astype(bf16)
            grad_ref[:, 128:192] += matmul(score_grad, queries) * HD**-0.5
            grad_ref[:, 192:] += matmul(probs.astype(bf16), upstream)
            grad_ref[rows, columns] = matmul(keys_turned, score_grad).T * HD**-0.5
    out_grad_ref[...] = matmul(mixed_ref[...].astype(f32).T.astype(bf16), branch_ref[...])
    gain = gain_ref[...]
    lane = lanes(256)
    sums_ref[...] = jnp.zeros((8, 256), f32)
    first_ref[...] = jnp.zeros((8, 1024), f32)
    for block in (4, 5, 6, 7, 0, 1, 2, 3):
        rows = slice(block * 128, block * 128 + 128)
        grads = grad_ref[rows, :]
        back = grads * twice(cosine_ref[rows, :]) - swap_halves(grads) * twice(sine_ref[rows, :])
        heads = head_ref[rows, :]
        sums_ref[0:1, :] += jnp.sum(back * heads, axis=0, keepdims=True)
        gained = back * gain
        entry = scale_ref[rows, :] * (gained - heads * head_means(gained * heads))
        pre_grad = jnp.where(lane < 192, entry, grads).astype(bf16)
        pre_grad_ref[rows, :] = pre_grad
        partial = matmul_nt(pre_grad, weight_ref[...])
        first_ref[0:1, :] += jnp.sum(partial * normed_ref[rows, :].astype(f32), axis=0, keepdims=True)
        if block < 4:
            own_ref[rows, :] = partial
        else:
            other_ref[(block - 4) * 128 : (block - 3) * 128, :] = partial.astype(bf16)


def attend_back(near, far, out_slot, kept, gain, tables, where):
    outs = [
        ((512, 1024), bf16),
        ((512, 1024), f32),
        ((1024, 256), bf16),
        ((128, 1024), f32),
        ((8, 256), f32),
        ((8, 1024), f32),
    ]
    arrays = (near, far, out_slot, *kept, gain, *tables)
    scratch = [
        pltpu.VMEM((1024, 1024), bf16),
        pltpu.VMEM((1024, 128), bf16),
        pltpu.VMEM((1024, 256), f32),
        pltpu.VMEM((128, 1024), bf16),
    ]
    return call(attend_back_kernel, spot([where[0]]), arrays, outs, scratch, 48, 4 * 1024**3)


def feed_kernel(
    spot_ref,
    half_ref,
    far_ref,
    upstream_ref,
    came_ref,
    lower_ref,
    upper_ref,
    down_ref,
    other_ref,
    own_ref,
    hidden_ref,
    pre_grad_ref,
    normed_ref,
    weight_ref,
):
    z_low, core = spot_ref[0], spot_ref[1]
    for at in range(4):
        across = lower_ref if at < 2 else upper_ref
        for piece, parity in ((came_ref[at], z_low), (across[at % 2], 1 - z_low)):
            weight_ref[pl.ds(pl.multiple_of((at * 2 + parity) * 128, 128), 128), :] = piece
    normed_ref[:512] = half_ref[...]
    normed_ref[512:] = far_ref[...]

    def rows_of(part, slot_core):
        slots = [
            pl.ds(pl.multiple_of((part * 4 + step * 2 + slot_core) * 128, 128), 128)
            for step in range(2)
        ]
        return slots, jnp.concatenate([upstream_ref[slot, :] for slot in slots], axis=0)

    def work(start, part, slot_core):
        rows = pl.ds(pl.multiple_of(start, 256), 256)
        slots, upstream = rows_of(part, slot_core)
        pre = matmul(normed_ref[rows, :], weight_ref[...])
        gate, up = pre[:, :576], pre[:, 576:]
        hidden_grad = matmul_nt(upstream, down_ref[...]).astype(bf16).astype(f32)
        sigmoid = 1.0 / (1.0 + jnp.exp(-gate))
        silu = gate * sigmoid
        hidden = (silu * up).astype(bf16)
        for step, slot in enumerate(slots):
            hidden_ref[slot, :] = hidden[step * 128 : step * 128 + 128]
        gate_grad = hidden_grad * up * sigmoid * (1.0 + gate * (1.0 - sigmoid))
        pre_grad = jnp.concatenate([gate_grad, hidden_grad * silu], axis=1).astype(bf16)
        pre_grad_ref[rows, :] = pre_grad
        return matmul_nt(pre_grad, weight_ref[...])

    def other_half(part, carry):
        rows = pl.ds(pl.multiple_of(part * 256, 256), 256)
        other_ref[rows, :] = work(part * 256 + 512, part, 1 - core).astype(bf16)
        return carry

    def own_half(part, carry):
        rows = pl.ds(pl.multiple_of(part * 256, 256), 256)
        own_ref[rows, :] = work(part * 256, part, core)
        return carry

    lax.fori_loop(0, 2, other_half, 0)
    lax.fori_loop(0, 2, own_half, 0)


def feed(half, far, upstream, weights, down_slot, where):
    arrays = (half, far, upstream, *weights, down_slot)
    outs = [
        ((512, 1024), bf16),
        ((512, 1024), f32),
        ((1024, 576), bf16),
        ((1024, 1152), bf16),
        ((1024, 1024), bf16),
    ]
    scratch = [pltpu.VMEM((1024, 1152), bf16)]
    scalars = spot([where[4], where[3]])
    return call(feed_kernel, scalars, arrays, outs, scratch, 44, 6 * 1024**3)


def feed_grads_kernel(spot_ref, mine_ref, other_ref, gate_ref, up_ref, down_ref):
    core, z_low = spot_ref[0], spot_ref[1]
    home = core == z_low
    for at in range(16):
        mine = mine_ref[at].astype(f32)
        other = other_ref[at].astype(f32)
        first = jnp.where(core == 0, mine[:288], other[:288])
        second = jnp.where(core == 0, other[:288], mine[:288])
        block = jnp.where(home, mine[288:], other[288:])
        rows = slice(at * 8, at * 8 + 8)
        for x in range(4):
            wide = [
                jnp.concatenate(
                    [one[(x * 9 + i) * 8 : (x * 9 + i) * 8 + 8] for i in range(9)], axis=1
                )
                for one in (first, second)
            ]
            columns = slice(x * 1152, x * 1152 + 1152)
            gate_ref[rows, columns] = jnp.concatenate([one[:, :576] for one in wide], axis=1)
            up_ref[rows, columns] = jnp.concatenate([one[:, 576:] for one in wide], axis=1)
        for i in range(18):
            for j in range(2):
                piece = block[(i * 2 + j) * 8 : (i * 2 + j) * 8 + 8]
                low, left = at // 4 * 144 + i * 8, at % 4 * 256 + j * 128
                down_ref[low : low + 8, left : left + 128] = piece


def feed_grads(mine, other, where):
    outs = [((128, 4608), f32), ((128, 4608), f32), ((576, 1024), f32)]
    return call(feed_grads_kernel, spot(where[3:]), (mine, other), outs, (), 40)


def attention_grads_kernel(spot_ref, mine_ref, other_ref, q_ref, k_ref, v_ref, out_ref, extra_ref):
    core, z_low, x, y, z = (spot_ref[i] for i in range(5))
    home = core == z_low
    for y_step in range(4):
        for z_step in range(4):
            mine = mine_ref[y_step, z_step].astype(f32)
            other = other_ref[y_step, z_step].astype(f32)
            first = jnp.where(core == 0, mine[:96], other[:96])
            second = jnp.where(core == 0, other[:96], mine[:96])
            block = jnp.where(home, mine[96:], other[96:])
            y_at, z_at = (y + y_step) % 4, (z + z_step) % 4
            rows = pl.ds(pl.multiple_of((y_at * 4 + z_at) * 8, 8), 8)
            extra = jnp.zeros((8, 128), f32)
            for step in range(4):
                slot, low = (x + step) % 4, step * 24
                to = pl.multiple_of(slot * 256, 128)
                q_ref[rows, pl.ds(to, 128)] = first[low : low + 8]
                q_ref[rows, pl.ds(to + 128, 128)] = second[low : low + 8]
                one, two = first[low + 8 : low + 16], second[low + 8 : low + 16]
                columns = pl.ds(pl.multiple_of(slot * 128, 128), 128)
                k_ref[rows, columns] = jnp.concatenate([one[:, :64], two[:, :64]], axis=1)
                v_ref[rows, columns] = jnp.concatenate([one[:, 64:], two[:, 64:]], axis=1)
                extra = extra + first[low + 16 : low + 24] + second[low + 16 : low + 24]
            extra_ref[rows, :] = extra
            for i in range(4):
                for j in range(2):
                    to = pl.ds(pl.multiple_of(y_at * 32 + i * 8, 8), 8)
                    columns = pl.ds(pl.multiple_of(z_at * 256 + j * 128, 128), 128)
                    out_ref[to, columns] = block[(i * 2 + j) * 8 : (i * 2 + j) * 8 + 8]


def attention_grads(mine, other, where):
    outs = [
        ((128, 1024), f32),
        ((128, 512), f32),
        ((128, 512), f32),
        ((128, 1024), f32),
        ((128, 128), f32),
    ]
    x, y, z, core, z_low = where
    return call(
        attention_grads_kernel, spot([core, z_low, x, y, z]), (mine, other), outs, (), 24
    )


def on_device(
    tokens,
    seq_lengths,
    token_places,
    attention_gain,
    query_weight,
    key_weight,
    value_weight,
    query_gain,
    key_gain,
    out_weight,
    feedforward_gain,
    gate_weight,
    up_weight,
    down_weight,
    cotangent,
):
    shard, replica = lax.axis_index("shard"), lax.axis_index("replica")
    x, z_low = shard // 2, shard % 2
    y, z, core = replica // 4, (replica // 2) % 2 * 2 + z_low, replica % 2
    where = (x, y, z, core, z_low)

    facts = cat([token_places, jnp.broadcast_to(seq_lengths[:, :1], (1, 128))], 1)
    facts = jnp.where(core == z_low, facts, send(facts, other_core))
    places = facts[0, :1024].reshape(4, 2, 128)
    places = jnp.stack([pick(places, core, 1), pick(places, 1 - core, 1)]).reshape(1, 1024)
    starts = jnp.where(places >= facts[:, 1024:1025], facts[:, 1024:1025], 0)
    lane = jnp.arange(128)
    frequency = rope_base ** (-2.0 * (lane % 32).astype(f32) / HD)
    angles = (places - starts).astype(f32).reshape(1024, 1) * frequency[None, :]
    cosine, sine = jnp.cos(angles), jnp.sin(angles) * jnp.where(lane % 64 < 32, -1.0, 1.0)
    places_f = places.astype(f32)
    tables = (cosine, sine, places_f.reshape(1024, 1), places_f, starts.astype(f32))

    small = cat([query_gain, key_gain, jnp.zeros((112,), bf16)])
    packed = pack(tokens[0], attention_gain[None], feedforward_gain[None], small[None])
    packed = send(packed, regroup)
    packed_out, for_feed = pick_columns(
        query_weight, key_weight, value_weight, gate_weight, up_weight, packed, core
    )
    half = exchange(packed_out, x_rings)
    rows_held = cat([out_weight, down_weight])
    half, for_feed, rows_held, tables = join(half, for_feed, rows_held, tables)

    across = send(half[:, :128, 1024:], z_up)
    far = send(half, other_core)
    rows_got = [send(rows_held[:352], z_up_home), send(rows_held[352:], z_down_home)]
    feed_came = exchange(for_feed, x_rings)
    upstream_own = send(cotangent[0], regroup)
    far, across, upstream_own = join(far, across, upstream_own)
    upstream = lax.all_gather(upstream_own, AXES, axis=0, axis_index_groups=x_groups, tiled=True)
    rows_slot = jnp.where(core == z_low, rows_held, cat(rows_got))
    out_slot, down_slot = rows_slot[:128], rows_slot[128:]
    inputs = packed[:128].astype(f32)
    notes = jnp.stack([half[:, 128, 256:272], far[:, 128, 256:272]], axis=1)
    notes = jnp.where(core == 0, notes, notes[:, ::-1]).astype(f32)
    gain_query, gain_key = notes[..., :8].reshape(64), notes[..., 8:].reshape(64)
    gain = cat([gain_query, gain_query, gain_key, jnp.ones((64,), f32)])[None]

    attention_slice, first_normed, qkv, heads, scales, mixed, logs, gains = attend(
        half, far, across, gain, tables, where
    )
    gain_first, gain_second = gains[0], gains[8]
    other_half = matmul(mixed[512:], out_slot).astype(bf16)
    other_half, mixed, feed_came = join(other_half, mixed, feed_came)
    got = send(other_half, other_core)
    own_half = matmul(mixed[:512], out_slot)
    parts = scatter_sums(own_half, got)
    parts, feed_came = join(parts, feed_came)

    lower, upper = send(feed_came[:2], z_up), send(feed_came[2:], z_down)
    middle = inputs + add_up(parts)
    second_scale = rms_scale(middle)
    half = gather_half((middle * second_scale * gain_second).astype(bf16)).reshape(512, 1024)
    far = send(half, other_core)
    other_half, own_half, hidden, pre_grad, normed_all = feed(
        half, far, upstream, (feed_came, lower, upper), down_slot, where
    )
    got = send(other_half, other_core)
    result_rows = matmul(hidden, down_slot).astype(bf16)
    got, result_rows, pre_grad = join(got, result_rows, pre_grad)

    result_sum = lax.psum_scatter(
        result_rows, AXES, scatter_dimension=0, axis_index_groups=x_groups, tiled=True
    )
    parts = scatter_sums(own_half, got)
    feed_weight_grad = matmul_tn(normed_all, pre_grad)
    down_weight_grad = matmul_tn(hidden, upstream)
    feed_parts = cat(
        [
            rows_for_planes(feed_weight_grad).reshape(16, 72, 8, 128),
            block_for_planes(down_weight_grad).reshape(16, 36, 8, 128),
        ],
        1,
    )
    parts, feed_parts = join(parts, feed_parts)

    feed_parts = exchange(feed_parts, planes)
    second_grad = add_up(parts)
    middle_norm_grad, second_gain_terms = norm_back(middle, second_scale, gain_second, second_grad)
    middle_grad = upstream_own.astype(f32) + middle_norm_grad
    second_gain_grad = jnp.sum(second_gain_terms, axis=0)
    near = cat(gather_x(middle_grad.astype(bf16)))
    far = send(near, other_core)
    other_half, own_half, pre_grad, out_weight_grad, gain_terms, first_terms = attend_back(
        near,
        far,
        out_slot,
        (attention_slice, first_normed, qkv, heads, scales, mixed, logs),
        gain,
        tables,
        where,
    )
    got = send(other_half, other_core)
    attention_weight_grad = matmul_tn(first_normed, pre_grad)
    first_gain_grad = first_terms[0] / gain_first
    small = jnp.stack([gain_terms[0, :64] + gain_terms[0, 64:128], gain_terms[0, 128:192]], 1)
    small = jnp.pad(small.reshape(8, 8, 2), ((0, 0), (0, 120), (0, 0))).reshape(1024, 2)
    extra = cat([first_gain_grad[:, None], second_gain_grad[:, None], small], 1)
    extra = jnp.pad(extra, ((0, 0), (0, 124)))
    by_row = rows_for_planes(cat([attention_weight_grad, extra], 1)).reshape(4, 4, 24, 8, 128)
    by_block = block_for_planes(out_weight_grad).reshape(4, 4, 8, 8, 128)
    attention_parts = cat([by_row, by_block], 2)
    first, rest = scatter_parts(turn_back(own_half, x), turn_back(got, x))
    first, rest, attention_parts = join(first, rest, attention_parts)

    parts = send_x(*rest)
    pieces = [pick(attention_parts, (y + step) % 4, 0) for step in range(4)]
    ring = send_ring(pieces, y_up, y_down, y_far)
    first, parts, ring, feed_parts = join(first, parts, ring, feed_parts)
    rows = add_up(feed_parts).astype(bf16)
    feed_got = exchange_rows(rows[:72].reshape(8, 9, 8, 128))
    feed_mine = return_planes(feed_got, rows[72:])

    rows = pieces[0].astype(f32) + add_up(jnp.stack(ring))
    pieces = [pick(rows, (z + step) % 4, 0) for step in range(4)]
    ring = send_ring(pieces, z_up, z_down, z_far)
    rows = (pieces[0] + add_up(jnp.stack(ring))).astype(bf16)
    attention_got = exchange_x(rows[:24].reshape(8, 3, 8, 128), x)
    first_grad = first + add_up(jnp.stack(parts))
    input_norm_grad, _ = norm_back(inputs, rms_scale(inputs), gain_first, first_grad)
    input_grad = middle_grad + input_norm_grad
    result = send((middle + result_sum.astype(f32)).astype(bf16), regroup)
    input_grad = send(input_grad.astype(bf16), regroup)
    mine = gather_y(gather_z(attention_got, rows[24:], z_low))
    query_sum, key_sum, value_sum, out_sum, gain_sums = attention_grads(
        mine, send(mine, other_core), where
    )
    gate_sum, up_sum, down_sum = feed_grads(feed_mine, send(feed_mine, other_core), where)
    return (
        result[None],
        input_grad.astype(f32)[None],
        gain_sums[:, 0],
        query_sum,
        key_sum,
        value_sum,
        gain_sums[:8, 2],
        gain_sums[:8, 3],
        out_sum,
        gain_sums[:, 1],
        gate_sum,
        up_sum,
        down_sum,
    )


def solution(mesh):
    placed = (
        P("replica", "shard", None),
        P("replica", None),
        P("replica", None),
        P("shard"),
        P("shard", None),
        P("shard", None),
        P("shard", None),
        P("shard"),
        P("shard"),
        P("shard", None),
        P("shard"),
        P("shard", None),
        P("shard", None),
        P("shard", None),
        P("replica", "shard", None),
    )
    return jax.shard_map(
        on_device,
        mesh=mesh,
        in_specs=placed,
        out_specs=(
            P("replica", "shard", None),
            P("replica", "shard", None),
            P("shard"),
            P("shard", None),
            P("shard", None),
            P("shard", None),
            P("shard"),
            P("shard"),
            P("shard", None),
            P("shard"),
            P("shard", None),
            P("shard", None),
            P("shard", None),
        ),
        check_vma=False,
    )
```

time: 488 us -> 423 us (0.87)
  local copies, waits for them, and re-layouts: 109 us -> 34.1 us
  Pallas kernels: 0 us -> 52.4 us
  other arithmetic: 71.2 us -> 44.2 us
  starting transfers between devices: 131 us -> 105 us
  matrix products: 39.2 us -> 16.2 us
  blocking collectives: 0 us -> 16.8 us
  waiting for transfers between devices: 123 us -> 132 us
  between operations: 7.17 us -> 15.4 us
    ppermute x84 -> x39, starting transfers between devices: 131 us -> 69.6 us  [send(): return lax.ppermute(values, AXES, moves)]
    all_to_all x0 -> x7, waiting for transfers between devices: none -> 53.6 us  [exchange(): return lax.all_to_all(values, AXES, 0, 0, axis_index_groups=groups)]
    pallas_call x0 -> x7, Pallas kernels: none -> 52.4 us  [the longest x6 50.7 us: call(): pl.pallas_call(kernel, out_shape=[jax.ShapeDtypeStruct(shape, kind) for s...]
    ppermute x84 -> x39, waiting for transfers between devices: 123 us -> 78.4 us  [send(): return lax.ppermute(values, AXES, moves)]
    all_to_all x0 -> x7, starting transfers between devices: none -> 35.2 us  [exchange(): return lax.all_to_all(values, AXES, 0, 0, axis_index_groups=groups)]
    unnamed x213 -> x113, local copies, waits for them, and re-layouts: 46.7 us -> 20.7 us
    dot_general x10 -> x0, matrix products: 21.9 us -> none  [the longest x4 12.5 us: matmul_nt(): lax.dot_general(left_side, right_side, (((1,), (1,)), ((), ())), preferre...]
    slice x35 -> x13, local copies, waits for them, and re-layouts: 24.4 us -> 5.5 us  [the longest x1 1.68 us: on_device(): across = send(half[:, :128, 1024:], z_up)]
  transfers between devices with their start and end apart: 84 -> 48, of which waited for: 34 -> 28; matrix products, arithmetic and copies ran while one was open for 36% -> 16% of each run, Pallas kernels for 0% -> 8%
where the time goes in v2:
time: 423 us; the launch traced here: 416 us
  waiting for transfers between devices  132 us (31%)
  starting transfers between devices  105 us (25%)
  Pallas kernels  52.4 us (12%)
  other arithmetic  44.2 us (10%)
  local copies, waits for them, and re-layouts  34.1 us (8%)
  blocking collectives  16.8 us (4%)
  matrix products  16.2 us (4%)
  between operations  15.4 us (4%)
    ppermute x39, waiting for transfers between devices, send(): return lax.ppermute(values, AXES, moves)  78.4 us
    ppermute x39, starting transfers between devices, send(): return lax.ppermute(values, AXES, moves)  69.6 us
    all_to_all x7, waiting for transfers between devices, exchange(): return lax.all_to_all(values, AXES, 0, 0, axis_index_groups=groups)  53.6 us
    pallas_call x6, Pallas kernels, call(): pl.pallas_call(kernel, out_shape=[jax.ShapeDtypeStruct(shape, kind) for s...  50.7 us
    all_to_all x7, starting transfers between devices, exchange(): return lax.all_to_all(values, AXES, 0, 0, axis_index_groups=groups)  35.2 us
    unnamed x113, local copies, waits for them, and re-layouts  20.7 us
    all_to_all x1, blocking collectives, exchange(): return lax.all_to_all(values, AXES, 0, 0, axis_index_groups=groups)  16.8 us
    unnamed x16, other arithmetic  10.1 us
  transfers between devices with their start and end apart: 48, of which 28 were waited for; matrix products, arithmetic and copies ran while one was open for 16% of the time, Pallas kernels for 8%

profile of v2, /device:TPU:1, one launch (start us, length us, event | category | flops | bytes accessed | tf_op | source)
XLA Modules:
  0.0 416.2 jit_solution(15806599941558121815)
XLA Ops:
  10.4 4.9 %collective-permute-start = (bf16[144,1024]{1,0:T(8,128)(2,1)}, bf16[144,1024]{1,0:T(8,128)(2,1)S(1)}, u32[]{:S(2)}, u32[]{:S(2)}) collective-permute-start(bf16[144,1024]{1,0:T(8,128)(2,1)} %shard_map.246), channel_id=1, source_target_pairs={{0,0},{1,16},{16,1},{17,17},{2,2},{3,18},{18,3},{19,19},{4,4},{5,2... | collective-permute-start | bytes 884744 | tf_op jit(solution)/shard_map/ppermute | solution.py:55
  22.6 4.5 %all-to-all-start = ((bf16[4,144,1280]{2,1,0:T(8,128)(2,1)}), bf16[4,144,1280]{2,1,0:T(8,128)(2,1)}, u32[]{:S(2)}, u32[]{:S(2)}) async-start(bf16[4,144,1280]{2,1,0:T(8,128)(2,1)} %get-tuple-element.76), calls=%async_computation | async-start | bytes 2949120 | tf_op jit(solution)/shard_map/all_to_all | solution.py:89
  30.9 16.2 %all-to-all-done.half_ref = bf16[4,144,1280]{2,1,0:T(8,128)(2,1)} async-done(((bf16[4,144,1280]{2,1,0:T(8,128)(2,1)}), bf16[4,144,1280]{2,1,0:T(8,128)(2,1)}, u32[]{:S(2)}, u32[]{:S(2)}) %all-to-all-start) | async-done | bytes 1474592 | tf_op jit(solution)/shard_map/all_to_all | solution.py:89
  56.0 6.1 %collective-permute-start.3 = (bf16[4,128,256]{2,1,0:T(8,128)(2,1)}, bf16[4,128,256]{2,1,0:T(8,128)(2,1)S(1)}, u32[]{:S(2)}, u32[]{:S(2)}) collective-permute-start(bf16[4,128,256]{2,1,0:T(8,128)(2,1)} %slice.137), channel_id=1, source_target_pairs={{0,16},{1,17},{16,2},{17,3},{2,18},{3,19},{18,0},{19,1},{4,20},{5,... | collective-permute-start | bytes 786440 | tf_op jit(solution)/shard_map/ppermute | solution.py:55
  62.3 3.5 all-to-all-start.1
  66.1 3.1 maximum_select_fusion
  73.5 11.9 %shard_map.248 = (bf16[1024,256]{1,0:T(8,128)(2,1)S(1)}, bf16[1024,1024]{1,0:T(8,128)(2,1)S(1)}, bf16[1024,256]{1,0:T(8,128)(2,1)S(1)}, f32[1024,256]{1,0:T(8,12...) custom-call(s32[2]{0:T(128)S(1)} %pad_add_fusion.1.spot_ref, ...), custom_call_target="tpu_custom_call" | custom-call | flops 2147483648 | bytes 4273152 | tf_op jit(solution)/shard_map/pallas_call | solution.py:181
  98.0 3.5 all-to-all-start.2
  101.5 23.6 %all-to-all-done.2 = bf16[4,128,1024]{2,1,0:T(8,128)(2,1)S(1)} async-done(((bf16[4,128,1024]{2,1,0:T(8,128)(2,1)}), bf16[4,128,1024]{2,1,0:T(8,128)(2,1)S(1)}, u32[]{:S(2)}, u32[]{:S(2)}) %all-to-all-start.2) | async-done | bytes 1048608 | tf_op jit(solution)/shard_map/all_to_all | solution.py:89
  127.0 16.8 %all_to_all.40 = bf16[4,128,1024]{2,1,0:T(8,128)(2,1)S(1)} all-to-all(bf16[4,128,1024]{2,1,0:T(8,128)(2,1)S(1)} %broadcast_in_dim.80), channel_id=1, replica_groups={{0,32,64,96},{16,48,80,112},{2,34,66,98},{18,50,82,114},{4,36,68,100},{..., dimensions={0} | all-to-all | bytes 2097152 | tf_op jit(solution)/shard_map/all_to_all | solution.py:89
  149.1 13.3 %collective-permute-done.9.lower_ref = bf16[2,128,1152]{2,1,0:T(8,128)(2,1)S(1)} collective-permute-done((bf16[2,128,1152]{2,1,0:T(8,128)(2,1)S(1)}, bf16[2,128,1152]{2,1,0:T(8,128)(2,1)S(1)}, u32[]{:S(2)}, u32[]{:S(2)}) %collective-permute-start.9) | collective-permute-done | bytes 589856 | tf_op jit(solution)/shard_map/ppermute | solution.py:55
  169.6 12.0 %shard_map.249 = (bf16[512,1024]{1,0:T(8,128)(2,1)}, f32[512,1024]{1,0:T(8,128)S(1)}, bf16[1024,576]{1,0:T(8,128)(2,1)S(1)}, bf16[1024,1152]{1,0:T(8,128)(2,1)}, bf16[1024,1024]{1,0:T(8,128)(2,1)}) custom-call(s32[2]{0:T(128)S(1)} %pad_add_fusion.1.spot_ref, bf16[512,1024]{1,0:T(8,128)(2,1)S(1)} %bitcast.169, bf16[512,1024]{1,0:T(8,128)(2,1)S(1)} %copy-done.14, ...), custom_call_target="tpu_custom_call" | custom-call | flops 6442450944 | bytes 7733248 | tf_op jit(solution)/shard_map/pallas_call | solution.py:181
  191.3 3.5 all-to-all-start.4
  194.8 5.2 %convolution_convert_fusion = bf16[1024,1152]{1,0:T(8,128)(2,1)S(1)} fusion(bf16[1024,1024]{1,0:T(8,128)(2,1)} %get-tuple-element.102, bf16[1024,1152]{1,0:T(8,128)(2,1)} %get-tuple-element.103), kind=kOutput, calls=%fused_computation.2 | convolution fusion | flops 2417098752 | bytes 6815744 | tf_op jit(solution)/shard_map/dot_general | solution.py:208
  203.4 6.6 %all-to-all-done.4 = bf16[4,128,1024]{2,1,0:T(8,128)(2,1)S(1)} async-done(((bf16[4,128,1024]{2,1,0:T(8,128)(2,1)}), bf16[4,128,1024]{2,1,0:T(8,128)(2,1)S(1)}, u32[]{:S(2)}, u32[]{:S(2)}) %all-to-all-start.4) | async-done | bytes 1048608 | tf_op jit(solution)/shard_map/all_to_all | solution.py:89
  214.8 5.9 %collective-permute-done.15 = bf16[128,1024]{1,0:T(8,128)(2,1)S(1)} collective-permute-done((bf16[128,1024]{1,0:T(8,128)(2,1)S(1)}, bf16[128,1024]{1,0:T(8,128)(2,1)S(1)}, u32[]{:S(2)}, u32[]{:S(2)}) %collective-permute-start.15) | collective-permute-done | bytes 262176 | tf_op jit(solution)/shard_map/ppermute | solution.py:55
  220.7 4.5 %collective-permute-done.14 = bf16[128,1024]{1,0:T(8,128)(2,1)S(1)} collective-permute-done((bf16[128,1024]{1,0:T(8,128)(2,1)S(1)}, bf16[128,1024]{1,0:T(8,128)(2,1)S(1)}, u32[]{:S(2)}, u32[]{:S(2)}) %collective-permute-start.14) | collective-permute-done | bytes 262176 | tf_op jit(solution)/shard_map/ppermute | solution.py:55
  228.3 5.9 %all-to-all-start.5 = ((bf16[16,108,8,128]{3,2,1,0:T(8,128)(2,1)}), bf16[16,108,8,128]{3,2,1,0:T(8,128)(2,1)}, u32[]{:S(2)}, u32[]{:S(2)}) async-start(bf16[16,108,8,128]{3,2,1,0:T(8,128)(2,1)} %pad_maximum_fusion), calls=%async_computation.6 | async-start | bytes 7077888 | tf_op jit(solution)/shard_map/all_to_all | solution.py:89
  237.4 16.2 %shard_map.250 = (bf16[512,1024]{1,0:T(8,128)(2,1)S(1)}, f32[512,1024]{1,0:T(8,128)}, bf16[1024,256]{1,0:T(8,128)(2,1)S(1)}, f32[128,1024]{1,0:T(8,128)S(1)}, f3...) custom-call(s32[1]{0:T(128)} %bitcast.28.spot_ref, bf16[512,1024]{1,0:T(8,128)(2,1)} %copy-done.39, ...), custom_call_target="tpu_custom_call" | custom-call | flops 4294967296 | bytes 8958976 | tf_op jit(solution)/shard_map/pallas_call | solution.py:181
  263.5 3.3 collective-permute-start.19
  275.1 3.4 collective-permute-done.19
  278.5 6.8 %collective-permute-done.21 = bf16[4,32,8,128]{3,2,1,0:T(8,128)(2,1)S(1)} collective-permute-done((bf16[4,32,8,128]{3,2,1,0:T(8,128)(2,1)}, bf16[4,32,8,128]{3,2,1,0:T(8,128)(2,1)S(1)}, u32[]{:S(2)}, u32[]{:S(2)}) %collective-permute-start.21) | collective-permute-done | bytes 262176 | tf_op jit(solution)/shard_map/ppermute | solution.py:55
  285.3 5.4 %collective-permute-done.22 = bf16[4,32,8,128]{3,2,1,0:T(8,128)(2,1)S(1)} collective-permute-done((bf16[4,32,8,128]{3,2,1,0:T(8,128)(2,1)}, bf16[4,32,8,128]{3,2,1,0:T(8,128)(2,1)S(1)}, u32[]{:S(2)}, u32[]{:S(2)}) %collective-permute-start.22) | collective-permute-done | bytes 262176 | tf_op jit(solution)/shard_map/ppermute | solution.py:55
  294.2 6.0 %all-to-all-start.6 = ((bf16[4,2,9,8,128]{4,3,2,1,0:T(8,128)(2,1)}), bf16[4,2,9,8,128]{4,3,2,1,0:T(8,128)(2,1)S(1)}, u32[]{:S(2)}, u32[]{:S(2)}) async-start(bf16[4,2,9,8,128]{4,3,2,1,0:T(8,128)(2,1)} %bitcast.81), calls=%async_computation.7 | async-start | bytes 294912 | tf_op jit(solution)/shard_map/all_to_all | solution.py:89
  300.3 5.2 %all-to-all-done.6 = bf16[4,2,9,8,128]{4,3,2,1,0:T(8,128)(2,1)S(1)} async-done(((bf16[4,2,9,8,128]{4,3,2,1,0:T(8,128)(2,1)}), bf16[4,2,9,8,128]{4,3,2,1,0:T(8,128)(2,1)S(1)}, u32[]{:S(2)}, u32[]{:S(2)}) %all-to-all-start.6) | async-done | bytes 147488 | tf_op jit(solution)/shard_map/all_to_all | solution.py:89
  316.2 8.2 %all-to-all-start.7 = ((bf16[16,576,128]{2,1,0:T(8,128)(2,1)}), bf16[16,576,128]{2,1,0:T(8,128)(2,1)S(1)}, u32[]{:S(2)}, u32[]{:S(2)}) async-start(bf16[16,576,128]{2,1,0:T(8,128)(2,1)} %constant_dynamic-update-slice_fusion), calls=%async_computation.8 | async-start | bytes 4718592 | tf_op jit(solution)/shard_map/all_to_all | solution.py:89
  333.2 6.1 %collective-permute-done.26 = bf16[32,8,128]{2,1,0:T(8,128)(2,1)S(1)} collective-permute-done((bf16[32,8,128]{2,1,0:T(8,128)(2,1)S(1)}, bf16[32,8,128]{2,1,0:T(8,128)(2,1)S(1)}, u32[]{:S(2)}, u32[]{:S(2)}) %collective-permute-start.26) | collective-permute-done | bytes 65568 | tf_op jit(solution)/shard_map/ppermute | solution.py:55
  339.4 10.7 %collective-permute-done.25 = bf16[32,8,128]{2,1,0:T(8,128)(2,1)S(1)} collective-permute-done((bf16[32,8,128]{2,1,0:T(8,128)(2,1)S(1)}, bf16[32,8,128]{2,1,0:T(8,128)(2,1)S(1)}, u32[]{:S(2)}, u32[]{:S(2)}) %collective-permute-start.25) | collective-permute-done | bytes 65568 | tf_op jit(solution)/shard_map/ppermute | solution.py:55
  352.2 6.0 %collective-permute-start.38 = (bf16[16,576,128]{2,1,0:T(8,128)(2,1)S(1)}, bf16[16,576,128]{2,1,0:T(8,128)(2,1)}, u32[]{:S(2)}, u32[]{:S(2)}) collective-permute-start(bf16[16,576,128]{2,1,0:T(8,128)(2,1)S(1)} %all-to-all-done.7.mine_ref), channel_id=1, source_target_pairs={{0,1},{1,0},{16,17},{17,16},{2,3},{3,2},{18,19},{19,18},{4,5},{5,4... | collective-permute-start | bytes 7077896 | tf_op jit(solution)/shard_map/ppermute | solution.py:55
  379.1 4.7 %collective-permute-start.37 = (bf16[4,4,160,128]{3,2,1,0:T(8,128)(2,1)S(1)}, bf16[4,4,160,128]{3,2,1,0:T(8,128)(2,1)}, u32[]{:S(2)}, u32[]{:S(2)}) collective-permute-start(bf16[4,4,160,128]{3,2,1,0:T(8,128)(2,1)S(1)} %pad_maximum_fusion.5.mine_ref), channel_id=1, source_target_pairs={{0,1},{1,0},{16,17},{17,16},{2,3},{3,2},{18,19},{19,18},{4,5},{5,4... | collective-permute-start | bytes 1966088 | tf_op jit(solution)/shard_map/ppermute | solution.py:55
  388.4 3.6 collective-permute-start.24
  402.2 5.2 %shard_map.252 = (f32[128,4608]{1,0:T(8,128)}, f32[128,4608]{1,0:T(8,128)}, f32[576,1024]{1,0:T(8,128)}) custom-call(s32[2]{0:T(128)S(1)} %pad_add_fusion.2.spot_ref, bf16[16,576,128]{2,1,0:T(8,128)(2,1)S(1)} %all-to-all-done.7.mine_ref, bf16[16,576,128]{2,1,0:T(8,128)(2,1)} %collective-permute-done.38.other_ref), custom_call_target="tpu_custom_call" | custom-call | bytes 4718592 | tf_op jit(solution)/shard_map/pallas_call | solution.py:181
  (297 shorter events, 158.7 us)
Async XLA Ops:
  10.4 9.5 %collective-permute-start = (bf16[144,1024]{1,0:T(8,128)(2,1)}, bf16[144,1024]{1,0:T(8,128)(2,1)S(1)}, u32[]{:S(2)}, u32[]{:S(2)}) collective-permute-start(bf16[144,1024]{1,0:T(8,128)(2,1)} %shard_map.246), channel_id=1, source_target_pairs={{0,0},{1,16},{16,1},{17,17},{2,2},{3,18},{18,3},{19,19},{4,4},{5,2... | collective-permute-start | bytes 884744 | tf_op jit(solution)/shard_map/ppermute | solution.py:55
  16.6 10.5 %collective-permute-start.1 = (s32[1,1152]{1,0:T(1,128)S(1)}, s32[1,1152]{1,0:T(1,128)S(1)}, u32[]{:S(2)}, u32[]{:S(2)}) collective-permute-start(s32[1,1152]{1,0:T(1,128)S(1)} %concatenate.54), channel_id=1, source_target_pairs={{0,1},{1,0},{16,17},{17,16},{2,3},{3,2},{18,19},{19,18},{4,5},{5,4... | collective-permute-start | bytes 13832 | tf_op jit(solution)/shard_map/ppermute | solution.py:55
  22.6 24.5 %all-to-all-start = ((bf16[4,144,1280]{2,1,0:T(8,128)(2,1)}), bf16[4,144,1280]{2,1,0:T(8,128)(2,1)}, u32[]{:S(2)}, u32[]{:S(2)}) async-start(bf16[4,144,1280]{2,1,0:T(8,128)(2,1)} %get-tuple-element.76), calls=%async_computation | async-start | bytes 2949120 | tf_op jit(solution)/shard_map/all_to_all | solution.py:89
  47.1 24.4 %collective-permute-start.2 = (bf16[4,144,1280]{2,1,0:T(8,128)(2,1)}, bf16[4,144,1280]{2,1,0:T(8,128)(2,1)}, u32[]{:S(2)}, u32[]{:S(2)}) collective-permute-start(bf16[4,144,1280]{2,1,0:T(8,128)(2,1)} %all-to-all-done.half_ref), channel_id=1, source_target_pairs={{0,1},{1,0},{16,17},{17,16},{2,3},{3,2},{18,19},{19,18},{4,5},{5,4... | collective-permute-start | bytes 4423688 | tf_op jit(solution)/shard_map/ppermute | solution.py:55
  49.0 17.1 %collective-permute-start.6 = (bf16[352,1024]{1,0:T(8,128)(2,1)}, bf16[352,1024]{1,0:T(8,128)(2,1)}, u32[]{:S(2)}, u32[]{:S(2)}) collective-permute-start(bf16[352,1024]{1,0:T(8,128)(2,1)} %get-tuple-element.154), channel_id=1, source_target_pairs={{0,18},{17,1},{2,16},{19,3},{4,22},{21,5},{6,20},{23,7},{8,26},{25... | collective-permute-start | bytes 2162696 | tf_op jit(solution)/shard_map/ppermute | solution.py:55
  50.3 15.8 %collective-permute-start.5 = (bf16[352,1024]{1,0:T(8,128)(2,1)}, bf16[352,1024]{1,0:T(8,128)(2,1)}, u32[]{:S(2)}, u32[]{:S(2)}) collective-permute-start(bf16[352,1024]{1,0:T(8,128)(2,1)} %get-tuple-element.153), channel_id=1, source_target_pairs={{0,16},{17,3},{2,18},{19,1},{4,20},{21,7},{6,22},{23,5},{8,24},{25... | collective-permute-start | bytes 2162696 | tf_op jit(solution)/shard_map/ppermute | solution.py:55
  51.6 17.7 %collective-permute-start.4 = (bf16[128,1024]{1,0:T(8,128)(2,1)}, bf16[128,1024]{1,0:T(8,128)(2,1)}, u32[]{:S(2)}, u32[]{:S(2)}) collective-permute-start(bf16[128,1024]{1,0:T(8,128)(2,1)} %bitcast.15), channel_id=1, source_target_pairs={{0,0},{1,16},{16,1},{17,17},{2,2},{3,18},{18,3},{19,19},{4,4},{5,2... | collective-permute-start | bytes 786440 | tf_op jit(solution)/shard_map/ppermute | solution.py:55
  56.0 14.8 %collective-permute-start.3 = (bf16[4,128,256]{2,1,0:T(8,128)(2,1)}, bf16[4,128,256]{2,1,0:T(8,128)(2,1)S(1)}, u32[]{:S(2)}, u32[]{:S(2)}) collective-permute-start(bf16[4,128,256]{2,1,0:T(8,128)(2,1)} %slice.137), channel_id=1, source_target_pairs={{0,16},{1,17},{16,2},{17,3},{2,18},{3,19},{18,0},{19,1},{4,20},{5,... | collective-permute-start | bytes 786440 | tf_op jit(solution)/shard_map/ppermute | solution.py:55
  62.3 29.4 %all-to-all-start.1 = ((bf16[4,128,1152]{2,1,0:T(8,128)(2,1)}), bf16[4,128,1152]{2,1,0:T(8,128)(2,1)S(1)}, u32[]{:S(2)}, u32[]{:S(2)}) async-start(bf16[4,128,1152]{2,1,0:T(8,128)(2,1)} %get-tuple-element.88), calls=%async_computation.1 | async-start | bytes 2359296 | tf_op jit(solution)/shard_map/all_to_all | solution.py:89
  65.9 99.2 %all-gather.2.cloned.1.call-start = ((), (), s32[]{:S(2)}) async-start(), calls=%async_computation.9 | async-start | bytes 2359296 | tf_op jit(solution)/shard_map/all_gather | solution.py:664
  98.0 27.1 %all-to-all-start.2 = ((bf16[4,128,1024]{2,1,0:T(8,128)(2,1)}), bf16[4,128,1024]{2,1,0:T(8,128)(2,1)S(1)}, u32[]{:S(2)}, u32[]{:S(2)}) async-start(bf16[4,128,1024]{2,1,0:T(8,128)(2,1)} %bitcast.195), calls=%async_computation.2 | async-start | bytes 2097152 | tf_op jit(solution)/shard_map/all_to_all | solution.py:89
  143.9 20.2 %collective-permute-start.8 = (bf16[512,1024]{1,0:T(8,128)(2,1)S(1)}, bf16[512,1024]{1,0:T(8,128)(2,1)S(1)}, u32[]{:S(2)}, u32[]{:S(2)}) collective-permute-start(bf16[512,1024]{1,0:T(8,128)(2,1)S(1)} %bitcast.168), channel_id=1, source_target_pairs={{0,1},{1,0},{16,17},{17,16},{2,3},{3,2},{18,19},{19,18},{4,5},{5,4... | collective-permute-start | bytes 3145736 | tf_op jit(solution)/shard_map/ppermute | solution.py:55
  145.8 16.6 %collective-permute-start.9 = (bf16[2,128,1152]{2,1,0:T(8,128)(2,1)S(1)}, bf16[2,128,1152]{2,1,0:T(8,128)(2,1)S(1)}, u32[]{:S(2)}, u32[]{:S(2)}) collective-permute-start(bf16[2,128,1152]{2,1,0:T(8,128)(2,1)S(1)} %get-tuple-element.156), channel_id=1, source_target_pairs={{0,16},{1,17},{16,2},{17,3},{2,18},{3,19},{18,0},{19,1},{4,20},{5,... | collective-permute-start | bytes 1769480 | tf_op jit(solution)/shard_map/ppermute | solution.py:55
  147.6 15.7 %collective-permute-start.10 = (bf16[2,128,1152]{2,1,0:T(8,128)(2,1)S(1)}, bf16[2,128,1152]{2,1,0:T(8,128)(2,1)S(1)}, u32[]{:S(2)}, u32[]{:S(2)}) collective-permute-start(bf16[2,128,1152]{2,1,0:T(8,128)(2,1)S(1)} %get-tuple-element.155), channel_id=1, source_target_pairs={{0,18},{1,19},{16,0},{17,1},{2,16},{3,17},{18,2},{19,3},{4,22},{5,... | collective-permute-start | bytes 1769480 | tf_op jit(solution)/shard_map/ppermute | solution.py:55
  191.3 18.7 %all-to-all-start.4 = ((bf16[4,128,1024]{2,1,0:T(8,128)(2,1)}), bf16[4,128,1024]{2,1,0:T(8,128)(2,1)S(1)}, u32[]{:S(2)}, u32[]{:S(2)}) async-start(bf16[4,128,1024]{2,1,0:T(8,128)(2,1)} %bitcast.196), calls=%async_computation.5 | async-start | bytes 2097152 | tf_op jit(solution)/shard_map/all_to_all | solution.py:89
  211.7 8.9 %collective-permute-start.15 = (bf16[128,1024]{1,0:T(8,128)(2,1)S(1)}, bf16[128,1024]{1,0:T(8,128)(2,1)S(1)}, u32[]{:S(2)}, u32[]{:S(2)}) collective-permute-start(bf16[128,1024]{1,0:T(8,128)(2,1)S(1)} %fusion.46), channel_id=1, source_target_pairs={{0,32},{1,33},{16,48},{17,49},{2,34},{3,35},{18,50},{19,51},{4,36}... | collective-permute-start | bytes 786440 | tf_op jit(solution)/shard_map/ppermute | solution.py:55
  212.1 13.0 %collective-permute-start.14 = (bf16[128,1024]{1,0:T(8,128)(2,1)S(1)}, bf16[128,1024]{1,0:T(8,128)(2,1)S(1)}, u32[]{:S(2)}, u32[]{:S(2)}) collective-permute-start(bf16[128,1024]{1,0:T(8,128)(2,1)S(1)} %fusion.46), channel_id=1, source_target_pairs={{0,64},{1,65},{16,80},{17,81},{2,66},{3,67},{18,82},{19,83},{4,68}... | collective-permute-start | bytes 786440 | tf_op jit(solution)/shard_map/ppermute | solution.py:55
  214.0 12.2 %collective-permute-start.13 = (bf16[128,1024]{1,0:T(8,128)(2,1)S(1)}, bf16[128,1024]{1,0:T(8,128)(2,1)S(1)}, u32[]{:S(2)}, u32[]{:S(2)}) collective-permute-start(bf16[128,1024]{1,0:T(8,128)(2,1)S(1)} %fusion.46), channel_id=1, source_target_pairs={{0,96},{1,97},{16,112},{17,113},{2,98},{3,99},{18,114},{19,115},{4... | collective-permute-start | bytes 786440 | tf_op jit(solution)/shard_map/ppermute | solution.py:55
  226.3 9.0 %collective-permute-start.16 = (bf16[512,1024]{1,0:T(8,128)(2,1)S(1)}, bf16[512,1024]{1,0:T(8,128)(2,1)}, u32[]{:S(2)}, u32[]{:S(2)}) collective-permute-start(bf16[512,1024]{1,0:T(8,128)(2,1)S(1)} %pad_maximum_fusion.2.near_ref), channel_id=1, source_target_pairs={{0,1},{1,0},{16,17},{17,16},{2,3},{3,2},{18,19},{19,18},{4,5},{5,4... | collective-permute-start | bytes 3145736 | tf_op jit(solution)/shard_map/ppermute | solution.py:55
  228.3 62.4 %all-to-all-start.5 = ((bf16[16,108,8,128]{3,2,1,0:T(8,128)(2,1)}), bf16[16,108,8,128]{3,2,1,0:T(8,128)(2,1)}, u32[]{:S(2)}, u32[]{:S(2)}) async-start(bf16[16,108,8,128]{3,2,1,0:T(8,128)(2,1)} %pad_maximum_fusion), calls=%async_computation.6 | async-start | bytes 7077888 | tf_op jit(solution)/shard_map/all_to_all | solution.py:89
  234.2 149.6 %reduce-scatter.2.cloned.1.call-start = ((), (), s32[]{:S(2)}) async-start(), calls=%async_computation.10 | async-start | bytes 2359296 | tf_op jit(solution)/shard_map/reduce_scatter | solution.py:696
  263.5 15.0 %collective-permute-start.19 = (bf16[128,1024]{1,0:T(8,128)(2,1)}, bf16[128,1024]{1,0:T(8,128)(2,1)S(1)}, u32[]{:S(2)}, u32[]{:S(2)}) collective-permute-start(bf16[128,1024]{1,0:T(8,128)(2,1)} %get-tuple-element.119), channel_id=1, source_target_pairs={{0,64},{1,65},{16,80},{17,81},{2,66},{3,67},{18,82},{19,83},{4,68}... | collective-permute-start | bytes 786440 | tf_op jit(solution)/shard_map/ppermute | solution.py:55
  266.8 11.7 %collective-permute-start.20 = (bf16[128,1024]{1,0:T(8,128)(2,1)}, bf16[128,1024]{1,0:T(8,128)(2,1)S(1)}, u32[]{:S(2)}, u32[]{:S(2)}) collective-permute-start(bf16[128,1024]{1,0:T(8,128)(2,1)} %get-tuple-element.120), channel_id=1, source_target_pairs={{0,96},{1,97},{16,112},{17,113},{2,98},{3,99},{18,114},{19,115},{4... | collective-permute-start | bytes 786440 | tf_op jit(solution)/shard_map/ppermute | solution.py:55
  267.7 17.6 %collective-permute-start.21 = (bf16[4,32,8,128]{3,2,1,0:T(8,128)(2,1)}, bf16[4,32,8,128]{3,2,1,0:T(8,128)(2,1)S(1)}, u32[]{:S(2)}, u32[]{:S(2)}) collective-permute-start(bf16[4,32,8,128]{3,2,1,0:T(8,128)(2,1)} %get-tuple-element.159), channel_id=1, source_target_pairs={{0,4},{1,5},{16,20},{17,21},{2,6},{3,7},{18,22},{19,23},{4,8},{5,9... | collective-permute-start | bytes 786440 | tf_op jit(solution)/shard_map/ppermute | solution.py:55
  269.3 21.4 %collective-permute-start.22 = (bf16[4,32,8,128]{3,2,1,0:T(8,128)(2,1)}, bf16[4,32,8,128]{3,2,1,0:T(8,128)(2,1)S(1)}, u32[]{:S(2)}, u32[]{:S(2)}) collective-permute-start(bf16[4,32,8,128]{3,2,1,0:T(8,128)(2,1)} %get-tuple-element.158), channel_id=1, source_target_pairs={{0,8},{1,9},{16,24},{17,25},{2,10},{3,11},{18,26},{19,27},{4,12},{... | collective-permute-start | bytes 786440 | tf_op jit(solution)/shard_map/ppermute | solution.py:55
  272.3 18.4 %collective-permute-start.23 = (bf16[4,32,8,128]{3,2,1,0:T(8,128)(2,1)}, bf16[4,32,8,128]{3,2,1,0:T(8,128)(2,1)S(1)}, u32[]{:S(2)}, u32[]{:S(2)}) collective-permute-start(bf16[4,32,8,128]{3,2,1,0:T(8,128)(2,1)} %get-tuple-element.157), channel_id=1, source_target_pairs={{0,12},{1,13},{16,28},{17,29},{2,14},{3,15},{18,30},{19,31},{4,0},... | collective-permute-start | bytes 786440 | tf_op jit(solution)/shard_map/ppermute | solution.py:55
  294.2 11.2 %all-to-all-start.6 = ((bf16[4,2,9,8,128]{4,3,2,1,0:T(8,128)(2,1)}), bf16[4,2,9,8,128]{4,3,2,1,0:T(8,128)(2,1)S(1)}, u32[]{:S(2)}, u32[]{:S(2)}) async-start(bf16[4,2,9,8,128]{4,3,2,1,0:T(8,128)(2,1)} %bitcast.81), calls=%async_computation.7 | async-start | bytes 294912 | tf_op jit(solution)/shard_map/all_to_all | solution.py:89
  316.2 36.0 %all-to-all-start.7 = ((bf16[16,576,128]{2,1,0:T(8,128)(2,1)}), bf16[16,576,128]{2,1,0:T(8,128)(2,1)S(1)}, u32[]{:S(2)}, u32[]{:S(2)}) async-start(bf16[16,576,128]{2,1,0:T(8,128)(2,1)} %constant_dynamic-update-slice_fusion), calls=%async_computation.8 | async-start | bytes 4718592 | tf_op jit(solution)/shard_map/all_to_all | solution.py:89
  329.7 9.7 %collective-permute-start.26 = (bf16[32,8,128]{2,1,0:T(8,128)(2,1)S(1)}, bf16[32,8,128]{2,1,0:T(8,128)(2,1)S(1)}, u32[]{:S(2)}, u32[]{:S(2)}) collective-permute-start(bf16[32,8,128]{2,1,0:T(8,128)(2,1)S(1)} %get-tuple-element.162), channel_id=1, source_target_pairs={{0,2},{1,3},{16,18},{17,19},{2,0},{3,1},{18,16},{19,17},{4,6},{5,7... | collective-permute-start | bytes 196616 | tf_op jit(solution)/shard_map/ppermute | solution.py:55
  330.2 19.9 %collective-permute-start.25 = (bf16[32,8,128]{2,1,0:T(8,128)(2,1)S(1)}, bf16[32,8,128]{2,1,0:T(8,128)(2,1)S(1)}, u32[]{:S(2)}, u32[]{:S(2)}) collective-permute-start(bf16[32,8,128]{2,1,0:T(8,128)(2,1)S(1)} %get-tuple-element.160), channel_id=1, source_target_pairs={{0,16},{1,17},{16,2},{17,3},{2,18},{3,19},{18,0},{19,1},{4,20},{5,... | collective-permute-start | bytes 196616 | tf_op jit(solution)/shard_map/ppermute | solution.py:55
  352.2 50.0 %collective-permute-start.38 = (bf16[16,576,128]{2,1,0:T(8,128)(2,1)S(1)}, bf16[16,576,128]{2,1,0:T(8,128)(2,1)}, u32[]{:S(2)}, u32[]{:S(2)}) collective-permute-start(bf16[16,576,128]{2,1,0:T(8,128)(2,1)S(1)} %all-to-all-done.7.mine_ref), channel_id=1, source_target_pairs={{0,1},{1,0},{16,17},{17,16},{2,3},{3,2},{18,19},{19,18},{4,5},{5,4... | collective-permute-start | bytes 7077896 | tf_op jit(solution)/shard_map/ppermute | solution.py:55
  379.1 19.0 %collective-permute-start.37 = (bf16[4,4,160,128]{3,2,1,0:T(8,128)(2,1)S(1)}, bf16[4,4,160,128]{3,2,1,0:T(8,128)(2,1)}, u32[]{:S(2)}, u32[]{:S(2)}) collective-permute-start(bf16[4,4,160,128]{3,2,1,0:T(8,128)(2,1)S(1)} %pad_maximum_fusion.5.mine_ref), channel_id=1, source_target_pairs={{0,1},{1,0},{16,17},{17,16},{2,3},{3,2},{18,19},{19,18},{4,5},{5,4... | collective-permute-start | bytes 1966088 | tf_op jit(solution)/shard_map/ppermute | solution.py:55
  (71 other events, 576.2 us)
Sparse Core Ops, SparseCore 0:
  93.0 30.3 all-gather.1
  275.2 29.7 reduce-scatter.1

commit v3 on v2

--- a/solution.py
+++ b/solution.py
@@ -122,7 +122,10 @@
 
 def return_planes(got, by_block):
     both = [cat([got[:, parity].reshape(-1, 128), by_block.reshape(-1, 128)]) for parity in range(2)]
-    return exchange(jnp.stack(both * 8), planes)
+    both = jnp.stack(both)
+    return exchange(
+        jnp.broadcast_to(both[None], (8, *both.shape)).reshape(16, *both.shape[1:]), planes
+    )
 
 
 def exchange_x(by_row, x):
@@ -159,13 +162,8 @@
 
 
 def scatter_parts(own, got):
-    sums = [quarter(own, step) + quarter(got, step).astype(f32) for step in range(4)]
+    sums = [quarter(own, step).astype(f32) + quarter(got, step).astype(f32) for step in range(4)]
     return sums[0], [part.astype(bf16) for part in sums[1:]]
-
-
-def turn_back(rows, x):
-    blocks = rows.reshape(4, 128, rows.shape[1])
-    return lax.dynamic_slice_in_dim(cat([blocks, blocks]), x, 4, 0).reshape(rows.shape)
 
 
 def whole(count):
@@ -254,6 +252,18 @@
     return pl.pallas_call(
         pack_kernel, out_shape=jax.ShapeDtypeStruct((144, 1024), bf16)
     )(*arrays)
+
+
+def place_tables(facts, core):
+    places = facts[0, :1024].reshape(4, 2, 128)
+    places = jnp.stack([pick(places, core, 1), pick(places, 1 - core, 1)]).reshape(1, 1024)
+    starts = jnp.where(places >= facts[:, 1024:1025], facts[:, 1024:1025], 0)
+    lane = jnp.arange(128)
+    frequency = rope_base ** (-2.0 * (lane % 32).astype(f32) / HD)
+    angles = (places - starts).astype(f32).reshape(1024, 1) * frequency[None, :]
+    cosine, sine = jnp.cos(angles), jnp.sin(angles) * jnp.where(lane % 64 < 32, -1.0, 1.0)
+    places = places.astype(f32)
+    return cosine, sine, places.reshape(1024, 1), places, starts.astype(f32)
 
 
 def lanes(width):
@@ -359,7 +369,7 @@
     arrays = (half, far, across, gain, *tables)
     scratch = [pltpu.VMEM((128, 1024), bf16)]
     scalars = spot([where[4], where[3]])
-    return call(attend_kernel, scalars, arrays, outs, scratch, 44, 2 * 1024**3)
+    return call(attend_kernel, scalars, arrays, outs, scratch, 30, 2 * 1024**3)
 
 
 def attend_back_kernel(
@@ -434,16 +444,17 @@
         pre_grad_ref[rows, :] = pre_grad
         partial = matmul_nt(pre_grad, weight_ref[...])
         first_ref[0:1, :] += jnp.sum(partial * normed_ref[rows, :].astype(f32), axis=0, keepdims=True)
+        to = pl.ds(pl.multiple_of(((block % 4 + 4 - x) % 4) * 128, 128), 128)
         if block < 4:
-            own_ref[rows, :] = partial
+            own_ref[to, :] = partial.astype(bf16)
         else:
-            other_ref[(block - 4) * 128 : (block - 3) * 128, :] = partial.astype(bf16)
+            other_ref[to, :] = partial.astype(bf16)
 
 
 def attend_back(near, far, out_slot, kept, gain, tables, where):
     outs = [
         ((512, 1024), bf16),
-        ((512, 1024), f32),
+        ((512, 1024), bf16),
         ((1024, 256), bf16),
         ((128, 1024), f32),
         ((8, 256), f32),
@@ -456,7 +467,7 @@
         pltpu.VMEM((1024, 256), f32),
         pltpu.VMEM((128, 1024), bf16),
     ]
-    return call(attend_back_kernel, spot([where[0]]), arrays, outs, scratch, 48, 4 * 1024**3)
+    return call(attend_back_kernel, spot([where[0]]), arrays, outs, scratch, 36, 4 * 1024**3)
 
 
 def feed_kernel(
@@ -475,7 +486,7 @@
     normed_ref,
     weight_ref,
 ):
-    z_low, core = spot_ref[0], spot_ref[1]
+    z_low, core, x = spot_ref[0], spot_ref[1], spot_ref[2]
     for at in range(4):
         across = lower_ref if at < 2 else upper_ref
         for piece, parity in ((came_ref[at], z_low), (across[at % 2], 1 - z_low)):
@@ -506,14 +517,17 @@
         pre_grad_ref[rows, :] = pre_grad
         return matmul_nt(pre_grad, weight_ref[...])
 
+    def keep(ref, part, partial):
+        for step in range(2):
+            to = pl.multiple_of(((part * 2 + step + 4 - x) % 4) * 128, 128)
+            ref[pl.ds(to, 128), :] = partial[step * 128 : step * 128 + 128].astype(bf16)
+
     def other_half(part, carry):
-        rows = pl.ds(pl.multiple_of(part * 256, 256), 256)
-        other_ref[rows, :] = work(part * 256 + 512, part, 1 - core).astype(bf16)
+        keep(other_ref, part, work(part * 256 + 512, part, 1 - core))
         return carry
 
     def own_half(part, carry):
-        rows = pl.ds(pl.multiple_of(part * 256, 256), 256)
-        own_ref[rows, :] = work(part * 256, part, core)
+        keep(own_ref, part, work(part * 256, part, core))
         return carry
 
     lax.fori_loop(0, 2, other_half, 0)
@@ -524,14 +538,14 @@
     arrays = (half, far, upstream, *weights, down_slot)
     outs = [
         ((512, 1024), bf16),
-        ((512, 1024), f32),
+        ((512, 1024), bf16),
         ((1024, 576), bf16),
         ((1024, 1152), bf16),
         ((1024, 1024), bf16),
     ]
     scratch = [pltpu.VMEM((1024, 1152), bf16)]
-    scalars = spot([where[4], where[3]])
-    return call(feed_kernel, scalars, arrays, outs, scratch, 44, 6 * 1024**3)
+    scalars = spot([where[4], where[3], where[0]])
+    return call(feed_kernel, scalars, arrays, outs, scratch, 34, 6 * 1024**3)
 
 
 def feed_grads_kernel(spot_ref, mine_ref, other_ref, gate_ref, up_ref, down_ref):
@@ -634,36 +648,32 @@
     where = (x, y, z, core, z_low)
 
     facts = cat([token_places, jnp.broadcast_to(seq_lengths[:, :1], (1, 128))], 1)
-    facts = jnp.where(core == z_low, facts, send(facts, other_core))
-    places = facts[0, :1024].reshape(4, 2, 128)
-    places = jnp.stack([pick(places, core, 1), pick(places, 1 - core, 1)]).reshape(1, 1024)
-    starts = jnp.where(places >= facts[:, 1024:1025], facts[:, 1024:1025], 0)
-    lane = jnp.arange(128)
-    frequency = rope_base ** (-2.0 * (lane % 32).astype(f32) / HD)
-    angles = (places - starts).astype(f32).reshape(1024, 1) * frequency[None, :]
-    cosine, sine = jnp.cos(angles), jnp.sin(angles) * jnp.where(lane % 64 < 32, -1.0, 1.0)
-    places_f = places.astype(f32)
-    tables = (cosine, sine, places_f.reshape(1024, 1), places_f, starts.astype(f32))
-
     small = cat([query_gain, key_gain, jnp.zeros((112,), bf16)])
     packed = pack(tokens[0], attention_gain[None], feedforward_gain[None], small[None])
     packed = send(packed, regroup)
+    facts = jnp.where(core == z_low, facts, send(facts, other_core))
     packed_out, for_feed = pick_columns(
         query_weight, key_weight, value_weight, gate_weight, up_weight, packed, core
     )
+    packed_out, for_feed, facts, rows_mine, cotangent = join(
+        packed_out, for_feed, facts, (out_weight, down_weight), cotangent
+    )
     half = exchange(packed_out, x_rings)
-    rows_held = cat([out_weight, down_weight])
-    half, for_feed, rows_held, tables = join(half, for_feed, rows_held, tables)
-
+    tables = place_tables(facts, core)
+    upstream_own = send(cotangent[0], regroup)
+    rows_got = [send(rows_mine[0], z_up_home), send(rows_mine[1], z_down_home)]
+    out_slot, down_slot = (
+        jnp.where(core == z_low, mine, got) for mine, got in zip(rows_mine, rows_got)
+    )
+    half, for_feed, upstream_own, out_slot, down_slot, tables = join(
+        half, for_feed, upstream_own, out_slot, down_slot, tables
+    )
+
+    upstream = lax.all_gather(upstream_own, AXES, axis=0, axis_index_groups=x_groups, tiled=True)
+    far = send(half, other_core)
     across = send(half[:, :128, 1024:], z_up)
-    far = send(half, other_core)
-    rows_got = [send(rows_held[:352], z_up_home), send(rows_held[352:], z_down_home)]
     feed_came = exchange(for_feed, x_rings)
-    upstream_own = send(cotangent[0], regroup)
-    far, across, upstream_own = join(far, across, upstream_own)
-    upstream = lax.all_gather(upstream_own, AXES, axis=0, axis_index_groups=x_groups, tiled=True)
-    rows_slot = jnp.where(core == z_low, rows_held, cat(rows_got))
-    out_slot, down_slot = rows_slot[:128], rows_slot[128:]
+    far, across = join(far, across)
     inputs = packed[:128].astype(f32)
     notes = jnp.stack([half[:, 128, 256:272], far[:, 128, 256:272]], axis=1)
     notes = jnp.where(core == 0, notes, notes[:, ::-1]).astype(f32)
@@ -678,10 +688,10 @@
     other_half, mixed, feed_came = join(other_half, mixed, feed_came)
     got = send(other_half, other_core)
     own_half = matmul(mixed[:512], out_slot)
+    lower, upper = send(feed_came[:2], z_up), send(feed_came[2:], z_down)
     parts = scatter_sums(own_half, got)
-    parts, feed_came = join(parts, feed_came)
-
-    lower, upper = send(feed_came[:2], z_up), send(feed_came[2:], z_down)
+    parts, lower, upper = join(parts, lower, upper)
+
     middle = inputs + add_up(parts)
     second_scale = rms_scale(middle)
     half = gather_half((middle * second_scale * gain_second).astype(bf16)).reshape(512, 1024)
@@ -689,14 +699,10 @@
     other_half, own_half, hidden, pre_grad, normed_all = feed(
         half, far, upstream, (feed_came, lower, upper), down_slot, where
     )
-    got = send(other_half, other_core)
-    result_rows = matmul(hidden, down_slot).astype(bf16)
-    got, result_rows, pre_grad = join(got, result_rows, pre_grad)
-
-    result_sum = lax.psum_scatter(
-        result_rows, AXES, scatter_dimension=0, axis_index_groups=x_groups, tiled=True
-    )
-    parts = scatter_sums(own_half, got)
+    first, rest = scatter_parts(own_half, send(other_half, other_core))
+    first, rest, pre_grad, hidden, normed_all = join(first, rest, pre_grad, hidden, normed_all)
+
+    parts = send_x(*rest)
     feed_weight_grad = matmul_tn(normed_all, pre_grad)
     down_weight_grad = matmul_tn(hidden, upstream)
     feed_parts = cat(
@@ -706,15 +712,20 @@
         ],
         1,
     )
-    parts, feed_parts = join(parts, feed_parts)
-
+    first, parts, feed_parts, hidden = join(first, parts, feed_parts, hidden)
     feed_parts = exchange(feed_parts, planes)
-    second_grad = add_up(parts)
+    second_grad = first + add_up(jnp.stack(parts))
     middle_norm_grad, second_gain_terms = norm_back(middle, second_scale, gain_second, second_grad)
     middle_grad = upstream_own.astype(f32) + middle_norm_grad
     second_gain_grad = jnp.sum(second_gain_terms, axis=0)
-    near = cat(gather_x(middle_grad.astype(bf16)))
+    near = gather_x(middle_grad.astype(bf16))
+    result_rows = matmul(hidden, down_slot).astype(bf16)
+    near, result_rows = join(near, result_rows)
+    near = cat(near)
     far = send(near, other_core)
+    result_sum = lax.psum_scatter(
+        result_rows, AXES, scatter_dimension=0, axis_index_groups=x_groups, tiled=True
+    )
     other_half, own_half, pre_grad, out_weight_grad, gain_terms, first_terms = attend_back(
         near,
         far,
@@ -724,7 +735,12 @@
         tables,
         where,
     )
-    got = send(other_half, other_core)
+    first, rest = scatter_parts(own_half, send(other_half, other_core))
+    first, rest, pre_grad, feed_parts = join(first, rest, pre_grad, feed_parts)
+
+    parts = send_x(*rest)
+    feed_rows = add_up(feed_parts).astype(bf16)
+    feed_got = exchange_rows(feed_rows[:72].reshape(8, 9, 8, 128))
     attention_weight_grad = matmul_tn(first_normed, pre_grad)
     first_gain_grad = first_terms[0] / gain_first
     small = jnp.stack([gain_terms[0, :64] + gain_terms[0, 64:128], gain_terms[0, 128:192]], 1)
@@ -734,28 +750,32 @@
     by_row = rows_for_planes(cat([attention_weight_grad, extra], 1)).reshape(4, 4, 24, 8, 128)
     by_block = block_for_planes(out_weight_grad).reshape(4, 4, 8, 8, 128)
     attention_parts = cat([by_row, by_block], 2)
-    first, rest = scatter_parts(turn_back(own_half, x), turn_back(got, x))
-    first, rest, attention_parts = join(first, rest, attention_parts)
-
-    parts = send_x(*rest)
+    first, parts, attention_parts, feed_got, feed_rows = join(
+        first, parts, attention_parts, feed_got, feed_rows
+    )
     pieces = [pick(attention_parts, (y + step) % 4, 0) for step in range(4)]
     ring = send_ring(pieces, y_up, y_down, y_far)
-    first, parts, ring, feed_parts = join(first, parts, ring, feed_parts)
-    rows = add_up(feed_parts).astype(bf16)
-    feed_got = exchange_rows(rows[:72].reshape(8, 9, 8, 128))
-    feed_mine = return_planes(feed_got, rows[72:])
+    first_grad = first + add_up(jnp.stack(parts))
+    input_norm_grad, _ = norm_back(inputs, rms_scale(inputs), gain_first, first_grad)
+    input_grad = (middle_grad + input_norm_grad).astype(bf16)
+    ring, feed_got, feed_rows, input_grad = join(ring, feed_got, feed_rows, input_grad)
 
     rows = pieces[0].astype(f32) + add_up(jnp.stack(ring))
     pieces = [pick(rows, (z + step) % 4, 0) for step in range(4)]
     ring = send_ring(pieces, z_up, z_down, z_far)
+    feed_mine = return_planes(feed_got, feed_rows[72:])
+    result = (middle + result_sum.astype(f32)).astype(bf16)
+    ring, input_grad, result = join(ring, input_grad, result)
+
     rows = (pieces[0] + add_up(jnp.stack(ring))).astype(bf16)
     attention_got = exchange_x(rows[:24].reshape(8, 3, 8, 128), x)
-    first_grad = first + add_up(jnp.stack(parts))
-    input_norm_grad, _ = norm_back(inputs, rms_scale(inputs), gain_first, first_grad)
-    input_grad = middle_grad + input_norm_grad
-    result = send((middle + result_sum.astype(f32)).astype(bf16), regroup)
-    input_grad = send(input_grad.astype(bf16), regroup)
-    mine = gather_y(gather_z(attention_got, rows[24:], z_low))
+    result = send(result, regroup)
+    attention_got, result = join(attention_got, result)
+    input_grad = send(input_grad, regroup)
+    block, input_grad, feed_mine = join(
+        gather_z(attention_got, rows[24:], z_low), input_grad, feed_mine
+    )
+    mine = gather_y(block)
     query_sum, key_sum, value_sum, out_sum, gain_sums = attention_grads(
         mine, send(mine, other_core), where
     )

time: 423 us -> 375 us (0.89)
  waiting for transfers between devices: 132 us -> 99.6 us
  local copies, waits for them, and re-layouts: 34.1 us -> 46.8 us
  other arithmetic: 44.2 us -> 31.7 us
  Pallas kernels: 52.4 us -> 45.4 us
  starting transfers between devices: 105 us -> 98.3 us
    all_to_all x7 -> x6, waiting for transfers between devices: 53.6 us -> 19 us  [exchange(): return lax.all_to_all(values, AXES, 0, 0, axis_index_groups=groups)]
    unnamed x113 -> x124, local copies, waits for them, and re-layouts: 20.7 us -> 34.2 us
    unnamed x16 -> x1, other arithmetic: 10.1 us -> 0.01 us
    pallas_call x6, Pallas kernels: 50.7 us -> 43.7 us  [call(): pl.pallas_call(kernel, out_shape=[jax.ShapeDtypeStruct(shape, kind) for s...]
    concatenate x9 -> x5, other arithmetic: 8 us -> 3.06 us  [cat(): return jnp.concatenate(pieces, axis=axis)]
    ppermute x39 -> x42, starting transfers between devices: 69.6 us -> 64.9 us  [send(): return lax.ppermute(values, AXES, moves)]
    all_to_all x7 -> x6, starting transfers between devices: 35.2 us -> 32.9 us  [exchange(): return lax.all_to_all(values, AXES, 0, 0, axis_index_groups=groups)]
    ppermute x39 -> x42, waiting for transfers between devices: 78.4 us -> 80.5 us  [send(): return lax.ppermute(values, AXES, moves)]
  transfers between devices with their start and end apart: 48 -> 50, of which waited for: 28 -> 24; matrix products, arithmetic and copies ran while one was open for 16% -> 15% of each run, Pallas kernels for 8% -> 8%
where the time goes in v3:
time: 375 us; the launch traced here: 369 us
  waiting for transfers between devices  99.6 us (27%)
  starting transfers between devices  98.3 us (26%)
  local copies, waits for them, and re-layouts  46.8 us (12%)
  Pallas kernels  45.4 us (12%)
  other arithmetic  31.7 us (8%)
  blocking collectives  17.4 us (5%)
  between operations  15.4 us (4%)
  matrix products  14.4 us (4%)
    ppermute x42, waiting for transfers between devices, send(): return lax.ppermute(values, AXES, moves)  80.5 us
    ppermute x42, starting transfers between devices, send(): return lax.ppermute(values, AXES, moves)  64.9 us
    pallas_call x6, Pallas kernels, call(): pl.pallas_call(kernel, out_shape=[jax.ShapeDtypeStruct(shape, kind) for s...  43.7 us
    unnamed x124, local copies, waits for them, and re-layouts  34.2 us
    all_to_all x6, starting transfers between devices, exchange(): return lax.all_to_all(values, AXES, 0, 0, axis_index_groups=groups)  32.9 us
    all_to_all x6, waiting for transfers between devices, exchange(): return lax.all_to_all(values, AXES, 0, 0, axis_index_groups=groups)  19 us
    all_to_all x1, blocking collectives, exchange(): return lax.all_to_all(values, AXES, 0, 0, axis_index_groups=groups)  17.4 us
  transfers between devices with their start and end apart: 50, of which 24 were waited for; matrix products, arithmetic and copies ran while one was open for 15% of the time, Pallas kernels for 8%

profile of v3, /device:TPU:1, one launch (start us, length us, event | category | flops | bytes accessed | tf_op | source)
XLA Modules:
  0.0 369.0 jit_solution(1427571825235134067)
XLA Ops:
  13.0 3.5 collective-permute-start
  17.9 3.3 collective-permute-done.packed_ref
  33.0 4.1 %all-to-all-start = ((bf16[4,144,1280]{2,1,0:T(8,128)(2,1)}), bf16[4,144,1280]{2,1,0:T(8,128)(2,1)S(1)}, u32[]{:S(2)}, u32[]{:S(2)}) async-start(bf16[4,144,1280]{2,1,0:T(8,128)(2,1)} %copy-done), calls=%async_computation | async-start | bytes 2949120 | tf_op jit(solution)/shard_map/all_to_all | solution.py:89
  38.4 3.7 %collective-permute-start.2 = (bf16[128,1024]{1,0:T(8,128)(2,1)}, bf16[128,1024]{1,0:T(8,128)(2,1)S(1)}, u32[]{:S(2)}, u32[]{:S(2)}) collective-permute-start(bf16[128,1024]{1,0:T(8,128)(2,1)} %bitcast.187), channel_id=1, source_target_pairs={{0,0},{1,16},{16,1},{17,17},{2,2},{3,18},{18,3},{19,19},{4,4},{5,2... | collective-permute-start | bytes 786440 | tf_op jit(solution)/shard_map/ppermute | solution.py:55
  42.1 3.1 fusion.7
  46.2 3.7 collective-permute-done.4
  52.3 5.4 %collective-permute-start.5 = (bf16[4,144,1280]{2,1,0:T(8,128)(2,1)S(1)}, bf16[4,144,1280]{2,1,0:T(8,128)(2,1)}, u32[]{:S(2)}, u32[]{:S(2)}) collective-permute-start(bf16[4,144,1280]{2,1,0:T(8,128)(2,1)S(1)} %all-to-all-done.half_ref), channel_id=1, source_target_pairs={{0,1},{1,0},{16,17},{17,16},{2,3},{3,2},{18,19},{19,18},{4,5},{5,4... | collective-permute-start | bytes 4423688 | tf_op jit(solution)/shard_map/ppermute | solution.py:55
  61.2 3.5 all-to-all-start.1
  65.3 3.4 collective-permute-done.6.across_ref
  74.5 11.4 %shard_map.248 = (bf16[1024,256]{1,0:T(8,128)(2,1)S(1)}, bf16[1024,1024]{1,0:T(8,128)(2,1)S(1)}, bf16[1024,256]{1,0:T(8,128)(2,1)S(1)}, f32[1024,256]{1,0:T(8,12...) custom-call(s32[2]{0:T(128)S(1)} %pad_add_fusion.1.spot_ref, ...), custom_call_target="tpu_custom_call" | custom-call | flops 2147483648 | bytes 4273152 | tf_op jit(solution)/shard_map/pallas_call | solution.py:179
  98.1 4.3 %all-to-all-start.2 = ((bf16[4,128,1024]{2,1,0:T(8,128)(2,1)}), bf16[4,128,1024]{2,1,0:T(8,128)(2,1)}, u32[]{:S(2)}, u32[]{:S(2)}) async-start(bf16[4,128,1024]{2,1,0:T(8,128)(2,1)} %bitcast.18), calls=%async_computation.2 | async-start | bytes 2097152 | tf_op jit(solution)/shard_map/all_to_all | solution.py:89
  105.2 13.2 %collective-permute-done.8.lower_ref = bf16[2,128,1152]{2,1,0:T(8,128)(2,1)S(1)} collective-permute-done((bf16[2,128,1152]{2,1,0:T(8,128)(2,1)S(1)}, bf16[2,128,1152]{2,1,0:T(8,128)(2,1)S(1)}, u32[]{:S(2)}, u32[]{:S(2)}) %collective-permute-start.8) | collective-permute-done | bytes 589856 | tf_op jit(solution)/shard_map/ppermute | solution.py:55
  118.4 6.4 %all-to-all-done.2 = bf16[4,128,1024]{2,1,0:T(8,128)(2,1)} async-done(((bf16[4,128,1024]{2,1,0:T(8,128)(2,1)}), bf16[4,128,1024]{2,1,0:T(8,128)(2,1)}, u32[]{:S(2)}, u32[]{:S(2)}) %all-to-all-start.2) | async-done | bytes 1048608 | tf_op jit(solution)/shard_map/all_to_all | solution.py:89
  128.0 17.4 %all_to_all.35 = bf16[4,128,1024]{2,1,0:T(8,128)(2,1)} all-to-all(bf16[4,128,1024]{2,1,0:T(8,128)(2,1)S(1)} %broadcast_in_dim.86), channel_id=1, replica_groups={{0,32,64,96},{16,48,80,112},{2,34,66,98},{18,50,82,114},{4,36,68,100},{..., dimensions={0} | all-to-all | bytes 2097152 | tf_op jit(solution)/shard_map/all_to_all | solution.py:89
  153.9 10.5 %shard_map.249 = (bf16[512,1024]{1,0:T(8,128)(2,1)S(1)}, bf16[512,1024]{1,0:T(8,128)(2,1)S(1)}, bf16[1024,576]{1,0:T(8,128)(2,1)S(1)}, bf16[1024,1152]{1,0:T(8,128)(2,1)S(1)}, bf16[1024,1024]{1,0:T(8,128)(2,1)S(1)}) custom-call(s32[3]{0:T(128)S(1)} %pad_add_fusion.2.spot_ref, bf16[512,1024]{1,0:T(8,128)(2,1)} %bitcast.20.half_ref, ...), custom_call_target="tpu_custom_call" | custom-call | flops 6442450944 | bytes 7733248 | tf_op jit(solution)/shard_map/pallas_call | solution.py:179
  170.4 3.2 convolution_convert_fusion
  177.6 3.8 %collective-permute-done.13 = bf16[128,1024]{1,0:T(8,128)(2,1)S(1)} collective-permute-done((bf16[128,1024]{1,0:T(8,128)(2,1)S(1)}, bf16[128,1024]{1,0:T(8,128)(2,1)S(1)}, u32[]{:S(2)}, u32[]{:S(2)}) %collective-permute-start.13) | collective-permute-done | bytes 262176 | tf_op jit(solution)/shard_map/ppermute | solution.py:55
  183.8 2.9 collective-permute-start.15
  187.4 6.8 %all-to-all-start.4 = ((bf16[16,108,8,128]{3,2,1,0:T(8,128)(2,1)}), bf16[16,108,8,128]{3,2,1,0:T(8,128)(2,1)}, u32[]{:S(2)}, u32[]{:S(2)}) async-start(bf16[16,108,8,128]{3,2,1,0:T(8,128)(2,1)} %pad_maximum_fusion), calls=%async_computation.4 | async-start | bytes 7077888 | tf_op jit(solution)/shard_map/all_to_all | solution.py:89
  194.2 4.4 %convolution_convert_fusion.1 = bf16[1024,1024]{1,0:T(8,128)(2,1)} fusion(bf16[1024,576]{1,0:T(8,128)(2,1)} %copy-done.22, bf16[576,1024]{1,0:T(8,128)(2,1)S(1)} %copy-done.4), kind=kOutput, calls=%fused_computation.4 | convolution fusion | flops 1209008128 | bytes 4456448 | tf_op jit(solution)/shard_map/dot_general | solution.py:202
  198.7 3.1 collective-permute-done.17
  214.3 12.6 %shard_map.250 = (bf16[512,1024]{1,0:T(8,128)(2,1)}, bf16[512,1024]{1,0:T(8,128)(2,1)S(1)}, bf16[1024,256]{1,0:T(8,128)(2,1)S(1)}, f32[128,1024]{1,0:T(8,128)S(1...) custom-call(s32[1]{0:T(128)} %bitcast.spot_ref, bf16[512,1024]{1,0:T(8,128)(2,1)S(1)} %constant_dynamic-update-slice_fusion.near_ref, ...), custom_call_target="tpu_custom_call" | custom-call | flops 4294967296 | bytes 8958976 | tf_op jit(solution)/shard_map/pallas_call | solution.py:179
  233.2 5.8 %all-to-all-done.4 = bf16[16,108,8,128]{3,2,1,0:T(8,128)(2,1)} async-done(((bf16[16,108,8,128]{3,2,1,0:T(8,128)(2,1)}), bf16[16,108,8,128]{3,2,1,0:T(8,128)(2,1)}, u32[]{:S(2)}, u32[]{:S(2)}) %all-to-all-start.4) | async-done | bytes 3538976 | tf_op jit(solution)/shard_map/all_to_all | solution.py:89
  249.4 4.0 %all-to-all-start.5 = ((bf16[4,2,9,8,128]{4,3,2,1,0:T(8,128)(2,1)}), bf16[4,2,9,8,128]{4,3,2,1,0:T(8,128)(2,1)}, u32[]{:S(2)}, u32[]{:S(2)}) async-start(bf16[4,2,9,8,128]{4,3,2,1,0:T(8,128)(2,1)} %bitcast.37), calls=%async_computation.5 | async-start | bytes 294912 | tf_op jit(solution)/shard_map/all_to_all | solution.py:89
  253.5 6.8 %all-to-all-done.5 = bf16[4,2,9,8,128]{4,3,2,1,0:T(8,128)(2,1)} async-done(((bf16[4,2,9,8,128]{4,3,2,1,0:T(8,128)(2,1)}), bf16[4,2,9,8,128]{4,3,2,1,0:T(8,128)(2,1)}, u32[]{:S(2)}, u32[]{:S(2)}) %all-to-all-start.5) | async-done | bytes 147488 | tf_op jit(solution)/shard_map/all_to_all | solution.py:89
  265.7 4.8 %collective-permute-done.23 = bf16[4,32,8,128]{3,2,1,0:T(8,128)(2,1)S(1)} collective-permute-done((bf16[4,32,8,128]{3,2,1,0:T(8,128)(2,1)S(1)}, bf16[4,32,8,128]{3,2,1,0:T(8,128)(2,1)S(1)}, u32[]{:S(2)}, u32[]{:S(2)}) %collective-permute-start.23) | collective-permute-done | bytes 262176 | tf_op jit(solution)/shard_map/ppermute | solution.py:55
  273.9 10.3 %all-to-all-start.6 = ((bf16[16,576,128]{2,1,0:T(8,128)(2,1)}), bf16[16,576,128]{2,1,0:T(8,128)(2,1)S(1)}, u32[]{:S(2)}, u32[]{:S(2)}) async-start(bf16[16,576,128]{2,1,0:T(8,128)(2,1)} %bitcast.139), calls=%async_computation.7 | async-start | bytes 4718592 | tf_op jit(solution)/shard_map/all_to_all | solution.py:89
  294.0 16.5 %collective-permute-done.26 = bf16[32,8,128]{2,1,0:T(8,128)(2,1)S(1)} collective-permute-done((bf16[32,8,128]{2,1,0:T(8,128)(2,1)}, bf16[32,8,128]{2,1,0:T(8,128)(2,1)S(1)}, u32[]{:S(2)}, u32[]{:S(2)}) %collective-permute-start.26) | collective-permute-done | bytes 65568 | tf_op jit(solution)/shard_map/ppermute | solution.py:55
  315.9 7.2 %collective-permute-start.32 = (bf16[128,1024]{1,0:T(8,128)(2,1)S(1)}, bf16[128,1024]{1,0:T(8,128)(2,1)S(1)}, u32[]{:S(2)}, u32[]{:S(2)}) collective-permute-start(bf16[128,1024]{1,0:T(8,128)(2,1)S(1)} %add_convert_fusion.1), channel_id=1, source_target_pairs={{0,0},{1,16},{16,1},{17,17},{2,2},{3,18},{18,3},{19,19},{4,4},{5,2... | collective-permute-start | bytes 786440 | tf_op jit(solution)/shard_map/ppermute | solution.py:55
  339.5 3.0 collective-permute-done.37
  345.1 4.2 %collective-permute-done.39 = bf16[4,160,128]{2,1,0:T(8,128)(2,1)S(1)} collective-permute-done((bf16[4,160,128]{2,1,0:T(8,128)(2,1)S(1)}, bf16[4,160,128]{2,1,0:T(8,128)(2,1)S(1)}, u32[]{:S(2)}, u32[]{:S(2)}) %collective-permute-start.39) | collective-permute-done | bytes 163872 | tf_op jit(solution)/shard_map/ppermute | solution.py:55
  356.0 5.2 %shard_map.252 = (f32[128,4608]{1,0:T(8,128)}, f32[128,4608]{1,0:T(8,128)}, f32[576,1024]{1,0:T(8,128)}) custom-call(s32[2]{0:T(128)S(1)} %pad_add_fusion.3.spot_ref, bf16[16,576,128]{2,1,0:T(8,128)(2,1)S(1)} %all-to-all-done.6.mine_ref, bf16[16,576,128]{2,1,0:T(8,128)(2,1)} %collective-permute-done.41.other_ref), custom_call_target="tpu_custom_call" | custom-call | bytes 4718592 | tf_op jit(solution)/shard_map/pallas_call | solution.py:179
  (296 shorter events, 152.0 us)
Async XLA Ops:
  29.8 20.0 %collective-permute-start.4 = (bf16[576,1024]{1,0:T(8,128)(2,1)S(1)}, bf16[576,1024]{1,0:T(8,128)(2,1)}, u32[]{:S(2)}, u32[]{:S(2)}) collective-permute-start(bf16[576,1024]{1,0:T(8,128)(2,1)S(1)} %copy-done.43), channel_id=1, source_target_pairs={{0,18},{17,1},{2,16},{19,3},{4,22},{21,5},{6,20},{23,7},{8,26},{25... | collective-permute-start | bytes 3538952 | tf_op jit(solution)/shard_map/ppermute | solution.py:55
  31.7 13.5 %collective-permute-start.3 = (bf16[128,1024]{1,0:T(8,128)(2,1)S(1)}, bf16[128,1024]{1,0:T(8,128)(2,1)}, u32[]{:S(2)}, u32[]{:S(2)}) collective-permute-start(bf16[128,1024]{1,0:T(8,128)(2,1)S(1)} %copy-done.55), channel_id=1, source_target_pairs={{0,16},{17,3},{2,18},{19,1},{4,20},{21,7},{6,22},{23,5},{8,24},{25... | collective-permute-start | bytes 786440 | tf_op jit(solution)/shard_map/ppermute | solution.py:55
  33.0 19.4 %all-to-all-start = ((bf16[4,144,1280]{2,1,0:T(8,128)(2,1)}), bf16[4,144,1280]{2,1,0:T(8,128)(2,1)S(1)}, u32[]{:S(2)}, u32[]{:S(2)}) async-start(bf16[4,144,1280]{2,1,0:T(8,128)(2,1)} %copy-done), calls=%async_computation | async-start | bytes 2949120 | tf_op jit(solution)/shard_map/all_to_all | solution.py:89
  38.4 13.9 %collective-permute-start.2 = (bf16[128,1024]{1,0:T(8,128)(2,1)}, bf16[128,1024]{1,0:T(8,128)(2,1)S(1)}, u32[]{:S(2)}, u32[]{:S(2)}) collective-permute-start(bf16[128,1024]{1,0:T(8,128)(2,1)} %bitcast.187), channel_id=1, source_target_pairs={{0,0},{1,16},{16,1},{17,17},{2,2},{3,18},{18,3},{19,19},{4,4},{5,2... | collective-permute-start | bytes 786440 | tf_op jit(solution)/shard_map/ppermute | solution.py:55
  52.3 17.0 %collective-permute-start.5 = (bf16[4,144,1280]{2,1,0:T(8,128)(2,1)S(1)}, bf16[4,144,1280]{2,1,0:T(8,128)(2,1)}, u32[]{:S(2)}, u32[]{:S(2)}) collective-permute-start(bf16[4,144,1280]{2,1,0:T(8,128)(2,1)S(1)} %all-to-all-done.half_ref), channel_id=1, source_target_pairs={{0,1},{1,0},{16,17},{17,16},{2,3},{3,2},{18,19},{19,18},{4,5},{5,4... | collective-permute-start | bytes 4423688 | tf_op jit(solution)/shard_map/ppermute | solution.py:55
  61.2 30.8 %all-to-all-start.1 = ((bf16[4,128,1152]{2,1,0:T(8,128)(2,1)}), bf16[4,128,1152]{2,1,0:T(8,128)(2,1)S(1)}, u32[]{:S(2)}, u32[]{:S(2)}) async-start(bf16[4,128,1152]{2,1,0:T(8,128)(2,1)} %copy-done.3), calls=%async_computation.1 | async-start | bytes 2359296 | tf_op jit(solution)/shard_map/all_to_all | solution.py:89
  64.7 82.9 %all-gather.2.cloned.1.call-start = ((), (), s32[]{:S(2)}) async-start(), calls=%async_computation.8 | async-start | bytes 2359296 | tf_op jit(solution)/shard_map/all_gather | solution.py:672
  98.1 26.7 %all-to-all-start.2 = ((bf16[4,128,1024]{2,1,0:T(8,128)(2,1)}), bf16[4,128,1024]{2,1,0:T(8,128)(2,1)}, u32[]{:S(2)}, u32[]{:S(2)}) async-start(bf16[4,128,1024]{2,1,0:T(8,128)(2,1)} %bitcast.18), calls=%async_computation.2 | async-start | bytes 2097152 | tf_op jit(solution)/shard_map/all_to_all | solution.py:89
  102.5 15.9 %collective-permute-start.8 = (bf16[2,128,1152]{2,1,0:T(8,128)(2,1)S(1)}, bf16[2,128,1152]{2,1,0:T(8,128)(2,1)S(1)}, u32[]{:S(2)}, u32[]{:S(2)}) collective-permute-start(bf16[2,128,1152]{2,1,0:T(8,128)(2,1)S(1)} %get-tuple-element.234), channel_id=1, source_target_pairs={{0,16},{1,17},{16,2},{17,3},{2,18},{3,19},{18,0},{19,1},{4,20},{5,... | collective-permute-start | bytes 1769480 | tf_op jit(solution)/shard_map/ppermute | solution.py:55
  102.6 15.8 %collective-permute-start.9 = (bf16[2,128,1152]{2,1,0:T(8,128)(2,1)S(1)}, bf16[2,128,1152]{2,1,0:T(8,128)(2,1)S(1)}, u32[]{:S(2)}, u32[]{:S(2)}) collective-permute-start(bf16[2,128,1152]{2,1,0:T(8,128)(2,1)S(1)} %get-tuple-element.233), channel_id=1, source_target_pairs={{0,18},{1,19},{16,0},{17,1},{2,16},{3,17},{18,2},{19,3},{4,22},{5,... | collective-permute-start | bytes 1769480 | tf_op jit(solution)/shard_map/ppermute | solution.py:55
  167.9 13.5 %collective-permute-start.13 = (bf16[128,1024]{1,0:T(8,128)(2,1)S(1)}, bf16[128,1024]{1,0:T(8,128)(2,1)S(1)}, u32[]{:S(2)}, u32[]{:S(2)}) collective-permute-start(bf16[128,1024]{1,0:T(8,128)(2,1)S(1)} %get-tuple-element.148), channel_id=1, source_target_pairs={{0,64},{1,65},{16,80},{17,81},{2,66},{3,67},{18,82},{19,83},{4,68}... | collective-permute-start | bytes 786440 | tf_op jit(solution)/shard_map/ppermute | solution.py:55
  169.7 12.6 %collective-permute-start.14 = (bf16[128,1024]{1,0:T(8,128)(2,1)S(1)}, bf16[128,1024]{1,0:T(8,128)(2,1)S(1)}, u32[]{:S(2)}, u32[]{:S(2)}) collective-permute-start(bf16[128,1024]{1,0:T(8,128)(2,1)S(1)} %get-tuple-element.149), channel_id=1, source_target_pairs={{0,96},{1,97},{16,112},{17,113},{2,98},{3,99},{18,114},{19,115},{4... | collective-permute-start | bytes 786440 | tf_op jit(solution)/shard_map/ppermute | solution.py:55
  183.8 14.8 %collective-permute-start.15 = (bf16[128,1024]{1,0:T(8,128)(2,1)}, bf16[128,1024]{1,0:T(8,128)(2,1)S(1)}, u32[]{:S(2)}, u32[]{:S(2)}) collective-permute-start(bf16[128,1024]{1,0:T(8,128)(2,1)} %get-tuple-element.158), channel_id=1, source_target_pairs={{0,96},{1,97},{16,112},{17,113},{2,98},{3,99},{18,114},{19,115},{4... | collective-permute-start | bytes 786440 | tf_op jit(solution)/shard_map/ppermute | solution.py:55
  186.8 11.9 %collective-permute-start.16 = (bf16[128,1024]{1,0:T(8,128)(2,1)}, bf16[128,1024]{1,0:T(8,128)(2,1)S(1)}, u32[]{:S(2)}, u32[]{:S(2)}) collective-permute-start(bf16[128,1024]{1,0:T(8,128)(2,1)} %get-tuple-element.158), channel_id=1, source_target_pairs={{0,64},{1,65},{16,80},{17,81},{2,66},{3,67},{18,82},{19,83},{4,68}... | collective-permute-start | bytes 786440 | tf_op jit(solution)/shard_map/ppermute | solution.py:55
  186.8 15.0 %collective-permute-start.17 = (bf16[128,1024]{1,0:T(8,128)(2,1)}, bf16[128,1024]{1,0:T(8,128)(2,1)S(1)}, u32[]{:S(2)}, u32[]{:S(2)}) collective-permute-start(bf16[128,1024]{1,0:T(8,128)(2,1)} %get-tuple-element.158), channel_id=1, source_target_pairs={{0,32},{1,33},{16,48},{17,49},{2,34},{3,35},{18,50},{19,51},{4,36}... | collective-permute-start | bytes 786440 | tf_op jit(solution)/shard_map/ppermute | solution.py:55
  187.4 51.6 %all-to-all-start.4 = ((bf16[16,108,8,128]{3,2,1,0:T(8,128)(2,1)}), bf16[16,108,8,128]{3,2,1,0:T(8,128)(2,1)}, u32[]{:S(2)}, u32[]{:S(2)}) async-start(bf16[16,108,8,128]{3,2,1,0:T(8,128)(2,1)} %pad_maximum_fusion), calls=%async_computation.4 | async-start | bytes 7077888 | tf_op jit(solution)/shard_map/all_to_all | solution.py:89
  194.2 98.8 %reduce-scatter.2.cloned.1.call-start = ((), (), s32[]{:S(2)}) async-start(), calls=%async_computation.9 | async-start | bytes 2359296 | tf_op jit(solution)/shard_map/reduce_scatter | solution.py:726
  239.0 21.4 %collective-permute-start.20 = (bf16[128,1024]{1,0:T(8,128)(2,1)}, bf16[128,1024]{1,0:T(8,128)(2,1)}, u32[]{:S(2)}, u32[]{:S(2)}) collective-permute-start(bf16[128,1024]{1,0:T(8,128)(2,1)} %get-tuple-element.173), channel_id=1, source_target_pairs={{0,32},{1,33},{16,48},{17,49},{2,34},{3,35},{18,50},{19,51},{4,36}... | collective-permute-start | bytes 786440 | tf_op jit(solution)/shard_map/ppermute | solution.py:55
  240.6 19.8 %collective-permute-start.21 = (bf16[128,1024]{1,0:T(8,128)(2,1)}, bf16[128,1024]{1,0:T(8,128)(2,1)}, u32[]{:S(2)}, u32[]{:S(2)}) collective-permute-start(bf16[128,1024]{1,0:T(8,128)(2,1)} %get-tuple-element.174), channel_id=1, source_target_pairs={{0,64},{1,65},{16,80},{17,81},{2,66},{3,67},{18,82},{19,83},{4,68}... | collective-permute-start | bytes 786440 | tf_op jit(solution)/shard_map/ppermute | solution.py:55
  242.3 18.1 %collective-permute-start.22 = (bf16[128,1024]{1,0:T(8,128)(2,1)}, bf16[128,1024]{1,0:T(8,128)(2,1)}, u32[]{:S(2)}, u32[]{:S(2)}) collective-permute-start(bf16[128,1024]{1,0:T(8,128)(2,1)} %get-tuple-element.175), channel_id=1, source_target_pairs={{0,96},{1,97},{16,112},{17,113},{2,98},{3,99},{18,114},{19,115},{4... | collective-permute-start | bytes 786440 | tf_op jit(solution)/shard_map/ppermute | solution.py:55
  249.4 10.9 %all-to-all-start.5 = ((bf16[4,2,9,8,128]{4,3,2,1,0:T(8,128)(2,1)}), bf16[4,2,9,8,128]{4,3,2,1,0:T(8,128)(2,1)}, u32[]{:S(2)}, u32[]{:S(2)}) async-start(bf16[4,2,9,8,128]{4,3,2,1,0:T(8,128)(2,1)} %bitcast.37), calls=%async_computation.5 | async-start | bytes 294912 | tf_op jit(solution)/shard_map/all_to_all | solution.py:89
  273.9 60.0 %all-to-all-start.6 = ((bf16[16,576,128]{2,1,0:T(8,128)(2,1)}), bf16[16,576,128]{2,1,0:T(8,128)(2,1)S(1)}, u32[]{:S(2)}, u32[]{:S(2)}) async-start(bf16[16,576,128]{2,1,0:T(8,128)(2,1)} %bitcast.139), calls=%async_computation.7 | async-start | bytes 4718592 | tf_op jit(solution)/shard_map/all_to_all | solution.py:89
  288.1 22.5 %collective-permute-start.26 = (bf16[32,8,128]{2,1,0:T(8,128)(2,1)}, bf16[32,8,128]{2,1,0:T(8,128)(2,1)S(1)}, u32[]{:S(2)}, u32[]{:S(2)}) collective-permute-start(bf16[32,8,128]{2,1,0:T(8,128)(2,1)} %get-tuple-element.240), channel_id=1, source_target_pairs={{0,16},{1,17},{16,2},{17,3},{2,18},{3,19},{18,0},{19,1},{4,20},{5,... | collective-permute-start | bytes 196616 | tf_op jit(solution)/shard_map/ppermute | solution.py:55
  289.4 21.1 %collective-permute-start.27 = (bf16[32,8,128]{2,1,0:T(8,128)(2,1)S(1)}, bf16[32,8,128]{2,1,0:T(8,128)(2,1)S(1)}, u32[]{:S(2)}, u32[]{:S(2)}) collective-permute-start(bf16[32,8,128]{2,1,0:T(8,128)(2,1)S(1)} %get-tuple-element.239), channel_id=1, source_target_pairs={{0,2},{1,3},{16,18},{17,19},{2,0},{3,1},{18,16},{19,17},{4,6},{5,7... | collective-permute-start | bytes 196616 | tf_op jit(solution)/shard_map/ppermute | solution.py:55
  291.8 21.5 %collective-permute-start.28 = (bf16[32,8,128]{2,1,0:T(8,128)(2,1)S(1)}, bf16[32,8,128]{2,1,0:T(8,128)(2,1)S(1)}, u32[]{:S(2)}, u32[]{:S(2)}) collective-permute-start(bf16[32,8,128]{2,1,0:T(8,128)(2,1)S(1)} %get-tuple-element.238), channel_id=1, source_target_pairs={{0,18},{1,19},{16,0},{17,1},{2,16},{3,17},{18,2},{19,3},{4,22},{5,... | collective-permute-start | bytes 196616 | tf_op jit(solution)/shard_map/ppermute | solution.py:55
  314.3 10.7 %collective-permute-start.29 = (bf16[2,3,8,128]{3,2,1,0:T(8,128)(2,1)S(1)}, bf16[2,3,8,128]{3,2,1,0:T(8,128)(2,1)S(1)}, u32[]{:S(2)}, u32[]{:S(2)}) collective-permute-start(bf16[2,3,8,128]{3,2,1,0:T(8,128)(2,1)S(1)} %get-tuple-element.253), channel_id=1, source_target_pairs={{0,96},{1,97},{16,112},{17,113},{2,98},{3,99},{18,114},{19,115},{4... | collective-permute-start | bytes 36872 | tf_op jit(solution)/shard_map/ppermute | solution.py:55
  314.4 10.6 %collective-permute-start.30 = (bf16[2,3,8,128]{3,2,1,0:T(8,128)(2,1)S(1)}, bf16[2,3,8,128]{3,2,1,0:T(8,128)(2,1)S(1)}, u32[]{:S(2)}, u32[]{:S(2)}) collective-permute-start(bf16[2,3,8,128]{3,2,1,0:T(8,128)(2,1)S(1)} %get-tuple-element.252), channel_id=1, source_target_pairs={{0,64},{1,65},{16,80},{17,81},{2,66},{3,67},{18,82},{19,83},{4,68}... | collective-permute-start | bytes 36872 | tf_op jit(solution)/shard_map/ppermute | solution.py:55
  314.8 10.3 %collective-permute-start.31 = (bf16[2,3,8,128]{3,2,1,0:T(8,128)(2,1)S(1)}, bf16[2,3,8,128]{3,2,1,0:T(8,128)(2,1)S(1)}, u32[]{:S(2)}, u32[]{:S(2)}) collective-permute-start(bf16[2,3,8,128]{3,2,1,0:T(8,128)(2,1)S(1)} %get-tuple-element.251), channel_id=1, source_target_pairs={{0,32},{1,33},{16,48},{17,49},{2,34},{3,35},{18,50},{19,51},{4,36}... | collective-permute-start | bytes 36872 | tf_op jit(solution)/shard_map/ppermute | solution.py:55
  315.9 11.3 %collective-permute-start.32 = (bf16[128,1024]{1,0:T(8,128)(2,1)S(1)}, bf16[128,1024]{1,0:T(8,128)(2,1)S(1)}, u32[]{:S(2)}, u32[]{:S(2)}) collective-permute-start(bf16[128,1024]{1,0:T(8,128)(2,1)S(1)} %add_convert_fusion.1), channel_id=1, source_target_pairs={{0,0},{1,16},{16,1},{17,17},{2,2},{3,18},{18,3},{19,19},{4,4},{5,2... | collective-permute-start | bytes 786440 | tf_op jit(solution)/shard_map/ppermute | solution.py:55
  323.1 10.8 %collective-permute-start.36 = (bf16[128,1024]{1,0:T(8,128)(2,1)S(1)}, bf16[128,1024]{1,0:T(8,128)(2,1)}, u32[]{:S(2)}, u32[]{:S(2)}) collective-permute-start(bf16[128,1024]{1,0:T(8,128)(2,1)S(1)} %copy-done.56), channel_id=1, source_target_pairs={{0,0},{1,16},{16,1},{17,17},{2,2},{3,18},{18,3},{19,19},{4,4},{5,2... | collective-permute-start | bytes 786440 | tf_op jit(solution)/shard_map/ppermute | solution.py:55
  334.0 22.1 %collective-permute-start.41 = (bf16[16,576,128]{2,1,0:T(8,128)(2,1)S(1)}, bf16[16,576,128]{2,1,0:T(8,128)(2,1)}, u32[]{:S(2)}, u32[]{:S(2)}) collective-permute-start(bf16[16,576,128]{2,1,0:T(8,128)(2,1)S(1)} %all-to-all-done.6.mine_ref), channel_id=1, source_target_pairs={{0,1},{1,0},{16,17},{17,16},{2,3},{3,2},{18,19},{19,18},{4,5},{5,4... | collective-permute-start | bytes 7077896 | tf_op jit(solution)/shard_map/ppermute | solution.py:55
  338.8 10.5 %collective-permute-start.39 = (bf16[4,160,128]{2,1,0:T(8,128)(2,1)S(1)}, bf16[4,160,128]{2,1,0:T(8,128)(2,1)S(1)}, u32[]{:S(2)}, u32[]{:S(2)}) collective-permute-start(bf16[4,160,128]{2,1,0:T(8,128)(2,1)S(1)} %pad_maximum_fusion.7), channel_id=1, source_target_pairs={{0,4},{1,5},{16,20},{17,21},{2,6},{3,7},{18,22},{19,23},{4,8},{5,9... | collective-permute-start | bytes 491528 | tf_op jit(solution)/shard_map/ppermute | solution.py:55
  (77 other events, 408.2 us)
Sparse Core Ops, SparseCore 0:
  93.2 28.6 all-gather.1
  229.0 37.1 reduce-scatter.1

commit v4 on v3

--- a/solution.py
+++ b/solution.py
@@ -166,8 +166,8 @@
     return sums[0], [part.astype(bf16) for part in sums[1:]]
 
 
-def whole(count):
-    return [pl.BlockSpec(memory_space=pltpu.VMEM)] * count
+def whole(shape):
+    return pl.BlockSpec(shape, lambda i: (0,) * len(shape), pipeline_mode=pl.Buffered(1))
 
 
 def spot(values):
@@ -179,8 +179,9 @@
     return pl.pallas_call(
         kernel,
         out_shape=[jax.ShapeDtypeStruct(shape, kind) for shape, kind in outs],
-        in_specs=[pl.BlockSpec(memory_space=pltpu.SMEM)] + whole(len(arrays)),
-        out_specs=whole(len(outs)),
+        grid=(1,),
+        in_specs=[pl.BlockSpec(memory_space=pltpu.SMEM)] + [whole(a.shape) for a in arrays],
+        out_specs=[whole(shape) for shape, _ in outs],
         scratch_shapes=list(scratch),
         compiler_params=pltpu.CompilerParams(vmem_limit_bytes=limit * 2**20),
         cost_estimate=pl.CostEstimate(flops=flops, bytes_accessed=size, transcendentals=0),
@@ -237,7 +238,7 @@
 def pick_columns(query_weight, key_weight, value_weight, gate_weight, up_weight, packed, core):
     outs = [((4, 144, 1280), bf16), ((4, 128, 1152), bf16)]
     arrays = (query_weight, key_weight, value_weight, gate_weight, up_weight, packed)
-    return call(columns_kernel, spot([core]), arrays, outs, limit=16)
+    return call(columns_kernel, spot([core]), arrays, outs, limit=58)
 
 
 def pack_kernel(tokens_ref, first_ref, second_ref, small_ref, out_ref):
@@ -369,7 +370,7 @@
     arrays = (half, far, across, gain, *tables)
     scratch = [pltpu.VMEM((128, 1024), bf16)]
     scalars = spot([where[4], where[3]])
-    return call(attend_kernel, scalars, arrays, outs, scratch, 30, 2 * 1024**3)
+    return call(attend_kernel, scalars, arrays, outs, scratch, 58, 2 * 1024**3)
 
 
 def attend_back_kernel(
@@ -467,7 +468,7 @@
         pltpu.VMEM((1024, 256), f32),
         pltpu.VMEM((128, 1024), bf16),
     ]
-    return call(attend_back_kernel, spot([where[0]]), arrays, outs, scratch, 36, 4 * 1024**3)
+    return call(attend_back_kernel, spot([where[0]]), arrays, outs, scratch, 58, 4 * 1024**3)
 
 
 def feed_kernel(
@@ -475,6 +476,7 @@
     half_ref,
     far_ref,
     upstream_ref,
+    upstream_far_ref,
     came_ref,
     lower_ref,
     upper_ref,
@@ -484,6 +486,7 @@
     hidden_ref,
     pre_grad_ref,
     normed_ref,
+    turned_ref,
     weight_ref,
 ):
     z_low, core, x = spot_ref[0], spot_ref[1], spot_ref[2]
@@ -494,16 +497,13 @@
     normed_ref[:512] = half_ref[...]
     normed_ref[512:] = far_ref[...]
 
-    def rows_of(part, slot_core):
+    def work(start, part, slot_core, from_ref):
+        rows = pl.ds(pl.multiple_of(start, 256), 256)
+        upstream = from_ref[pl.ds(pl.multiple_of(part * 256, 256), 256), :]
         slots = [
             pl.ds(pl.multiple_of((part * 4 + step * 2 + slot_core) * 128, 128), 128)
             for step in range(2)
         ]
-        return slots, jnp.concatenate([upstream_ref[slot, :] for slot in slots], axis=0)
-
-    def work(start, part, slot_core):
-        rows = pl.ds(pl.multiple_of(start, 256), 256)
-        slots, upstream = rows_of(part, slot_core)
         pre = matmul(normed_ref[rows, :], weight_ref[...])
         gate, up = pre[:, :576], pre[:, 576:]
         hidden_grad = matmul_nt(upstream, down_ref[...]).astype(bf16).astype(f32)
@@ -512,6 +512,7 @@
         hidden = (silu * up).astype(bf16)
         for step, slot in enumerate(slots):
             hidden_ref[slot, :] = hidden[step * 128 : step * 128 + 128]
+            turned_ref[slot, :] = upstream[step * 128 : step * 128 + 128]
         gate_grad = hidden_grad * up * sigmoid * (1.0 + gate * (1.0 - sigmoid))
         pre_grad = jnp.concatenate([gate_grad, hidden_grad * silu], axis=1).astype(bf16)
         pre_grad_ref[rows, :] = pre_grad
@@ -523,29 +524,30 @@
             ref[pl.ds(to, 128), :] = partial[step * 128 : step * 128 + 128].astype(bf16)
 
     def other_half(part, carry):
-        keep(other_ref, part, work(part * 256 + 512, part, 1 - core))
+        keep(other_ref, part, work(part * 256 + 512, part, 1 - core, upstream_far_ref))
         return carry
 
     def own_half(part, carry):
-        keep(own_ref, part, work(part * 256, part, core))
+        keep(own_ref, part, work(part * 256, part, core, upstream_ref))
         return carry
 
     lax.fori_loop(0, 2, other_half, 0)
     lax.fori_loop(0, 2, own_half, 0)
 
 
-def feed(half, far, upstream, weights, down_slot, where):
-    arrays = (half, far, upstream, *weights, down_slot)
+def feed(half, far, upstream, upstream_far, weights, down_slot, where):
+    arrays = (half, far, upstream, upstream_far, *weights, down_slot)
     outs = [
         ((512, 1024), bf16),
         ((512, 1024), bf16),
         ((1024, 576), bf16),
         ((1024, 1152), bf16),
         ((1024, 1024), bf16),
+        ((1024, 1024), bf16),
     ]
     scratch = [pltpu.VMEM((1024, 1152), bf16)]
     scalars = spot([where[4], where[3], where[0]])
-    return call(feed_kernel, scalars, arrays, outs, scratch, 34, 6 * 1024**3)
+    return call(feed_kernel, scalars, arrays, outs, scratch, 58, 6 * 1024**3)
 
 
 def feed_grads_kernel(spot_ref, mine_ref, other_ref, gate_ref, up_ref, down_ref):
@@ -655,21 +657,19 @@
     packed_out, for_feed = pick_columns(
         query_weight, key_weight, value_weight, gate_weight, up_weight, packed, core
     )
-    packed_out, for_feed, facts, rows_mine, cotangent = join(
-        packed_out, for_feed, facts, (out_weight, down_weight), cotangent
+    packed_out, for_feed, facts, out_mine, cotangent = join(
+        packed_out, for_feed, facts, out_weight, cotangent
     )
     half = exchange(packed_out, x_rings)
     tables = place_tables(facts, core)
     upstream_own = send(cotangent[0], regroup)
-    rows_got = [send(rows_mine[0], z_up_home), send(rows_mine[1], z_down_home)]
-    out_slot, down_slot = (
-        jnp.where(core == z_low, mine, got) for mine, got in zip(rows_mine, rows_got)
-    )
-    half, for_feed, upstream_own, out_slot, down_slot, tables = join(
-        half, for_feed, upstream_own, out_slot, down_slot, tables
-    )
-
-    upstream = lax.all_gather(upstream_own, AXES, axis=0, axis_index_groups=x_groups, tiled=True)
+    out_slot = jnp.where(core == z_low, out_mine, send(out_mine, z_up_home))
+    half, for_feed, upstream_own, out_slot, tables, down_mine = join(
+        half, for_feed, upstream_own, out_slot, tables, down_weight
+    )
+
+    upstream = lax.all_gather(upstream_own, AXES, axis=0, axis_index_groups=x_rings, tiled=True)
+    down_got = send(down_mine, z_down_home)
     far = send(half, other_core)
     across = send(half[:, :128, 1024:], z_up)
     feed_came = exchange(for_feed, x_rings)
@@ -685,19 +685,22 @@
     )
     gain_first, gain_second = gains[0], gains[8]
     other_half = matmul(mixed[512:], out_slot).astype(bf16)
-    other_half, mixed, feed_came = join(other_half, mixed, feed_came)
+    other_half, mixed, feed_came, down_got = join(other_half, mixed, feed_came, down_got)
+    down_slot = jnp.where(core == z_low, down_mine, down_got)
     got = send(other_half, other_core)
     own_half = matmul(mixed[:512], out_slot)
     lower, upper = send(feed_came[:2], z_up), send(feed_came[2:], z_down)
     parts = scatter_sums(own_half, got)
-    parts, lower, upper = join(parts, lower, upper)
+    parts, lower, upper, down_slot = join(parts, lower, upper, down_slot)
 
     middle = inputs + add_up(parts)
     second_scale = rms_scale(middle)
     half = gather_half((middle * second_scale * gain_second).astype(bf16)).reshape(512, 1024)
+    half, upstream = join(half, upstream)
     far = send(half, other_core)
-    other_half, own_half, hidden, pre_grad, normed_all = feed(
-        half, far, upstream, (feed_came, lower, upper), down_slot, where
+    upstream_far = send(upstream, other_core)
+    other_half, own_half, hidden, pre_grad, normed_all, upstream = feed(
+        half, far, upstream, upstream_far, (feed_came, lower, upper), down_slot, where
     )
     first, rest = scatter_parts(own_half, send(other_half, other_core))
     first, rest, pre_grad, hidden, normed_all = join(first, rest, pre_grad, hidden, normed_all)
@@ -736,11 +739,9 @@
         where,
     )
     first, rest = scatter_parts(own_half, send(other_half, other_core))
-    first, rest, pre_grad, feed_parts = join(first, rest, pre_grad, feed_parts)
+    first, rest, pre_grad = join(first, rest, pre_grad)
 
     parts = send_x(*rest)
-    feed_rows = add_up(feed_parts).astype(bf16)
-    feed_got = exchange_rows(feed_rows[:72].reshape(8, 9, 8, 128))
     attention_weight_grad = matmul_tn(first_normed, pre_grad)
     first_gain_grad = first_terms[0] / gain_first
     small = jnp.stack([gain_terms[0, :64] + gain_terms[0, 64:128], gain_terms[0, 128:192]], 1)
@@ -750,16 +751,15 @@
     by_row = rows_for_planes(cat([attention_weight_grad, extra], 1)).reshape(4, 4, 24, 8, 128)
     by_block = block_for_planes(out_weight_grad).reshape(4, 4, 8, 8, 128)
     attention_parts = cat([by_row, by_block], 2)
-    first, parts, attention_parts, feed_got, feed_rows = join(
-        first, parts, attention_parts, feed_got, feed_rows
-    )
     pieces = [pick(attention_parts, (y + step) % 4, 0) for step in range(4)]
     ring = send_ring(pieces, y_up, y_down, y_far)
+    feed_rows = add_up(feed_parts).astype(bf16)
+    feed_got = exchange_rows(feed_rows[:72].reshape(8, 9, 8, 128))
+    first, parts, ring, feed_got, feed_rows = join(first, parts, ring, feed_got, feed_rows)
+
     first_grad = first + add_up(jnp.stack(parts))
     input_norm_grad, _ = norm_back(inputs, rms_scale(inputs), gain_first, first_grad)
     input_grad = (middle_grad + input_norm_grad).astype(bf16)
-    ring, feed_got, feed_rows, input_grad = join(ring, feed_got, feed_rows, input_grad)
-
     rows = pieces[0].astype(f32) + add_up(jnp.stack(ring))
     pieces = [pick(rows, (z + step) % 4, 0) for step in range(4)]
     ring = send_ring(pieces, z_up, z_down, z_far)

time: 375 us -> 355 us (0.947)
  local copies, waits for them, and re-layouts: 46.8 us -> 22.1 us
  blocking collectives: 17.4 us -> 0 us
  Pallas kernels: 45.4 us -> 59.2 us
  starting transfers between devices: 98.3 us -> 106 us
    unnamed x124 -> x68, local copies, waits for them, and re-layouts: 34.2 us -> 4.6 us
    all_to_all x1 -> x0, blocking collectives: 17.4 us -> none  [exchange(): return lax.all_to_all(values, AXES, 0, 0, axis_index_groups=groups)]
    pallas_call x6, Pallas kernels: 43.7 us -> 57.5 us  [call(): pl.pallas_call(kernel, out_shape=[jax.ShapeDtypeStruct(shape, kind) for s...]
    ppermute x42 -> x43, starting transfers between devices: 64.9 us -> 72.6 us  [send(): return lax.ppermute(values, AXES, moves)]
    all_gather x1, waiting for transfers between devices: 0.01 us -> 6.33 us  [on_device(): lax.all_gather(upstream_own, AXES, axis=0, axis_index_groups=x_rings, til...]
    all_to_all x6 -> x7, waiting for transfers between devices: 19 us -> 15.7 us  [exchange(): return lax.all_to_all(values, AXES, 0, 0, axis_index_groups=groups)]
    ppermute x42 -> x43, waiting for transfers between devices: 80.5 us -> 77.8 us  [send(): return lax.ppermute(values, AXES, moves)]
    all_to_all x6 -> x7, starting transfers between devices: 32.9 us -> 33.2 us  [exchange(): return lax.all_to_all(values, AXES, 0, 0, axis_index_groups=groups)]
  transfers between devices with their start and end apart: 50 -> 52, of which waited for: 24 -> 25; matrix products, arithmetic and copies ran while one was open for 15% -> 17% of each run, Pallas kernels for 8% -> 10%
where the time goes in v4:
time: 355 us; the launch traced here: 350 us
  starting transfers between devices  106 us (30%)
  waiting for transfers between devices  99.9 us (28%)
  Pallas kernels  59.2 us (17%)
  other arithmetic  34.4 us (10%)
  local copies, waits for them, and re-layouts  22.1 us (6%)
  between operations  15.1 us (4%)
  matrix products  13.5 us (4%)
    ppermute x43, waiting for transfers between devices, send(): return lax.ppermute(values, AXES, moves)  77.8 us
    ppermute x43, starting transfers between devices, send(): return lax.ppermute(values, AXES, moves)  72.6 us
    pallas_call x6, Pallas kernels, call(): pl.pallas_call(kernel, out_shape=[jax.ShapeDtypeStruct(shape, kind) for s...  57.5 us
    all_to_all x7, starting transfers between devices, exchange(): return lax.all_to_all(values, AXES, 0, 0, axis_index_groups=groups)  33.2 us
    all_to_all x7, waiting for transfers between devices, exchange(): return lax.all_to_all(values, AXES, 0, 0, axis_index_groups=groups)  15.7 us
  transfers between devices with their start and end apart: 52, of which 25 were waited for; matrix products, arithmetic and copies ran while one was open for 17% of the time, Pallas kernels for 10%

profile of v4, /device:TPU:1, one launch (start us, length us, event | category | flops | bytes accessed | tf_op | source)
XLA Modules:
  0.0 350.0 jit_solution(1112532014519708189)
XLA Ops:
  12.9 3.5 %collective-permute-start = (bf16[144,1024]{1,0:T(8,128)(2,1)}, bf16[144,1024]{1,0:T(8,128)(2,1)S(1)}, u32[]{:S(2)}, u32[]{:S(2)}) collective-permute-start(bf16[144,1024]{1,0:T(8,128)(2,1)} %shard_map.246), channel_id=1, source_target_pairs={{0,0},{1,16},{16,1},{17,17},{2,2},{3,18},{18,3},{19,19},{4,4},{5,2... | collective-permute-start | bytes 884744 | tf_op jit(solution)/shard_map/ppermute | solution.py:55
  17.8 3.3 collective-permute-done.packed_ref
  21.9 4.5 %shard_map.247 = (bf16[4,144,1280]{2,1,0:T(8,128)(2,1)}, bf16[4,128,1152]{2,1,0:T(8,128)(2,1)}) custom-call(s32[1]{0:T(128)} %bitcast.1.spot_ref, bf16[128,1024]{1,0:T(8,128)(2,1)} %q_ref.1, bf16[128,512]{1,0:T(8,128)(2,1)} %k_ref.1, bf16[128,512]{1,0:T(8,128)(2,1)} %v_ref.1, bf16[128,4608]{1,0:T(8,128)(2,1)} %gate_ref.1, bf16[128,4608]{1,0:T(8,128)(2,1)} %up_ref.1, ...), custom_call_target="tpu_custom_call" | custom-call | bytes 3178496 | tf_op jit(solution)/shard_map/pallas_call | solution.py:179
  26.4 4.2 %all-to-all-start = ((bf16[4,144,1280]{2,1,0:T(8,128)(2,1)}), bf16[4,144,1280]{2,1,0:T(8,128)(2,1)S(1)}, u32[]{:S(2)}, u32[]{:S(2)}) async-start(bf16[4,144,1280]{2,1,0:T(8,128)(2,1)} %get-tuple-element.114), calls=%async_computation | async-start | bytes 2949120 | tf_op jit(solution)/shard_map/all_to_all | solution.py:89
  34.4 3.7 %collective-permute-start.2 = (bf16[128,1024]{1,0:T(8,128)(2,1)S(1)}, bf16[128,1024]{1,0:T(8,128)(2,1)S(1)}, u32[]{:S(2)}, u32[]{:S(2)}) collective-permute-start(bf16[128,1024]{1,0:T(8,128)(2,1)S(1)} %bitcast.190), channel_id=1, source_target_pairs={{0,0},{1,16},{16,1},{17,17},{2,2},{3,18},{18,3},{19,19},{4,4},{5,2... | collective-permute-start | bytes 786440 | tf_op jit(solution)/shard_map/ppermute | solution.py:55
  38.1 3.1 fusion.7
  42.2 3.9 %all-to-all-done.half_ref = bf16[4,144,1280]{2,1,0:T(8,128)(2,1)S(1)} async-done(((bf16[4,144,1280]{2,1,0:T(8,128)(2,1)}), bf16[4,144,1280]{2,1,0:T(8,128)(2,1)S(1)}, u32[]{:S(2)}, u32[]{:S(2)}) %all-to-all-start) | async-done | bytes 1474592 | tf_op jit(solution)/shard_map/all_to_all | solution.py:89
  50.6 3.7 %all-to-all-start.1 = ((bf16[4,128,1152]{2,1,0:T(8,128)(2,1)}), bf16[4,128,1152]{2,1,0:T(8,128)(2,1)S(1)}, u32[]{:S(2)}, u32[]{:S(2)}) async-start(bf16[4,128,1152]{2,1,0:T(8,128)(2,1)} %get-tuple-element.131), calls=%async_computation.1 | async-start | bytes 2359296 | tf_op jit(solution)/shard_map/all_to_all | solution.py:89
  58.3 13.1 %shard_map.248 = (bf16[1024,256]{1,0:T(8,128)(2,1)}, bf16[1024,1024]{1,0:T(8,128)(2,1)}, bf16[1024,256]{1,0:T(8,128)(2,1)}, f32[1024,256]{1,0:T(8,128)}, f32[102...) custom-call(s32[2]{0:T(128)} %pad_add_fusion.1.spot_ref, ...), custom_call_target="tpu_custom_call" | custom-call | flops 2147483648 | bytes 4273152 | tf_op jit(solution)/shard_map/pallas_call | solution.py:179
  79.2 4.5 %all-to-all-start.2 = ((bf16[4,128,1024]{2,1,0:T(8,128)(2,1)}), bf16[4,128,1024]{2,1,0:T(8,128)(2,1)S(1)}, u32[]{:S(2)}, u32[]{:S(2)}) async-start(bf16[4,128,1024]{2,1,0:T(8,128)(2,1)} %bitcast.18), calls=%async_computation.2 | async-start | bytes 2097152 | tf_op jit(solution)/shard_map/all_to_all | solution.py:89
  89.9 9.6 %collective-permute-done.8.lower_ref = bf16[2,128,1152]{2,1,0:T(8,128)(2,1)} collective-permute-done((bf16[2,128,1152]{2,1,0:T(8,128)(2,1)S(1)}, bf16[2,128,1152]{2,1,0:T(8,128)(2,1)}, u32[]{:S(2)}, u32[]{:S(2)}) %collective-permute-start.8) | collective-permute-done | bytes 589856 | tf_op jit(solution)/shard_map/ppermute | solution.py:55
  101.6 3.9 %all-to-all-start.3 = ((bf16[4,128,1024]{2,1,0:T(8,128)(2,1)}), bf16[4,128,1024]{2,1,0:T(8,128)(2,1)S(1)}, u32[]{:S(2)}, u32[]{:S(2)}) async-start(bf16[4,128,1024]{2,1,0:T(8,128)(2,1)} %broadcast_in_dim.86), calls=%async_computation.3 | async-start | bytes 2097152 | tf_op jit(solution)/shard_map/all_to_all | solution.py:89
  105.5 6.3 %all-gather.2.cloned.1.call-done.upstream_ref = bf16[512,1024]{1,0:T(8,128)(2,1)} async-done(((bf16[128,1024]{1,0:T(8,128)(2,1)}), bf16[512,1024]{1,0:T(8,128)(2,1)}) %all-gather.2.cloned.1.call-update) | async-done | bytes 1048592 | tf_op jit(solution)/shard_map/all_gather | solution.py:671
  111.8 8.2 %all-to-all-done.3 = bf16[4,128,1024]{2,1,0:T(8,128)(2,1)S(1)} async-done(((bf16[4,128,1024]{2,1,0:T(8,128)(2,1)}), bf16[4,128,1024]{2,1,0:T(8,128)(2,1)S(1)}, u32[]{:S(2)}, u32[]{:S(2)}) %all-to-all-start.3) | async-done | bytes 1048608 | tf_op jit(solution)/shard_map/all_to_all | solution.py:89
  127.0 15.1 %shard_map.249 = (bf16[512,1024]{1,0:T(8,128)(2,1)}, bf16[512,1024]{1,0:T(8,128)(2,1)}, bf16[1024,576]{1,0:T(8,128)(2,1)}, bf16[1024,1152]{1,0:T(8,128)(2,1)}, b...) custom-call(s32[3]{0:T(128)} %pad_add_fusion.2.spot_ref, bf16[512,1024]{1,0:T(8,128)(2,1)} %bitcast.145, ...), custom_call_target="tpu_custom_call" | custom-call | flops 6442450944 | bytes 7733248 | tf_op jit(solution)/shard_map/pallas_call | solution.py:179
  150.5 4.6 %convolution_convert_fusion = bf16[1024,1152]{1,0:T(8,128)(2,1)S(1)} fusion(bf16[1024,1024]{1,0:T(8,128)(2,1)} %get-tuple-element.153, bf16[1024,1152]{1,0:T(8,128)(2,1)S(1)} %copy-done.30), kind=kOutput, calls=%fused_computation | convolution fusion | flops 2417098752 | bytes 6815744 | tf_op jit(solution)/shard_map/dot_general | solution.py:207
  162.9 3.3 collective-permute-start.16
  167.0 3.1 convolution_convert_fusion.1
  170.1 6.8 %collective-permute-done.16 = bf16[128,1024]{1,0:T(8,128)(2,1)S(1)} collective-permute-done((bf16[128,1024]{1,0:T(8,128)(2,1)S(1)}, bf16[128,1024]{1,0:T(8,128)(2,1)S(1)}, u32[]{:S(2)}, u32[]{:S(2)}) %collective-permute-start.16) | collective-permute-done | bytes 262176 | tf_op jit(solution)/shard_map/ppermute | solution.py:55
  176.9 4.7 %collective-permute-done.18 = bf16[128,1024]{1,0:T(8,128)(2,1)S(1)} collective-permute-done((bf16[128,1024]{1,0:T(8,128)(2,1)S(1)}, bf16[128,1024]{1,0:T(8,128)(2,1)S(1)}, u32[]{:S(2)}, u32[]{:S(2)}) %collective-permute-start.18) | collective-permute-done | bytes 262176 | tf_op jit(solution)/shard_map/ppermute | solution.py:55
  185.0 6.5 %all-to-all-start.4 = ((bf16[16,108,8,128]{3,2,1,0:T(8,128)(2,1)}), bf16[16,108,8,128]{3,2,1,0:T(8,128)(2,1)S(1)}, u32[]{:S(2)}, u32[]{:S(2)}) async-start(bf16[16,108,8,128]{3,2,1,0:T(8,128)(2,1)} %pad_maximum_fusion), calls=%async_computation.4 | async-start | bytes 7077888 | tf_op jit(solution)/shard_map/all_to_all | solution.py:89
  191.5 16.8 %shard_map.250 = (bf16[512,1024]{1,0:T(8,128)(2,1)}, bf16[512,1024]{1,0:T(8,128)(2,1)}, bf16[1024,256]{1,0:T(8,128)(2,1)}, f32[128,1024]{1,0:T(8,128)}, f32[8,256]{1,0:T(8,128)}, /*index=5*/f32[8,1024]{1,0:T(8,128)}) custom-call(s32[1]{0:T(128)} %bitcast.17.spot_ref, bf16[512,1024]{1,0:T(8,128)(2,1)} %constant_dynamic-update-slice_fusion.near_ref, ...), custom_call_target="tpu_custom_call" | custom-call | flops 4294967296 | bytes 8958976 | tf_op jit(solution)/shard_map/pallas_call | solution.py:179
  230.1 12.9 %collective-permute-done.24 = bf16[4,32,8,128]{3,2,1,0:T(8,128)(2,1)} collective-permute-done((bf16[4,32,8,128]{3,2,1,0:T(8,128)(2,1)S(1)}, bf16[4,32,8,128]{3,2,1,0:T(8,128)(2,1)}, u32[]{:S(2)}, u32[]{:S(2)}) %collective-permute-start.24) | collective-permute-done | bytes 262176 | tf_op jit(solution)/shard_map/ppermute | solution.py:55
  246.0 3.3 all-to-all-start.5
  250.6 3.7 %all-to-all-done.5 = bf16[4,2,9,8,128]{4,3,2,1,0:T(8,128)(2,1)S(1)} async-done(((bf16[4,2,9,8,128]{4,3,2,1,0:T(8,128)(2,1)}), bf16[4,2,9,8,128]{4,3,2,1,0:T(8,128)(2,1)S(1)}, u32[]{:S(2)}, u32[]{:S(2)}) %all-to-all-start.5) | async-done | bytes 147488 | tf_op jit(solution)/shard_map/all_to_all | solution.py:89
  257.1 7.1 %all-to-all-start.6 = ((bf16[16,576,128]{2,1,0:T(8,128)(2,1)}), bf16[16,576,128]{2,1,0:T(8,128)(2,1)S(1)}, u32[]{:S(2)}, u32[]{:S(2)}) async-start(bf16[16,576,128]{2,1,0:T(8,128)(2,1)} %bitcast.134), calls=%async_computation.7 | async-start | bytes 4718592 | tf_op jit(solution)/shard_map/all_to_all | solution.py:89
  274.2 9.3 %collective-permute-done.27 = bf16[32,8,128]{2,1,0:T(8,128)(2,1)S(1)} collective-permute-done((bf16[32,8,128]{2,1,0:T(8,128)(2,1)S(1)}, bf16[32,8,128]{2,1,0:T(8,128)(2,1)S(1)}, u32[]{:S(2)}, u32[]{:S(2)}) %collective-permute-start.27) | collective-permute-done | bytes 65568 | tf_op jit(solution)/shard_map/ppermute | solution.py:55
  286.6 14.6 %collective-permute-start.33 = (bf16[128,1024]{1,0:T(8,128)(2,1)S(1)}, bf16[128,1024]{1,0:T(8,128)(2,1)S(1)}, u32[]{:S(2)}, u32[]{:S(2)}) collective-permute-start(bf16[128,1024]{1,0:T(8,128)(2,1)S(1)} %add_convert_fusion.1), channel_id=1, source_target_pairs={{0,0},{1,16},{16,1},{17,17},{2,2},{3,18},{18,3},{19,19},{4,4},{5,2... | collective-permute-start | bytes 786440 | tf_op jit(solution)/shard_map/ppermute | solution.py:55
  305.4 4.7 %collective-permute-start.35 = (bf16[160,128]{1,0:T(8,128)(2,1)S(1)}, bf16[160,128]{1,0:T(8,128)(2,1)S(1)}, u32[]{:S(2)}, u32[]{:S(2)}) collective-permute-start(bf16[160,128]{1,0:T(8,128)(2,1)S(1)} %get-tuple-element.253), channel_id=1, source_target_pairs={{0,2},{1,3},{16,18},{17,19},{2,0},{3,1},{18,16},{19,17},{4,6},{5,7... | collective-permute-start | bytes 122888 | tf_op jit(solution)/shard_map/ppermute | solution.py:55
  319.9 6.2 %collective-permute-done.38 = bf16[4,160,128]{2,1,0:T(8,128)(2,1)S(1)} collective-permute-done((bf16[4,160,128]{2,1,0:T(8,128)(2,1)S(1)}, bf16[4,160,128]{2,1,0:T(8,128)(2,1)S(1)}, u32[]{:S(2)}, u32[]{:S(2)}) %collective-permute-start.38) | collective-permute-done | bytes 163872 | tf_op jit(solution)/shard_map/ppermute | solution.py:55
  326.2 4.2 %collective-permute-done.40 = bf16[4,160,128]{2,1,0:T(8,128)(2,1)S(1)} collective-permute-done((bf16[4,160,128]{2,1,0:T(8,128)(2,1)S(1)}, bf16[4,160,128]{2,1,0:T(8,128)(2,1)S(1)}, u32[]{:S(2)}, u32[]{:S(2)}) %collective-permute-start.40) | collective-permute-done | bytes 163872 | tf_op jit(solution)/shard_map/ppermute | solution.py:55
  337.0 5.2 %shard_map.252 = (f32[128,4608]{1,0:T(8,128)}, f32[128,4608]{1,0:T(8,128)}, f32[576,1024]{1,0:T(8,128)}) custom-call(s32[2]{0:T(128)S(1)} %pad_add_fusion.3.spot_ref, bf16[16,576,128]{2,1,0:T(8,128)(2,1)S(1)} %all-to-all-done.6.mine_ref, bf16[16,576,128]{2,1,0:T(8,128)(2,1)} %collective-permute-done.42.other_ref), custom_call_target="tpu_custom_call" | custom-call | bytes 4718592 | tf_op jit(solution)/shard_map/pallas_call | solution.py:179
  (242 shorter events, 127.4 us)
Async XLA Ops:
  26.4 19.6 %all-to-all-start = ((bf16[4,144,1280]{2,1,0:T(8,128)(2,1)}), bf16[4,144,1280]{2,1,0:T(8,128)(2,1)S(1)}, u32[]{:S(2)}, u32[]{:S(2)}) async-start(bf16[4,144,1280]{2,1,0:T(8,128)(2,1)} %get-tuple-element.114), calls=%async_computation | async-start | bytes 2949120 | tf_op jit(solution)/shard_map/all_to_all | solution.py:89
  46.0 10.6 %collective-permute-start.4 = (bf16[4,144,1280]{2,1,0:T(8,128)(2,1)S(1)}, bf16[4,144,1280]{2,1,0:T(8,128)(2,1)}, u32[]{:S(2)}, u32[]{:S(2)}) collective-permute-start(bf16[4,144,1280]{2,1,0:T(8,128)(2,1)S(1)} %all-to-all-done.half_ref), channel_id=1, source_target_pairs={{0,1},{1,0},{16,17},{17,16},{2,3},{3,2},{18,19},{19,18},{4,5},{5,4... | collective-permute-start | bytes 4423688 | tf_op jit(solution)/shard_map/ppermute | solution.py:55
  47.7 25.0 %collective-permute-start.6 = (bf16[576,1024]{1,0:T(8,128)(2,1)}, bf16[576,1024]{1,0:T(8,128)(2,1)}, u32[]{:S(2)}, u32[]{:S(2)}) collective-permute-start(bf16[576,1024]{1,0:T(8,128)(2,1)} %param.28), channel_id=1, source_target_pairs={{0,18},{17,1},{2,16},{19,3},{4,22},{21,5},{6,20},{23,7},{8,26},{25... | collective-permute-start | bytes 3538952 | tf_op jit(solution)/shard_map/ppermute | solution.py:55
  50.6 22.1 %all-to-all-start.1 = ((bf16[4,128,1152]{2,1,0:T(8,128)(2,1)}), bf16[4,128,1152]{2,1,0:T(8,128)(2,1)S(1)}, u32[]{:S(2)}, u32[]{:S(2)}) async-start(bf16[4,128,1152]{2,1,0:T(8,128)(2,1)} %get-tuple-element.131), calls=%async_computation.1 | async-start | bytes 2359296 | tf_op jit(solution)/shard_map/all_to_all | solution.py:89
  79.2 20.2 %all-to-all-start.2 = ((bf16[4,128,1024]{2,1,0:T(8,128)(2,1)}), bf16[4,128,1024]{2,1,0:T(8,128)(2,1)S(1)}, u32[]{:S(2)}, u32[]{:S(2)}) async-start(bf16[4,128,1024]{2,1,0:T(8,128)(2,1)} %bitcast.18), calls=%async_computation.2 | async-start | bytes 2097152 | tf_op jit(solution)/shard_map/all_to_all | solution.py:89
  83.7 28.1 %all-gather.2.cloned.1.call-start = ((), (), s32[]{:S(2)}) async-start(), calls=%async_computation.8 | async-start | bytes 1310720 | tf_op jit(solution)/shard_map/all_gather | solution.py:671
  83.8 15.6 %collective-permute-start.8 = (bf16[2,128,1152]{2,1,0:T(8,128)(2,1)S(1)}, bf16[2,128,1152]{2,1,0:T(8,128)(2,1)}, u32[]{:S(2)}, u32[]{:S(2)}) collective-permute-start(bf16[2,128,1152]{2,1,0:T(8,128)(2,1)S(1)} %get-tuple-element.232), channel_id=1, source_target_pairs={{0,16},{1,17},{16,2},{17,3},{2,18},{3,19},{18,0},{19,1},{4,20},{5,... | collective-permute-start | bytes 1769480 | tf_op jit(solution)/shard_map/ppermute | solution.py:55
  83.9 15.5 %collective-permute-start.9 = (bf16[2,128,1152]{2,1,0:T(8,128)(2,1)S(1)}, bf16[2,128,1152]{2,1,0:T(8,128)(2,1)}, u32[]{:S(2)}, u32[]{:S(2)}) collective-permute-start(bf16[2,128,1152]{2,1,0:T(8,128)(2,1)S(1)} %get-tuple-element.231), channel_id=1, source_target_pairs={{0,18},{1,19},{16,0},{17,1},{2,16},{3,17},{18,2},{19,3},{4,22},{5,... | collective-permute-start | bytes 1769480 | tf_op jit(solution)/shard_map/ppermute | solution.py:55
  101.6 18.4 %all-to-all-start.3 = ((bf16[4,128,1024]{2,1,0:T(8,128)(2,1)}), bf16[4,128,1024]{2,1,0:T(8,128)(2,1)S(1)}, u32[]{:S(2)}, u32[]{:S(2)}) async-start(bf16[4,128,1024]{2,1,0:T(8,128)(2,1)} %broadcast_in_dim.86), calls=%async_computation.3 | async-start | bytes 2097152 | tf_op jit(solution)/shard_map/all_to_all | solution.py:89
  146.7 12.5 %collective-permute-start.13 = (bf16[128,1024]{1,0:T(8,128)(2,1)S(1)}, bf16[128,1024]{1,0:T(8,128)(2,1)S(1)}, u32[]{:S(2)}, u32[]{:S(2)}) collective-permute-start(bf16[128,1024]{1,0:T(8,128)(2,1)S(1)} %get-tuple-element.150), channel_id=1, source_target_pairs={{0,32},{1,33},{16,48},{17,49},{2,34},{3,35},{18,50},{19,51},{4,36}... | collective-permute-start | bytes 786440 | tf_op jit(solution)/shard_map/ppermute | solution.py:55
  148.0 13.5 %collective-permute-start.14 = (bf16[128,1024]{1,0:T(8,128)(2,1)S(1)}, bf16[128,1024]{1,0:T(8,128)(2,1)S(1)}, u32[]{:S(2)}, u32[]{:S(2)}) collective-permute-start(bf16[128,1024]{1,0:T(8,128)(2,1)S(1)} %get-tuple-element.151), channel_id=1, source_target_pairs={{0,64},{1,65},{16,80},{17,81},{2,66},{3,67},{18,82},{19,83},{4,68}... | collective-permute-start | bytes 786440 | tf_op jit(solution)/shard_map/ppermute | solution.py:55
  149.8 11.7 %collective-permute-start.15 = (bf16[128,1024]{1,0:T(8,128)(2,1)S(1)}, bf16[128,1024]{1,0:T(8,128)(2,1)S(1)}, u32[]{:S(2)}, u32[]{:S(2)}) collective-permute-start(bf16[128,1024]{1,0:T(8,128)(2,1)S(1)} %get-tuple-element.152), channel_id=1, source_target_pairs={{0,96},{1,97},{16,112},{17,113},{2,98},{3,99},{18,114},{19,115},{4... | collective-permute-start | bytes 786440 | tf_op jit(solution)/shard_map/ppermute | solution.py:55
  162.9 14.0 %collective-permute-start.16 = (bf16[128,1024]{1,0:T(8,128)(2,1)S(1)}, bf16[128,1024]{1,0:T(8,128)(2,1)S(1)}, u32[]{:S(2)}, u32[]{:S(2)}) collective-permute-start(bf16[128,1024]{1,0:T(8,128)(2,1)S(1)} %get-tuple-element.162), channel_id=1, source_target_pairs={{0,96},{1,97},{16,112},{17,113},{2,98},{3,99},{18,114},{19,115},{4... | collective-permute-start | bytes 786440 | tf_op jit(solution)/shard_map/ppermute | solution.py:55
  166.2 10.7 %collective-permute-start.17 = (bf16[128,1024]{1,0:T(8,128)(2,1)S(1)}, bf16[128,1024]{1,0:T(8,128)(2,1)S(1)}, u32[]{:S(2)}, u32[]{:S(2)}) collective-permute-start(bf16[128,1024]{1,0:T(8,128)(2,1)S(1)} %get-tuple-element.162), channel_id=1, source_target_pairs={{0,64},{1,65},{16,80},{17,81},{2,66},{3,67},{18,82},{19,83},{4,68}... | collective-permute-start | bytes 786440 | tf_op jit(solution)/shard_map/ppermute | solution.py:55
  166.7 14.9 %collective-permute-start.18 = (bf16[128,1024]{1,0:T(8,128)(2,1)S(1)}, bf16[128,1024]{1,0:T(8,128)(2,1)S(1)}, u32[]{:S(2)}, u32[]{:S(2)}) collective-permute-start(bf16[128,1024]{1,0:T(8,128)(2,1)S(1)} %get-tuple-element.162), channel_id=1, source_target_pairs={{0,32},{1,33},{16,48},{17,49},{2,34},{3,35},{18,50},{19,51},{4,36}... | collective-permute-start | bytes 786440 | tf_op jit(solution)/shard_map/ppermute | solution.py:55
  185.0 58.3 %all-to-all-start.4 = ((bf16[16,108,8,128]{3,2,1,0:T(8,128)(2,1)}), bf16[16,108,8,128]{3,2,1,0:T(8,128)(2,1)S(1)}, u32[]{:S(2)}, u32[]{:S(2)}) async-start(bf16[16,108,8,128]{3,2,1,0:T(8,128)(2,1)} %pad_maximum_fusion), calls=%async_computation.4 | async-start | bytes 7077888 | tf_op jit(solution)/shard_map/all_to_all | solution.py:89
  191.5 81.7 %reduce-scatter.2.cloned.1.call-start = ((), (), s32[]{:S(2)}) async-start(), calls=%async_computation.9 | async-start | bytes 2359296 | tf_op jit(solution)/shard_map/reduce_scatter | solution.py:729
  223.3 19.6 %collective-permute-start.24 = (bf16[4,32,8,128]{3,2,1,0:T(8,128)(2,1)S(1)}, bf16[4,32,8,128]{3,2,1,0:T(8,128)(2,1)}, u32[]{:S(2)}, u32[]{:S(2)}) collective-permute-start(bf16[4,32,8,128]{3,2,1,0:T(8,128)(2,1)S(1)} %get-tuple-element.234), channel_id=1, source_target_pairs={{0,4},{1,5},{16,20},{17,21},{2,6},{3,7},{18,22},{19,23},{4,8},{5,9... | collective-permute-start | bytes 786440 | tf_op jit(solution)/shard_map/ppermute | solution.py:55
  225.0 25.6 %collective-permute-start.25 = (bf16[4,32,8,128]{3,2,1,0:T(8,128)(2,1)}, bf16[4,32,8,128]{3,2,1,0:T(8,128)(2,1)}, u32[]{:S(2)}, u32[]{:S(2)}) collective-permute-start(bf16[4,32,8,128]{3,2,1,0:T(8,128)(2,1)} %get-tuple-element.235), channel_id=1, source_target_pairs={{0,8},{1,9},{16,24},{17,25},{2,10},{3,11},{18,26},{19,27},{4,12},{... | collective-permute-start | bytes 786440 | tf_op jit(solution)/shard_map/ppermute | solution.py:55
  227.4 23.2 %collective-permute-start.26 = (bf16[4,32,8,128]{3,2,1,0:T(8,128)(2,1)}, bf16[4,32,8,128]{3,2,1,0:T(8,128)(2,1)}, u32[]{:S(2)}, u32[]{:S(2)}) collective-permute-start(bf16[4,32,8,128]{3,2,1,0:T(8,128)(2,1)} %get-tuple-element.233), channel_id=1, source_target_pairs={{0,12},{1,13},{16,28},{17,29},{2,14},{3,15},{18,30},{19,31},{4,0},... | collective-permute-start | bytes 786440 | tf_op jit(solution)/shard_map/ppermute | solution.py:55
  228.6 22.0 %collective-permute-start.21 = (bf16[128,1024]{1,0:T(8,128)(2,1)}, bf16[128,1024]{1,0:T(8,128)(2,1)}, u32[]{:S(2)}, u32[]{:S(2)}) collective-permute-start(bf16[128,1024]{1,0:T(8,128)(2,1)} %get-tuple-element.179), channel_id=1, source_target_pairs={{0,32},{1,33},{16,48},{17,49},{2,34},{3,35},{18,50},{19,51},{4,36}... | collective-permute-start | bytes 786440 | tf_op jit(solution)/shard_map/ppermute | solution.py:55
  228.6 22.0 %collective-permute-start.22 = (bf16[128,1024]{1,0:T(8,128)(2,1)}, bf16[128,1024]{1,0:T(8,128)(2,1)}, u32[]{:S(2)}, u32[]{:S(2)}) collective-permute-start(bf16[128,1024]{1,0:T(8,128)(2,1)} %get-tuple-element.180), channel_id=1, source_target_pairs={{0,64},{1,65},{16,80},{17,81},{2,66},{3,67},{18,82},{19,83},{4,68}... | collective-permute-start | bytes 786440 | tf_op jit(solution)/shard_map/ppermute | solution.py:55
  257.1 57.1 %all-to-all-start.6 = ((bf16[16,576,128]{2,1,0:T(8,128)(2,1)}), bf16[16,576,128]{2,1,0:T(8,128)(2,1)S(1)}, u32[]{:S(2)}, u32[]{:S(2)}) async-start(bf16[16,576,128]{2,1,0:T(8,128)(2,1)} %bitcast.134), calls=%async_computation.7 | async-start | bytes 4718592 | tf_op jit(solution)/shard_map/all_to_all | solution.py:89
  265.6 17.9 %collective-permute-start.27 = (bf16[32,8,128]{2,1,0:T(8,128)(2,1)S(1)}, bf16[32,8,128]{2,1,0:T(8,128)(2,1)S(1)}, u32[]{:S(2)}, u32[]{:S(2)}) collective-permute-start(bf16[32,8,128]{2,1,0:T(8,128)(2,1)S(1)} %get-tuple-element.238), channel_id=1, source_target_pairs={{0,16},{1,17},{16,2},{17,3},{2,18},{3,19},{18,0},{19,1},{4,20},{5,... | collective-permute-start | bytes 196616 | tf_op jit(solution)/shard_map/ppermute | solution.py:55
  267.1 16.4 %collective-permute-start.28 = (bf16[32,8,128]{2,1,0:T(8,128)(2,1)S(1)}, bf16[32,8,128]{2,1,0:T(8,128)(2,1)S(1)}, u32[]{:S(2)}, u32[]{:S(2)}) collective-permute-start(bf16[32,8,128]{2,1,0:T(8,128)(2,1)S(1)} %get-tuple-element.237), channel_id=1, source_target_pairs={{0,2},{1,3},{16,18},{17,19},{2,0},{3,1},{18,16},{19,17},{4,6},{5,7... | collective-permute-start | bytes 196616 | tf_op jit(solution)/shard_map/ppermute | solution.py:55
  269.5 14.0 %collective-permute-start.29 = (bf16[32,8,128]{2,1,0:T(8,128)(2,1)S(1)}, bf16[32,8,128]{2,1,0:T(8,128)(2,1)S(1)}, u32[]{:S(2)}, u32[]{:S(2)}) collective-permute-start(bf16[32,8,128]{2,1,0:T(8,128)(2,1)S(1)} %get-tuple-element.236), channel_id=1, source_target_pairs={{0,18},{1,19},{16,0},{17,1},{2,16},{3,17},{18,2},{19,3},{4,22},{5,... | collective-permute-start | bytes 196616 | tf_op jit(solution)/shard_map/ppermute | solution.py:55
  284.5 18.6 %collective-permute-start.30 = (bf16[2,3,8,128]{3,2,1,0:T(8,128)(2,1)S(1)}, bf16[2,3,8,128]{3,2,1,0:T(8,128)(2,1)S(1)}, u32[]{:S(2)}, u32[]{:S(2)}) collective-permute-start(bf16[2,3,8,128]{3,2,1,0:T(8,128)(2,1)S(1)} %get-tuple-element.251), channel_id=1, source_target_pairs={{0,96},{1,97},{16,112},{17,113},{2,98},{3,99},{18,114},{19,115},{4... | collective-permute-start | bytes 36872 | tf_op jit(solution)/shard_map/ppermute | solution.py:55
  285.5 17.7 %collective-permute-start.31 = (bf16[2,3,8,128]{3,2,1,0:T(8,128)(2,1)S(1)}, bf16[2,3,8,128]{3,2,1,0:T(8,128)(2,1)S(1)}, u32[]{:S(2)}, u32[]{:S(2)}) collective-permute-start(bf16[2,3,8,128]{3,2,1,0:T(8,128)(2,1)S(1)} %get-tuple-element.250), channel_id=1, source_target_pairs={{0,64},{1,65},{16,80},{17,81},{2,66},{3,67},{18,82},{19,83},{4,68}... | collective-permute-start | bytes 36872 | tf_op jit(solution)/shard_map/ppermute | solution.py:55
  286.6 16.5 %collective-permute-start.32 = (bf16[2,3,8,128]{3,2,1,0:T(8,128)(2,1)S(1)}, bf16[2,3,8,128]{3,2,1,0:T(8,128)(2,1)S(1)}, u32[]{:S(2)}, u32[]{:S(2)}) collective-permute-start(bf16[2,3,8,128]{3,2,1,0:T(8,128)(2,1)S(1)} %get-tuple-element.249), channel_id=1, source_target_pairs={{0,32},{1,33},{16,48},{17,49},{2,34},{3,35},{18,50},{19,51},{4,36}... | collective-permute-start | bytes 36872 | tf_op jit(solution)/shard_map/ppermute | solution.py:55
  286.6 18.6 %collective-permute-start.33 = (bf16[128,1024]{1,0:T(8,128)(2,1)S(1)}, bf16[128,1024]{1,0:T(8,128)(2,1)S(1)}, u32[]{:S(2)}, u32[]{:S(2)}) collective-permute-start(bf16[128,1024]{1,0:T(8,128)(2,1)S(1)} %add_convert_fusion.1), channel_id=1, source_target_pairs={{0,0},{1,16},{16,1},{17,17},{2,2},{3,18},{18,3},{19,19},{4,4},{5,2... | collective-permute-start | bytes 786440 | tf_op jit(solution)/shard_map/ppermute | solution.py:55
  301.2 12.9 %collective-permute-start.37 = (bf16[128,1024]{1,0:T(8,128)(2,1)}, bf16[128,1024]{1,0:T(8,128)(2,1)S(1)}, u32[]{:S(2)}, u32[]{:S(2)}) collective-permute-start(bf16[128,1024]{1,0:T(8,128)(2,1)} %fusion.6), channel_id=1, source_target_pairs={{0,0},{1,16},{16,1},{17,17},{2,2},{3,18},{18,3},{19,19},{4,4},{5,2... | collective-permute-start | bytes 786440 | tf_op jit(solution)/shard_map/ppermute | solution.py:55
  314.2 22.8 %collective-permute-start.42 = (bf16[16,576,128]{2,1,0:T(8,128)(2,1)S(1)}, bf16[16,576,128]{2,1,0:T(8,128)(2,1)}, u32[]{:S(2)}, u32[]{:S(2)}) collective-permute-start(bf16[16,576,128]{2,1,0:T(8,128)(2,1)S(1)} %all-to-all-done.6.mine_ref), channel_id=1, source_target_pairs={{0,1},{1,0},{16,17},{17,16},{2,3},{3,2},{18,19},{19,18},{4,5},{5,4... | collective-permute-start | bytes 7077896 | tf_op jit(solution)/shard_map/ppermute | solution.py:55
  (51 other events, 462.2 us)
Sparse Core Ops, SparseCore 0:
  86.8 24.9 all-gather.1
  209.1 34.8 reduce-scatter.1

commit v5 on v4

--- a/solution.py
+++ b/solution.py
@@ -391,12 +391,15 @@
     place_ref,
     place_row_ref,
     start_row_ref,
+    gains_ref,
+    second_ref,
     other_ref,
     own_ref,
-    pre_grad_ref,
-    out_grad_ref,
+    parts_ref,
     sums_ref,
     first_ref,
+    out_grad_ref,
+    pre_grad_ref,
     branch_ref,
     mixed_grad_ref,
     grad_ref,
@@ -451,18 +454,43 @@
         else:
             other_ref[to, :] = partial.astype(bf16)
 
-
-def attend_back(near, far, out_slot, kept, gain, tables, where):
-    outs = [
-        ((512, 1024), bf16),
-        ((512, 1024), bf16),
-        ((1024, 256), bf16),
-        ((128, 1024), f32),
-        ((8, 256), f32),
-        ((8, 1024), f32),
-    ]
-    arrays = (near, far, out_slot, *kept, gain, *tables)
+    turned_grad = matmul(pre_grad_ref[...].astype(f32).T.astype(bf16), normed_ref[...])
+    column = lax.broadcasted_iota(jnp.int32, (256, 1024), 1)
+    entry = lax.broadcasted_iota(jnp.int32, (256, 1024), 0)
+    wanted = jnp.where(column % 128 < 8, column // 128 * 8 + column % 128, -1)
+    row = lax.broadcasted_iota(jnp.int32, (128, 1024), 0)
+    rows = []
+    for inside in (entry < 128, (entry >= 128) & (entry < 192)):
+        chosen = jnp.where(inside & (entry % 64 == wanted), 1.0, 0.0).astype(bf16)
+        rows.append(matmul(sums_ref[...].astype(bf16), chosen)[0:1, :])
+    rows = [first_ref[0:1, :] / gains_ref[0:1, :], second_ref[...]] + rows
+    extra = jnp.zeros((128, 1024), f32)
+    for at, some in enumerate(rows):
+        extra = jnp.where(row == at, some, extra)
+    for shard in range(8):
+        span = slice(shard * 128, shard * 128 + 128)
+        tiles = (turned_grad[:128, span].T, turned_grad[128:, span].T, extra[:, span].T)
+        for j, tile in enumerate(tiles):
+            for at in range(16):
+                parts_ref[at // 4, at % 4, shard * 3 + j] = tile[at * 8 : at * 8 + 8]
+    for y in range(4):
+        for i in range(4):
+            for z in range(4):
+                for j in range(2):
+                    low, left = y * 32 + i * 8, z * 256 + j * 128
+                    parts_ref[y, z, 24 + i * 2 + j] = out_grad_ref[
+                        low : low + 8, left : left + 128
+                    ]
+
+
+def attend_back(near, far, out_slot, kept, gain, tables, gains, second, where):
+    outs = [((512, 1024), bf16), ((512, 1024), bf16), ((4, 4, 32, 8, 128), f32)]
+    arrays = (near, far, out_slot, *kept, gain, *tables, gains, second)
     scratch = [
+        pltpu.VMEM((8, 256), f32),
+        pltpu.VMEM((8, 1024), f32),
+        pltpu.VMEM((128, 1024), f32),
+        pltpu.VMEM((1024, 256), bf16),
         pltpu.VMEM((1024, 1024), bf16),
         pltpu.VMEM((1024, 128), bf16),
         pltpu.VMEM((1024, 256), f32),
@@ -664,12 +692,11 @@
     tables = place_tables(facts, core)
     upstream_own = send(cotangent[0], regroup)
     out_slot = jnp.where(core == z_low, out_mine, send(out_mine, z_up_home))
-    half, for_feed, upstream_own, out_slot, tables, down_mine = join(
-        half, for_feed, upstream_own, out_slot, tables, down_weight
+    half, for_feed, upstream_own, out_slot, tables = join(
+        half, for_feed, upstream_own, out_slot, tables
     )
 
     upstream = lax.all_gather(upstream_own, AXES, axis=0, axis_index_groups=x_rings, tiled=True)
-    down_got = send(down_mine, z_down_home)
     far = send(half, other_core)
     across = send(half[:, :128, 1024:], z_up)
     feed_came = exchange(for_feed, x_rings)
@@ -685,18 +712,19 @@
     )
     gain_first, gain_second = gains[0], gains[8]
     other_half = matmul(mixed[512:], out_slot).astype(bf16)
-    other_half, mixed, feed_came, down_got = join(other_half, mixed, feed_came, down_got)
-    down_slot = jnp.where(core == z_low, down_mine, down_got)
+    other_half, mixed, feed_came = join(other_half, mixed, feed_came)
     got = send(other_half, other_core)
     own_half = matmul(mixed[:512], out_slot)
     lower, upper = send(feed_came[:2], z_up), send(feed_came[2:], z_down)
     parts = scatter_sums(own_half, got)
-    parts, lower, upper, down_slot = join(parts, lower, upper, down_slot)
+    parts, lower, upper, down_mine = join(parts, lower, upper, down_weight)
 
     middle = inputs + add_up(parts)
     second_scale = rms_scale(middle)
     half = gather_half((middle * second_scale * gain_second).astype(bf16)).reshape(512, 1024)
-    half, upstream = join(half, upstream)
+    down_got = send(down_mine, z_down_home)
+    half, upstream, down_got = join(half, upstream, down_got)
+    down_slot = jnp.where(core == z_low, down_mine, down_got)
     far = send(half, other_core)
     upstream_far = send(upstream, other_core)
     other_half, own_half, hidden, pre_grad, normed_all, upstream = feed(
@@ -708,54 +736,45 @@
     parts = send_x(*rest)
     feed_weight_grad = matmul_tn(normed_all, pre_grad)
     down_weight_grad = matmul_tn(hidden, upstream)
-    feed_parts = cat(
-        [
-            rows_for_planes(feed_weight_grad).reshape(16, 72, 8, 128),
-            block_for_planes(down_weight_grad).reshape(16, 36, 8, 128),
-        ],
-        1,
-    )
-    first, parts, feed_parts, hidden = join(first, parts, feed_parts, hidden)
-    feed_parts = exchange(feed_parts, planes)
+    feed_parts = rows_for_planes(feed_weight_grad).reshape(16, 72, 8, 128)
+    down_parts = block_for_planes(down_weight_grad).reshape(16, 36, 8, 128)
+    first, parts, feed_parts, down_parts, hidden = join(
+        first, parts, feed_parts, down_parts, hidden
+    )
+    down_parts = exchange(down_parts, planes)
     second_grad = first + add_up(jnp.stack(parts))
     middle_norm_grad, second_gain_terms = norm_back(middle, second_scale, gain_second, second_grad)
     middle_grad = upstream_own.astype(f32) + middle_norm_grad
     second_gain_grad = jnp.sum(second_gain_terms, axis=0)
     near = gather_x(middle_grad.astype(bf16))
     result_rows = matmul(hidden, down_slot).astype(bf16)
-    near, result_rows = join(near, result_rows)
+    near, result_rows, down_parts, feed_parts = join(near, result_rows, down_parts, feed_parts)
+    feed_parts = exchange(feed_parts, planes)
     near = cat(near)
     far = send(near, other_core)
     result_sum = lax.psum_scatter(
         result_rows, AXES, scatter_dimension=0, axis_index_groups=x_groups, tiled=True
     )
-    other_half, own_half, pre_grad, out_weight_grad, gain_terms, first_terms = attend_back(
+    other_half, own_half, attention_parts = attend_back(
         near,
         far,
         out_slot,
         (attention_slice, first_normed, qkv, heads, scales, mixed, logs),
         gain,
         tables,
+        gains,
+        second_gain_grad[None],
         where,
     )
     first, rest = scatter_parts(own_half, send(other_half, other_core))
-    first, rest, pre_grad = join(first, rest, pre_grad)
+    first, rest, attention_parts = join(first, rest, attention_parts)
 
     parts = send_x(*rest)
-    attention_weight_grad = matmul_tn(first_normed, pre_grad)
-    first_gain_grad = first_terms[0] / gain_first
-    small = jnp.stack([gain_terms[0, :64] + gain_terms[0, 64:128], gain_terms[0, 128:192]], 1)
-    small = jnp.pad(small.reshape(8, 8, 2), ((0, 0), (0, 120), (0, 0))).reshape(1024, 2)
-    extra = cat([first_gain_grad[:, None], second_gain_grad[:, None], small], 1)
-    extra = jnp.pad(extra, ((0, 0), (0, 124)))
-    by_row = rows_for_planes(cat([attention_weight_grad, extra], 1)).reshape(4, 4, 24, 8, 128)
-    by_block = block_for_planes(out_weight_grad).reshape(4, 4, 8, 8, 128)
-    attention_parts = cat([by_row, by_block], 2)
     pieces = [pick(attention_parts, (y + step) % 4, 0) for step in range(4)]
     ring = send_ring(pieces, y_up, y_down, y_far)
-    feed_rows = add_up(feed_parts).astype(bf16)
-    feed_got = exchange_rows(feed_rows[:72].reshape(8, 9, 8, 128))
-    first, parts, ring, feed_got, feed_rows = join(first, parts, ring, feed_got, feed_rows)
+    feed_got = exchange_rows(add_up(feed_parts).astype(bf16).reshape(8, 9, 8, 128))
+    down_rows = add_up(down_parts).astype(bf16)
+    first, parts, ring, feed_got, down_rows = join(first, parts, ring, feed_got, down_rows)
 
     first_grad = first + add_up(jnp.stack(parts))
     input_norm_grad, _ = norm_back(inputs, rms_scale(inputs), gain_first, first_grad)
@@ -763,7 +782,7 @@
     rows = pieces[0].astype(f32) + add_up(jnp.stack(ring))
     pieces = [pick(rows, (z + step) % 4, 0) for step in range(4)]
     ring = send_ring(pieces, z_up, z_down, z_far)
-    feed_mine = return_planes(feed_got, feed_rows[72:])
+    feed_mine = return_planes(feed_got, down_rows)
     result = (middle + result_sum.astype(f32)).astype(bf16)
     ring, input_grad, result = join(ring, input_grad, result)
 
@@ -776,10 +795,11 @@
         gather_z(attention_got, rows[24:], z_low), input_grad, feed_mine
     )
     mine = gather_y(block)
+    gate_sum, up_sum, down_sum = feed_grads(feed_mine, send(feed_mine, other_core), where)
+    mine, gate_sum, up_sum, down_sum = join(mine, gate_sum, up_sum, down_sum)
     query_sum, key_sum, value_sum, out_sum, gain_sums = attention_grads(
         mine, send(mine, other_core), where
     )
-    gate_sum, up_sum, down_sum = feed_grads(feed_mine, send(feed_mine, other_core), where)
     return (
         result[None],
         input_grad.astype(f32)[None],

time: 355 us -> 343 us (0.966)
  starting transfers between devices: 106 us -> 99.3 us
  other arithmetic: 34.4 us -> 28.6 us
    ppermute x43, starting transfers between devices: 72.6 us -> 63 us  [send(): return lax.ppermute(values, AXES, moves)]
    ppermute x43, waiting for transfers between devices: 77.8 us -> 84.5 us  [send(): return lax.ppermute(values, AXES, moves)]
    all_gather x1, waiting for transfers between devices: 6.33 us -> 2.32 us  [on_device(): lax.all_gather(upstream_own, AXES, axis=0, axis_index_groups=x_rings, til...]
    all_to_all x7 -> x8, starting transfers between devices: 33.2 us -> 36.3 us  [exchange(): return lax.all_to_all(values, AXES, 0, 0, axis_index_groups=groups)]
    all_to_all x7 -> x8, waiting for transfers between devices: 15.7 us -> 14.8 us  [exchange(): return lax.all_to_all(values, AXES, 0, 0, axis_index_groups=groups)]
  transfers between devices with their start and end apart: 52 -> 53, of which waited for: 25 -> 28; matrix products, arithmetic and copies ran while one was open for 17% -> 16% of each run, Pallas kernels for 10% -> 10%
where the time goes in v5:
time: 343 us; the launch traced here: 338 us
  waiting for transfers between devices  102 us (30%)
  starting transfers between devices  99.3 us (29%)
  Pallas kernels  58.7 us (17%)
  other arithmetic  28.6 us (8%)
  local copies, waits for them, and re-layouts  22.5 us (7%)
  between operations  15 us (4%)
  matrix products  12.7 us (4%)
    ppermute x43, waiting for transfers between devices, send(): return lax.ppermute(values, AXES, moves)  84.5 us
    ppermute x43, starting transfers between devices, send(): return lax.ppermute(values, AXES, moves)  63 us
    pallas_call x6, Pallas kernels, call(): pl.pallas_call(kernel, out_shape=[jax.ShapeDtypeStruct(shape, kind) for s...  57 us
    all_to_all x8, starting transfers between devices, exchange(): return lax.all_to_all(values, AXES, 0, 0, axis_index_groups=groups)  36.3 us
    all_to_all x8, waiting for transfers between devices, exchange(): return lax.all_to_all(values, AXES, 0, 0, axis_index_groups=groups)  14.8 us
  transfers between devices with their start and end apart: 53, of which 28 were waited for; matrix products, arithmetic and copies ran while one was open for 16% of the time, Pallas kernels for 10%

profile of v5, /device:TPU:1, one launch (start us, length us, event | category | flops | bytes accessed | tf_op | source)
XLA Modules:
  0.0 338.5 jit_solution(4950501279125006693)
XLA Ops:
  12.9 3.5 %collective-permute-start = (bf16[144,1024]{1,0:T(8,128)(2,1)}, bf16[144,1024]{1,0:T(8,128)(2,1)S(1)}, u32[]{:S(2)}, u32[]{:S(2)}) collective-permute-start(bf16[144,1024]{1,0:T(8,128)(2,1)} %shard_map.246), channel_id=1, source_target_pairs={{0,0},{1,16},{16,1},{17,17},{2,2},{3,18},{18,3},{19,19},{4,4},{5,2... | collective-permute-start | bytes 884744 | tf_op jit(solution)/shard_map/ppermute | solution.py:55
  17.8 3.3 collective-permute-done.packed_ref
  21.9 4.5 %shard_map.247 = (bf16[4,144,1280]{2,1,0:T(8,128)(2,1)}, bf16[4,128,1152]{2,1,0:T(8,128)(2,1)}) custom-call(s32[1]{0:T(128)} %bitcast.1.spot_ref, bf16[128,1024]{1,0:T(8,128)(2,1)} %q_ref.1, bf16[128,512]{1,0:T(8,128)(2,1)} %k_ref.1, bf16[128,512]{1,0:T(8,128)(2,1)} %v_ref.1, bf16[128,4608]{1,0:T(8,128)(2,1)} %gate_ref.1, bf16[128,4608]{1,0:T(8,128)(2,1)} %up_ref.1, ...), custom_call_target="tpu_custom_call" | custom-call | bytes 3178496 | tf_op jit(solution)/shard_map/pallas_call | solution.py:179
  26.4 4.5 %all-to-all-start = ((bf16[4,144,1280]{2,1,0:T(8,128)(2,1)}), bf16[4,144,1280]{2,1,0:T(8,128)(2,1)}, u32[]{:S(2)}, u32[]{:S(2)}) async-start(bf16[4,144,1280]{2,1,0:T(8,128)(2,1)} %get-tuple-element.117), calls=%async_computation | async-start | bytes 2949120 | tf_op jit(solution)/shard_map/all_to_all | solution.py:89
  34.6 3.5 %collective-permute-start.2 = (bf16[128,1024]{1,0:T(8,128)(2,1)S(1)}, bf16[128,1024]{1,0:T(8,128)(2,1)S(1)}, u32[]{:S(2)}, u32[]{:S(2)}) collective-permute-start(bf16[128,1024]{1,0:T(8,128)(2,1)S(1)} %bitcast.159), channel_id=1, source_target_pairs={{0,0},{1,16},{16,1},{17,17},{2,2},{3,18},{18,3},{19,19},{4,4},{5,2... | collective-permute-start | bytes 786440 | tf_op jit(solution)/shard_map/ppermute | solution.py:55
  38.2 3.1 fusion.7
  42.3 3.8 %all-to-all-done.half_ref = bf16[4,144,1280]{2,1,0:T(8,128)(2,1)} async-done(((bf16[4,144,1280]{2,1,0:T(8,128)(2,1)}), bf16[4,144,1280]{2,1,0:T(8,128)(2,1)}, u32[]{:S(2)}, u32[]{:S(2)}) %all-to-all-start) | async-done | bytes 1474592 | tf_op jit(solution)/shard_map/all_to_all | solution.py:89
  51.3 3.7 %all-to-all-start.1 = ((bf16[4,128,1152]{2,1,0:T(8,128)(2,1)}), bf16[4,128,1152]{2,1,0:T(8,128)(2,1)S(1)}, u32[]{:S(2)}, u32[]{:S(2)}) async-start(bf16[4,128,1152]{2,1,0:T(8,128)(2,1)} %get-tuple-element.133), calls=%async_computation.1 | async-start | bytes 2359296 | tf_op jit(solution)/shard_map/all_to_all | solution.py:89
  59.5 13.1 %shard_map.248 = (bf16[1024,256]{1,0:T(8,128)(2,1)}, bf16[1024,1024]{1,0:T(8,128)(2,1)}, bf16[1024,256]{1,0:T(8,128)(2,1)}, f32[1024,256]{1,0:T(8,128)}, f32[102...) custom-call(s32[2]{0:T(128)} %pad_add_fusion.1.spot_ref, ...), custom_call_target="tpu_custom_call" | custom-call | flops 2147483648 | bytes 4273152 | tf_op jit(solution)/shard_map/pallas_call | solution.py:179
  79.2 3.5 %all-to-all-start.2 = ((bf16[4,128,1024]{2,1,0:T(8,128)(2,1)}), bf16[4,128,1024]{2,1,0:T(8,128)(2,1)S(1)}, u32[]{:S(2)}, u32[]{:S(2)}) async-start(bf16[4,128,1024]{2,1,0:T(8,128)(2,1)} %bitcast.112), calls=%async_computation.2 | async-start | bytes 2097152 | tf_op jit(solution)/shard_map/all_to_all | solution.py:89
  87.4 12.5 %collective-permute-done.7.lower_ref = bf16[2,128,1152]{2,1,0:T(8,128)(2,1)S(1)} collective-permute-done((bf16[2,128,1152]{2,1,0:T(8,128)(2,1)}, bf16[2,128,1152]{2,1,0:T(8,128)(2,1)S(1)}, u32[]{:S(2)}, u32[]{:S(2)}) %collective-permute-start.7) | collective-permute-done | bytes 589856 | tf_op jit(solution)/shard_map/ppermute | solution.py:55
  102.8 4.3 %all-to-all-start.3 = ((bf16[4,128,1024]{2,1,0:T(8,128)(2,1)}), bf16[4,128,1024]{2,1,0:T(8,128)(2,1)}, u32[]{:S(2)}, u32[]{:S(2)}) async-start(bf16[4,128,1024]{2,1,0:T(8,128)(2,1)} %broadcast_in_dim.84), calls=%async_computation.3 | async-start | bytes 2097152 | tf_op jit(solution)/shard_map/all_to_all | solution.py:89
  109.4 7.5 %all-to-all-done.3 = bf16[4,128,1024]{2,1,0:T(8,128)(2,1)} async-done(((bf16[4,128,1024]{2,1,0:T(8,128)(2,1)}), bf16[4,128,1024]{2,1,0:T(8,128)(2,1)}, u32[]{:S(2)}, u32[]{:S(2)}) %all-to-all-start.3) | async-done | bytes 1048608 | tf_op jit(solution)/shard_map/all_to_all | solution.py:89
  117.6 5.6 %collective-permute-start.10 = (bf16[512,1024]{1,0:T(8,128)(2,1)}, bf16[512,1024]{1,0:T(8,128)(2,1)}, u32[]{:S(2)}, u32[]{:S(2)}) collective-permute-start(bf16[512,1024]{1,0:T(8,128)(2,1)} %bitcast.20.half_ref), channel_id=1, source_target_pairs={{0,1},{1,0},{16,17},{17,16},{2,3},{3,2},{18,19},{19,18},{4,5},{5,4... | collective-permute-start | bytes 3145736 | tf_op jit(solution)/shard_map/ppermute | solution.py:55
  127.4 15.2 %shard_map.249 = (bf16[512,1024]{1,0:T(8,128)(2,1)}, bf16[512,1024]{1,0:T(8,128)(2,1)}, bf16[1024,576]{1,0:T(8,128)(2,1)}, bf16[1024,1152]{1,0:T(8,128)(2,1)}, b...) custom-call(s32[3]{0:T(128)} %pad_add_fusion.2.spot_ref, bf16[512,1024]{1,0:T(8,128)(2,1)} %bitcast.20.half_ref, ...), custom_call_target="tpu_custom_call" | custom-call | flops 6442450944 | bytes 7733248 | tf_op jit(solution)/shard_map/pallas_call | solution.py:179
  149.9 4.6 %convolution_convert_fusion = bf16[1024,1152]{1,0:T(8,128)(2,1)S(1)} fusion(bf16[1024,1024]{1,0:T(8,128)(2,1)} %get-tuple-element.154, bf16[1024,1152]{1,0:T(8,128)(2,1)S(1)} %copy-done.23), kind=kOutput, calls=%fused_computation | convolution fusion | flops 2417098752 | bytes 6815744 | tf_op jit(solution)/shard_map/dot_general | solution.py:207
  161.8 6.6 %all-to-all-start.4 = ((bf16[16,36,8,128]{3,2,1,0:T(8,128)(2,1)}), bf16[16,36,8,128]{3,2,1,0:T(8,128)(2,1)S(1)}, u32[]{:S(2)}, u32[]{:S(2)}) async-start(bf16[16,36,8,128]{3,2,1,0:T(8,128)(2,1)} %bitcast.26), calls=%async_computation.4 | async-start | bytes 2359296 | tf_op jit(solution)/shard_map/all_to_all | solution.py:89
  170.4 2.9 collective-permute-start.16
  174.1 3.1 convolution_convert_fusion.1
  181.5 6.9 %collective-permute-done.18 = bf16[128,1024]{1,0:T(8,128)(2,1)S(1)} collective-permute-done((bf16[128,1024]{1,0:T(8,128)(2,1)S(1)}, bf16[128,1024]{1,0:T(8,128)(2,1)S(1)}, u32[]{:S(2)}, u32[]{:S(2)}) %collective-permute-start.18) | collective-permute-done | bytes 262176 | tf_op jit(solution)/shard_map/ppermute | solution.py:55
  192.0 6.7 %all-to-all-start.5 = ((bf16[16,72,8,128]{3,2,1,0:T(8,128)(2,1)}), bf16[16,72,8,128]{3,2,1,0:T(8,128)(2,1)S(1)}, u32[]{:S(2)}, u32[]{:S(2)}) async-start(bf16[16,72,8,128]{3,2,1,0:T(8,128)(2,1)} %bitcast.23), calls=%async_computation.5 | async-start | bytes 4718592 | tf_op jit(solution)/shard_map/all_to_all | solution.py:89
  198.7 18.0 %shard_map.250 = (bf16[512,1024]{1,0:T(8,128)(2,1)}, bf16[512,1024]{1,0:T(8,128)(2,1)}, f32[4,4,32,8,128]{4,3,2,1,0:T(8,128)}) custom-call(s32[1]{0:T(128)} %bitcast.spot_ref, bf16[512,1024]{1,0:T(8,128)(2,1)} %constant_dynamic-update-slice_fusion.near_ref, bf16[512,1024]{1,0:T(8,128)(2,1)} %collective-permute-done.19.far_ref, bf16[128,1024]{1,0:T(8,128)(2,1)} %copy-done.5, ...), custom_call_target="tpu_custom_call" | custom-call | flops 4294967296 | bytes 9028608 | tf_op jit(solution)/shard_map/pallas_call | solution.py:179
  231.6 7.2 %collective-permute-done.24 = bf16[4,32,8,128]{3,2,1,0:T(8,128)(2,1)} collective-permute-done((bf16[4,32,8,128]{3,2,1,0:T(8,128)(2,1)S(1)}, bf16[4,32,8,128]{3,2,1,0:T(8,128)(2,1)}, u32[]{:S(2)}, u32[]{:S(2)}) %collective-permute-start.24) | collective-permute-done | bytes 262176 | tf_op jit(solution)/shard_map/ppermute | solution.py:55
  240.3 3.3 all-to-all-start.6
  245.1 3.4 %all-to-all-done.6 = bf16[4,2,9,8,128]{4,3,2,1,0:T(8,128)(2,1)S(1)} async-done(((bf16[4,2,9,8,128]{4,3,2,1,0:T(8,128)(2,1)}), bf16[4,2,9,8,128]{4,3,2,1,0:T(8,128)(2,1)S(1)}, u32[]{:S(2)}, u32[]{:S(2)}) %all-to-all-start.6) | async-done | bytes 147488 | tf_op jit(solution)/shard_map/all_to_all | solution.py:89
  250.5 3.7 %all-to-all-start.7 = ((bf16[16,576,128]{2,1,0:T(8,128)(2,1)}), bf16[16,576,128]{2,1,0:T(8,128)(2,1)S(1)}, u32[]{:S(2)}, u32[]{:S(2)}) async-start(bf16[16,576,128]{2,1,0:T(8,128)(2,1)} %bitcast.111), calls=%async_computation.8 | async-start | bytes 4718592 | tf_op jit(solution)/shard_map/all_to_all | solution.py:89
  265.8 18.2 %collective-permute-done.27 = bf16[32,8,128]{2,1,0:T(8,128)(2,1)S(1)} collective-permute-done((bf16[32,8,128]{2,1,0:T(8,128)(2,1)}, bf16[32,8,128]{2,1,0:T(8,128)(2,1)S(1)}, u32[]{:S(2)}, u32[]{:S(2)}) %collective-permute-start.27) | collective-permute-done | bytes 65568 | tf_op jit(solution)/shard_map/ppermute | solution.py:55
  288.5 4.3 %collective-permute-start.33 = (bf16[128,1024]{1,0:T(8,128)(2,1)S(1)}, bf16[128,1024]{1,0:T(8,128)(2,1)S(1)}, u32[]{:S(2)}, u32[]{:S(2)}) collective-permute-start(bf16[128,1024]{1,0:T(8,128)(2,1)S(1)} %add_convert_fusion.1), channel_id=1, source_target_pairs={{0,0},{1,16},{16,1},{17,17},{2,2},{3,18},{18,3},{19,19},{4,4},{5,2... | collective-permute-start | bytes 786440 | tf_op jit(solution)/shard_map/ppermute | solution.py:55
  297.0 3.9 %collective-permute-start.35 = (bf16[160,128]{1,0:T(8,128)(2,1)S(1)}, bf16[160,128]{1,0:T(8,128)(2,1)S(1)}, u32[]{:S(2)}, u32[]{:S(2)}) collective-permute-start(bf16[160,128]{1,0:T(8,128)(2,1)S(1)} %get-tuple-element.257), channel_id=1, source_target_pairs={{0,2},{1,3},{16,18},{17,19},{2,0},{3,1},{18,16},{19,17},{4,6},{5,7... | collective-permute-start | bytes 122888 | tf_op jit(solution)/shard_map/ppermute | solution.py:55
  313.4 3.1 collective-permute-done.39
  316.5 4.2 %collective-permute-done.40 = bf16[4,160,128]{2,1,0:T(8,128)(2,1)S(1)} collective-permute-done((bf16[4,160,128]{2,1,0:T(8,128)(2,1)S(1)}, bf16[4,160,128]{2,1,0:T(8,128)(2,1)S(1)}, u32[]{:S(2)}, u32[]{:S(2)}) %collective-permute-start.40) | collective-permute-done | bytes 163872 | tf_op jit(solution)/shard_map/ppermute | solution.py:55
  320.8 4.1 %shard_map.251 = (f32[128,4608]{1,0:T(8,128)}, f32[128,4608]{1,0:T(8,128)}, f32[576,1024]{1,0:T(8,128)}) custom-call(s32[2]{0:T(128)S(1)} %pad_add_fusion.3.spot_ref, bf16[16,576,128]{2,1,0:T(8,128)(2,1)S(1)} %all-to-all-done.7.mine_ref, bf16[16,576,128]{2,1,0:T(8,128)(2,1)S(1)} %collective-permute-done.41.other_ref), custom_call_target="tpu_custom_call" | custom-call | bytes 4718592 | tf_op jit(solution)/shard_map/pallas_call | solution.py:179
  (214 shorter events, 127.7 us)
Async XLA Ops:
  26.4 19.7 %all-to-all-start = ((bf16[4,144,1280]{2,1,0:T(8,128)(2,1)}), bf16[4,144,1280]{2,1,0:T(8,128)(2,1)}, u32[]{:S(2)}, u32[]{:S(2)}) async-start(bf16[4,144,1280]{2,1,0:T(8,128)(2,1)} %get-tuple-element.117), calls=%async_computation | async-start | bytes 2949120 | tf_op jit(solution)/shard_map/all_to_all | solution.py:89
  31.4 9.8 %collective-permute-start.3 = (bf16[128,1024]{1,0:T(8,128)(2,1)S(1)}, bf16[128,1024]{1,0:T(8,128)(2,1)S(1)}, u32[]{:S(2)}, u32[]{:S(2)}) collective-permute-start(bf16[128,1024]{1,0:T(8,128)(2,1)S(1)} %copy-done.14), channel_id=1, source_target_pairs={{0,16},{17,3},{2,18},{19,1},{4,20},{21,7},{6,22},{23,5},{8,24},{25... | collective-permute-start | bytes 786440 | tf_op jit(solution)/shard_map/ppermute | solution.py:55
  46.1 11.7 %collective-permute-start.4 = (bf16[4,144,1280]{2,1,0:T(8,128)(2,1)}, bf16[4,144,1280]{2,1,0:T(8,128)(2,1)}, u32[]{:S(2)}, u32[]{:S(2)}) collective-permute-start(bf16[4,144,1280]{2,1,0:T(8,128)(2,1)} %all-to-all-done.half_ref), channel_id=1, source_target_pairs={{0,1},{1,0},{16,17},{17,16},{2,3},{3,2},{18,19},{19,18},{4,5},{5,4... | collective-permute-start | bytes 4423688 | tf_op jit(solution)/shard_map/ppermute | solution.py:55
  47.1 10.7 %collective-permute-start.5 = (bf16[4,128,256]{2,1,0:T(8,128)(2,1)S(1)}, bf16[4,128,256]{2,1,0:T(8,128)(2,1)S(1)}, u32[]{:S(2)}, u32[]{:S(2)}) collective-permute-start(bf16[4,128,256]{2,1,0:T(8,128)(2,1)S(1)} %slice.122), channel_id=1, source_target_pairs={{0,16},{1,17},{16,2},{17,3},{2,18},{3,19},{18,0},{19,1},{4,20},{5,... | collective-permute-start | bytes 786440 | tf_op jit(solution)/shard_map/ppermute | solution.py:55
  51.3 22.6 %all-to-all-start.1 = ((bf16[4,128,1152]{2,1,0:T(8,128)(2,1)}), bf16[4,128,1152]{2,1,0:T(8,128)(2,1)S(1)}, u32[]{:S(2)}, u32[]{:S(2)}) async-start(bf16[4,128,1152]{2,1,0:T(8,128)(2,1)} %get-tuple-element.133), calls=%async_computation.1 | async-start | bytes 2359296 | tf_op jit(solution)/shard_map/all_to_all | solution.py:89
  79.2 20.7 %all-to-all-start.2 = ((bf16[4,128,1024]{2,1,0:T(8,128)(2,1)}), bf16[4,128,1024]{2,1,0:T(8,128)(2,1)S(1)}, u32[]{:S(2)}, u32[]{:S(2)}) async-start(bf16[4,128,1024]{2,1,0:T(8,128)(2,1)} %bitcast.112), calls=%async_computation.2 | async-start | bytes 2097152 | tf_op jit(solution)/shard_map/all_to_all | solution.py:89
  82.7 26.7 %all-gather.2.cloned.1.call-start = ((), (), s32[]{:S(2)}) async-start(), calls=%async_computation.9 | async-start | bytes 1310720 | tf_op jit(solution)/shard_map/all_gather | solution.py:699
  83.9 16.0 %collective-permute-start.7 = (bf16[2,128,1152]{2,1,0:T(8,128)(2,1)}, bf16[2,128,1152]{2,1,0:T(8,128)(2,1)S(1)}, u32[]{:S(2)}, u32[]{:S(2)}) collective-permute-start(bf16[2,128,1152]{2,1,0:T(8,128)(2,1)} %get-tuple-element.239), channel_id=1, source_target_pairs={{0,16},{1,17},{16,2},{17,3},{2,18},{3,19},{18,0},{19,1},{4,20},{5,... | collective-permute-start | bytes 1769480 | tf_op jit(solution)/shard_map/ppermute | solution.py:55
  83.9 16.0 %collective-permute-start.8 = (bf16[2,128,1152]{2,1,0:T(8,128)(2,1)}, bf16[2,128,1152]{2,1,0:T(8,128)(2,1)S(1)}, u32[]{:S(2)}, u32[]{:S(2)}) collective-permute-start(bf16[2,128,1152]{2,1,0:T(8,128)(2,1)} %get-tuple-element.238), channel_id=1, source_target_pairs={{0,18},{1,19},{16,0},{17,1},{2,16},{3,17},{18,2},{19,3},{4,22},{5,... | collective-permute-start | bytes 1769480 | tf_op jit(solution)/shard_map/ppermute | solution.py:55
  100.1 17.6 %collective-permute-start.9 = (bf16[576,1024]{1,0:T(8,128)(2,1)}, bf16[576,1024]{1,0:T(8,128)(2,1)S(1)}, u32[]{:S(2)}, u32[]{:S(2)}) collective-permute-start(bf16[576,1024]{1,0:T(8,128)(2,1)} %param.28), channel_id=1, source_target_pairs={{0,18},{17,1},{2,16},{19,3},{4,22},{21,5},{6,20},{23,7},{8,26},{25... | collective-permute-start | bytes 3538952 | tf_op jit(solution)/shard_map/ppermute | solution.py:55
  102.8 14.1 %all-to-all-start.3 = ((bf16[4,128,1024]{2,1,0:T(8,128)(2,1)}), bf16[4,128,1024]{2,1,0:T(8,128)(2,1)}, u32[]{:S(2)}, u32[]{:S(2)}) async-start(bf16[4,128,1024]{2,1,0:T(8,128)(2,1)} %broadcast_in_dim.84), calls=%async_computation.3 | async-start | bytes 2097152 | tf_op jit(solution)/shard_map/all_to_all | solution.py:89
  147.1 11.9 %collective-permute-start.13 = (bf16[128,1024]{1,0:T(8,128)(2,1)S(1)}, bf16[128,1024]{1,0:T(8,128)(2,1)S(1)}, u32[]{:S(2)}, u32[]{:S(2)}) collective-permute-start(bf16[128,1024]{1,0:T(8,128)(2,1)S(1)} %get-tuple-element.151), channel_id=1, source_target_pairs={{0,32},{1,33},{16,48},{17,49},{2,34},{3,35},{18,50},{19,51},{4,36}... | collective-permute-start | bytes 786440 | tf_op jit(solution)/shard_map/ppermute | solution.py:55
  147.4 13.5 %collective-permute-start.14 = (bf16[128,1024]{1,0:T(8,128)(2,1)S(1)}, bf16[128,1024]{1,0:T(8,128)(2,1)S(1)}, u32[]{:S(2)}, u32[]{:S(2)}) collective-permute-start(bf16[128,1024]{1,0:T(8,128)(2,1)S(1)} %get-tuple-element.152), channel_id=1, source_target_pairs={{0,64},{1,65},{16,80},{17,81},{2,66},{3,67},{18,82},{19,83},{4,68}... | collective-permute-start | bytes 786440 | tf_op jit(solution)/shard_map/ppermute | solution.py:55
  149.2 12.6 %collective-permute-start.15 = (bf16[128,1024]{1,0:T(8,128)(2,1)S(1)}, bf16[128,1024]{1,0:T(8,128)(2,1)S(1)}, u32[]{:S(2)}, u32[]{:S(2)}) collective-permute-start(bf16[128,1024]{1,0:T(8,128)(2,1)S(1)} %get-tuple-element.153), channel_id=1, source_target_pairs={{0,96},{1,97},{16,112},{17,113},{2,98},{3,99},{18,114},{19,115},{4... | collective-permute-start | bytes 786440 | tf_op jit(solution)/shard_map/ppermute | solution.py:55
  161.8 26.6 %all-to-all-start.4 = ((bf16[16,36,8,128]{3,2,1,0:T(8,128)(2,1)}), bf16[16,36,8,128]{3,2,1,0:T(8,128)(2,1)S(1)}, u32[]{:S(2)}, u32[]{:S(2)}) async-start(bf16[16,36,8,128]{3,2,1,0:T(8,128)(2,1)} %bitcast.26), calls=%async_computation.4 | async-start | bytes 2359296 | tf_op jit(solution)/shard_map/all_to_all | solution.py:89
  168.4 96.4 %reduce-scatter.2.cloned.1.call-start = ((), (), s32[]{:S(2)}) async-start(), calls=%async_computation.10 | async-start | bytes 2359296 | tf_op jit(solution)/shard_map/reduce_scatter | solution.py:755
  170.4 9.6 %collective-permute-start.16 = (bf16[128,1024]{1,0:T(8,128)(2,1)S(1)}, bf16[128,1024]{1,0:T(8,128)(2,1)S(1)}, u32[]{:S(2)}, u32[]{:S(2)}) collective-permute-start(bf16[128,1024]{1,0:T(8,128)(2,1)S(1)} %get-tuple-element.165), channel_id=1, source_target_pairs={{0,96},{1,97},{16,112},{17,113},{2,98},{3,99},{18,114},{19,115},{4... | collective-permute-start | bytes 786440 | tf_op jit(solution)/shard_map/ppermute | solution.py:55
  173.3 15.1 %collective-permute-start.18 = (bf16[128,1024]{1,0:T(8,128)(2,1)S(1)}, bf16[128,1024]{1,0:T(8,128)(2,1)S(1)}, u32[]{:S(2)}, u32[]{:S(2)}) collective-permute-start(bf16[128,1024]{1,0:T(8,128)(2,1)S(1)} %get-tuple-element.165), channel_id=1, source_target_pairs={{0,32},{1,33},{16,48},{17,49},{2,34},{3,35},{18,50},{19,51},{4,36}... | collective-permute-start | bytes 786440 | tf_op jit(solution)/shard_map/ppermute | solution.py:55
  192.0 47.2 %all-to-all-start.5 = ((bf16[16,72,8,128]{3,2,1,0:T(8,128)(2,1)}), bf16[16,72,8,128]{3,2,1,0:T(8,128)(2,1)S(1)}, u32[]{:S(2)}, u32[]{:S(2)}) async-start(bf16[16,72,8,128]{3,2,1,0:T(8,128)(2,1)} %bitcast.23), calls=%async_computation.5 | async-start | bytes 4718592 | tf_op jit(solution)/shard_map/all_to_all | solution.py:89
  224.9 14.0 %collective-permute-start.24 = (bf16[4,32,8,128]{3,2,1,0:T(8,128)(2,1)S(1)}, bf16[4,32,8,128]{3,2,1,0:T(8,128)(2,1)}, u32[]{:S(2)}, u32[]{:S(2)}) collective-permute-start(bf16[4,32,8,128]{3,2,1,0:T(8,128)(2,1)S(1)} %get-tuple-element.229), channel_id=1, source_target_pairs={{0,4},{1,5},{16,20},{17,21},{2,6},{3,7},{18,22},{19,23},{4,8},{5,9... | collective-permute-start | bytes 786440 | tf_op jit(solution)/shard_map/ppermute | solution.py:55
  226.4 22.1 %collective-permute-start.25 = (bf16[4,32,8,128]{3,2,1,0:T(8,128)(2,1)}, bf16[4,32,8,128]{3,2,1,0:T(8,128)(2,1)}, u32[]{:S(2)}, u32[]{:S(2)}) collective-permute-start(bf16[4,32,8,128]{3,2,1,0:T(8,128)(2,1)} %get-tuple-element.228), channel_id=1, source_target_pairs={{0,8},{1,9},{16,24},{17,25},{2,10},{3,11},{18,26},{19,27},{4,12},{... | collective-permute-start | bytes 786440 | tf_op jit(solution)/shard_map/ppermute | solution.py:55
  228.9 19.6 %collective-permute-start.26 = (bf16[4,32,8,128]{3,2,1,0:T(8,128)(2,1)}, bf16[4,32,8,128]{3,2,1,0:T(8,128)(2,1)}, u32[]{:S(2)}, u32[]{:S(2)}) collective-permute-start(bf16[4,32,8,128]{3,2,1,0:T(8,128)(2,1)} %get-tuple-element.227), channel_id=1, source_target_pairs={{0,12},{1,13},{16,28},{17,29},{2,14},{3,15},{18,30},{19,31},{4,0},... | collective-permute-start | bytes 786440 | tf_op jit(solution)/shard_map/ppermute | solution.py:55
  230.0 18.5 %collective-permute-start.21 = (bf16[128,1024]{1,0:T(8,128)(2,1)}, bf16[128,1024]{1,0:T(8,128)(2,1)}, u32[]{:S(2)}, u32[]{:S(2)}) collective-permute-start(bf16[128,1024]{1,0:T(8,128)(2,1)} %get-tuple-element.180), channel_id=1, source_target_pairs={{0,32},{1,33},{16,48},{17,49},{2,34},{3,35},{18,50},{19,51},{4,36}... | collective-permute-start | bytes 786440 | tf_op jit(solution)/shard_map/ppermute | solution.py:55
  230.0 18.5 %collective-permute-start.22 = (bf16[128,1024]{1,0:T(8,128)(2,1)}, bf16[128,1024]{1,0:T(8,128)(2,1)}, u32[]{:S(2)}, u32[]{:S(2)}) collective-permute-start(bf16[128,1024]{1,0:T(8,128)(2,1)} %get-tuple-element.181), channel_id=1, source_target_pairs={{0,64},{1,65},{16,80},{17,81},{2,66},{3,67},{18,82},{19,83},{4,68}... | collective-permute-start | bytes 786440 | tf_op jit(solution)/shard_map/ppermute | solution.py:55
  238.8 9.7 %collective-permute-start.23 = (bf16[128,1024]{1,0:T(8,128)(2,1)}, bf16[128,1024]{1,0:T(8,128)(2,1)}, u32[]{:S(2)}, u32[]{:S(2)}) collective-permute-start(bf16[128,1024]{1,0:T(8,128)(2,1)} %get-tuple-element.182), channel_id=1, source_target_pairs={{0,96},{1,97},{16,112},{17,113},{2,98},{3,99},{18,114},{19,115},{4... | collective-permute-start | bytes 786440 | tf_op jit(solution)/shard_map/ppermute | solution.py:55
  250.5 54.6 %all-to-all-start.7 = ((bf16[16,576,128]{2,1,0:T(8,128)(2,1)}), bf16[16,576,128]{2,1,0:T(8,128)(2,1)S(1)}, u32[]{:S(2)}, u32[]{:S(2)}) async-start(bf16[16,576,128]{2,1,0:T(8,128)(2,1)} %bitcast.111), calls=%async_computation.8 | async-start | bytes 4718592 | tf_op jit(solution)/shard_map/all_to_all | solution.py:89
  257.5 26.5 %collective-permute-start.27 = (bf16[32,8,128]{2,1,0:T(8,128)(2,1)}, bf16[32,8,128]{2,1,0:T(8,128)(2,1)S(1)}, u32[]{:S(2)}, u32[]{:S(2)}) collective-permute-start(bf16[32,8,128]{2,1,0:T(8,128)(2,1)} %get-tuple-element.242), channel_id=1, source_target_pairs={{0,16},{1,17},{16,2},{17,3},{2,18},{3,19},{18,0},{19,1},{4,20},{5,... | collective-permute-start | bytes 196616 | tf_op jit(solution)/shard_map/ppermute | solution.py:55
  258.7 25.3 %collective-permute-start.28 = (bf16[32,8,128]{2,1,0:T(8,128)(2,1)}, bf16[32,8,128]{2,1,0:T(8,128)(2,1)S(1)}, u32[]{:S(2)}, u32[]{:S(2)}) collective-permute-start(bf16[32,8,128]{2,1,0:T(8,128)(2,1)} %get-tuple-element.241), channel_id=1, source_target_pairs={{0,2},{1,3},{16,18},{17,19},{2,0},{3,1},{18,16},{19,17},{4,6},{5,7... | collective-permute-start | bytes 196616 | tf_op jit(solution)/shard_map/ppermute | solution.py:55
  261.2 22.9 %collective-permute-start.29 = (bf16[32,8,128]{2,1,0:T(8,128)(2,1)}, bf16[32,8,128]{2,1,0:T(8,128)(2,1)}, u32[]{:S(2)}, u32[]{:S(2)}) collective-permute-start(bf16[32,8,128]{2,1,0:T(8,128)(2,1)} %get-tuple-element.240), channel_id=1, source_target_pairs={{0,18},{1,19},{16,0},{17,1},{2,16},{3,17},{18,2},{19,3},{4,22},{5,... | collective-permute-start | bytes 196616 | tf_op jit(solution)/shard_map/ppermute | solution.py:55
  292.9 12.1 %collective-permute-start.37 = (bf16[128,1024]{1,0:T(8,128)(2,1)}, bf16[128,1024]{1,0:T(8,128)(2,1)S(1)}, u32[]{:S(2)}, u32[]{:S(2)}) collective-permute-start(bf16[128,1024]{1,0:T(8,128)(2,1)} %fusion.6), channel_id=1, source_target_pairs={{0,0},{1,16},{16,1},{17,17},{2,2},{3,18},{18,3},{19,19},{4,4},{5,2... | collective-permute-start | bytes 786440 | tf_op jit(solution)/shard_map/ppermute | solution.py:55
  305.1 15.7 %collective-permute-start.41 = (bf16[16,576,128]{2,1,0:T(8,128)(2,1)S(1)}, bf16[16,576,128]{2,1,0:T(8,128)(2,1)S(1)}, u32[]{:S(2)}, u32[]{:S(2)}) collective-permute-start(bf16[16,576,128]{2,1,0:T(8,128)(2,1)S(1)} %all-to-all-done.7.mine_ref), channel_id=1, source_target_pairs={{0,1},{1,0},{16,17},{17,16},{2,3},{3,2},{18,19},{19,18},{4,5},{5,4... | collective-permute-start | bytes 7077896 | tf_op jit(solution)/shard_map/ppermute | solution.py:55
  310.6 10.1 %collective-permute-start.40 = (bf16[4,160,128]{2,1,0:T(8,128)(2,1)S(1)}, bf16[4,160,128]{2,1,0:T(8,128)(2,1)S(1)}, u32[]{:S(2)}, u32[]{:S(2)}) collective-permute-start(bf16[4,160,128]{2,1,0:T(8,128)(2,1)S(1)} %pad_maximum_fusion.4), channel_id=1, source_target_pairs={{0,4},{1,5},{16,20},{17,21},{2,6},{3,7},{18,22},{19,23},{4,8},{5,9... | collective-permute-start | bytes 491528 | tf_op jit(solution)/shard_map/ppermute | solution.py:55
  (45 other events, 364.7 us)
Sparse Core Ops, SparseCore 0:
  86.7 22.6 all-gather.1
  192.2 29.9 reduce-scatter.1

commit v6 on v5

--- a/solution.py
+++ b/solution.py
@@ -120,8 +120,17 @@
     return exchange(by_row.reshape(4, 2, *by_row.shape[1:]), x_rings)
 
 
-def return_planes(got, by_block):
-    both = [cat([got[:, parity].reshape(-1, 128), by_block.reshape(-1, 128)]) for parity in range(2)]
+def halve_block(by_block, core):
+    halves = by_block.reshape(2, 18, 8, 128)
+    mine, got = pick(halves, core, 0), send(pick(halves, 1 - core, 0), other_core)
+    return [jnp.where(core == at, mine, got) for at in range(2)]
+
+
+def return_planes(got, blocks):
+    both = [
+        cat([got[:, parity].reshape(-1, 128), blocks[parity].reshape(-1, 128)])
+        for parity in range(2)
+    ]
     both = jnp.stack(both)
     return exchange(
         jnp.broadcast_to(both[None], (8, *both.shape)).reshape(16, *both.shape[1:]), planes
@@ -579,14 +588,13 @@
 
 
 def feed_grads_kernel(spot_ref, mine_ref, other_ref, gate_ref, up_ref, down_ref):
-    core, z_low = spot_ref[0], spot_ref[1]
-    home = core == z_low
+    core = spot_ref[0]
     for at in range(16):
         mine = mine_ref[at].astype(f32)
         other = other_ref[at].astype(f32)
-        first = jnp.where(core == 0, mine[:288], other[:288])
-        second = jnp.where(core == 0, other[:288], mine[:288])
-        block = jnp.where(home, mine[288:], other[288:])
+        first = jnp.where(core == 0, mine, other)
+        second = jnp.where(core == 0, other, mine)
+        block = jnp.concatenate([first[288:], second[288:]], axis=0)
         rows = slice(at * 8, at * 8 + 8)
         for x in range(4):
             wide = [
@@ -773,7 +781,7 @@
     pieces = [pick(attention_parts, (y + step) % 4, 0) for step in range(4)]
     ring = send_ring(pieces, y_up, y_down, y_far)
     feed_got = exchange_rows(add_up(feed_parts).astype(bf16).reshape(8, 9, 8, 128))
-    down_rows = add_up(down_parts).astype(bf16)
+    down_rows = halve_block(add_up(down_parts).astype(bf16), core)
     first, parts, ring, feed_got, down_rows = join(first, parts, ring, feed_got, down_rows)
 
     first_grad = first + add_up(jnp.stack(parts))
@@ -788,12 +796,9 @@
 
     rows = (pieces[0] + add_up(jnp.stack(ring))).astype(bf16)
     attention_got = exchange_x(rows[:24].reshape(8, 3, 8, 128), x)
-    result = send(result, regroup)
-    attention_got, result = join(attention_got, result)
-    input_grad = send(input_grad, regroup)
-    block, input_grad, feed_mine = join(
-        gather_z(attention_got, rows[24:], z_low), input_grad, feed_mine
-    )
+    ends = send(jnp.stack([result, input_grad]), regroup)
+    attention_got, ends = join(attention_got, ends)
+    block, feed_mine = join(gather_z(attention_got, rows[24:], z_low), feed_mine)
     mine = gather_y(block)
     gate_sum, up_sum, down_sum = feed_grads(feed_mine, send(feed_mine, other_core), where)
     mine, gate_sum, up_sum, down_sum = join(mine, gate_sum, up_sum, down_sum)
@@ -801,8 +806,8 @@
         mine, send(mine, other_core), where
     )
     return (
-        result[None],
-        input_grad.astype(f32)[None],
+        ends[:1],
+        ends[1:].astype(f32),
         gain_sums[:, 0],
         query_sum,
         key_sum,

time: 343 us -> 340 us (level)
  waiting for transfers between devices: 102 us -> 95.2 us
    ppermute x43, waiting for transfers between devices: 84.5 us -> 77 us  [send(): return lax.ppermute(values, AXES, moves)]
where the time goes in v6:
time: 340 us; the launch traced here: 335 us
  starting transfers between devices  100 us (29%)
  waiting for transfers between devices  95.2 us (28%)
  Pallas kernels  58.5 us (17%)
  other arithmetic  31.7 us (9%)
  local copies, waits for them, and re-layouts  21.9 us (6%)
  between operations  14.9 us (4%)
  matrix products  12.8 us (4%)
    ppermute x43, waiting for transfers between devices, send(): return lax.ppermute(values, AXES, moves)  77 us
    ppermute x43, starting transfers between devices, send(): return lax.ppermute(values, AXES, moves)  63.7 us
    pallas_call x6, Pallas kernels, call(): pl.pallas_call(kernel, out_shape=[jax.ShapeDtypeStruct(shape, kind) for s...  56.8 us
    all_to_all x8, starting transfers between devices, exchange(): return lax.all_to_all(values, AXES, 0, 0, axis_index_groups=groups)  36.4 us
    all_to_all x8, waiting for transfers between devices, exchange(): return lax.all_to_all(values, AXES, 0, 0, axis_index_groups=groups)  14.9 us
  transfers between devices with their start and end apart: 53, of which 28 were waited for; matrix products, arithmetic and copies ran while one was open for 16% of the time, Pallas kernels for 10%

profile of v6, /device:TPU:1, one launch (start us, length us, event | category | flops | bytes accessed | tf_op | source)
XLA Modules:
  0.0 335.3 jit_solution(2392874309650387059)
XLA Ops:
  12.9 3.5 %collective-permute-start = (bf16[144,1024]{1,0:T(8,128)(2,1)}, bf16[144,1024]{1,0:T(8,128)(2,1)S(1)}, u32[]{:S(2)}, u32[]{:S(2)}) collective-permute-start(bf16[144,1024]{1,0:T(8,128)(2,1)} %shard_map.246), channel_id=1, source_target_pairs={{0,0},{1,16},{16,1},{17,17},{2,2},{3,18},{18,3},{19,19},{4,4},{5,2... | collective-permute-start | bytes 884744 | tf_op jit(solution)/shard_map/ppermute | solution.py:55
  17.8 3.3 collective-permute-done.packed_ref
  21.9 4.5 %shard_map.247 = (bf16[4,144,1280]{2,1,0:T(8,128)(2,1)}, bf16[4,128,1152]{2,1,0:T(8,128)(2,1)}) custom-call(s32[1]{0:T(128)} %bitcast.1.spot_ref, bf16[128,1024]{1,0:T(8,128)(2,1)} %q_ref.1, bf16[128,512]{1,0:T(8,128)(2,1)} %k_ref.1, bf16[128,512]{1,0:T(8,128)(2,1)} %v_ref.1, bf16[128,4608]{1,0:T(8,128)(2,1)} %gate_ref.1, bf16[128,4608]{1,0:T(8,128)(2,1)} %up_ref.1, ...), custom_call_target="tpu_custom_call" | custom-call | bytes 3178496 | tf_op jit(solution)/shard_map/pallas_call | solution.py:188
  26.4 4.5 %all-to-all-start = ((bf16[4,144,1280]{2,1,0:T(8,128)(2,1)}), bf16[4,144,1280]{2,1,0:T(8,128)(2,1)}, u32[]{:S(2)}, u32[]{:S(2)}) async-start(bf16[4,144,1280]{2,1,0:T(8,128)(2,1)} %get-tuple-element.117), calls=%async_computation | async-start | bytes 2949120 | tf_op jit(solution)/shard_map/all_to_all | solution.py:89
  34.6 3.5 %collective-permute-start.2 = (bf16[128,1024]{1,0:T(8,128)(2,1)S(1)}, bf16[128,1024]{1,0:T(8,128)(2,1)S(1)}, u32[]{:S(2)}, u32[]{:S(2)}) collective-permute-start(bf16[128,1024]{1,0:T(8,128)(2,1)S(1)} %bitcast.171), channel_id=1, source_target_pairs={{0,0},{1,16},{16,1},{17,17},{2,2},{3,18},{18,3},{19,19},{4,4},{5,2... | collective-permute-start | bytes 786440 | tf_op jit(solution)/shard_map/ppermute | solution.py:55
  38.2 3.1 fusion.7
  42.3 3.8 %all-to-all-done.half_ref = bf16[4,144,1280]{2,1,0:T(8,128)(2,1)} async-done(((bf16[4,144,1280]{2,1,0:T(8,128)(2,1)}), bf16[4,144,1280]{2,1,0:T(8,128)(2,1)}, u32[]{:S(2)}, u32[]{:S(2)}) %all-to-all-start) | async-done | bytes 1474592 | tf_op jit(solution)/shard_map/all_to_all | solution.py:89
  51.3 3.7 %all-to-all-start.1 = ((bf16[4,128,1152]{2,1,0:T(8,128)(2,1)}), bf16[4,128,1152]{2,1,0:T(8,128)(2,1)S(1)}, u32[]{:S(2)}, u32[]{:S(2)}) async-start(bf16[4,128,1152]{2,1,0:T(8,128)(2,1)} %get-tuple-element.133), calls=%async_computation.1 | async-start | bytes 2359296 | tf_op jit(solution)/shard_map/all_to_all | solution.py:89
  59.5 13.1 %shard_map.248 = (bf16[1024,256]{1,0:T(8,128)(2,1)}, bf16[1024,1024]{1,0:T(8,128)(2,1)}, bf16[1024,256]{1,0:T(8,128)(2,1)}, f32[1024,256]{1,0:T(8,128)}, f32[102...) custom-call(s32[2]{0:T(128)} %pad_add_fusion.1.spot_ref, ...), custom_call_target="tpu_custom_call" | custom-call | flops 2147483648 | bytes 4273152 | tf_op jit(solution)/shard_map/pallas_call | solution.py:188
  79.2 3.5 %all-to-all-start.2 = ((bf16[4,128,1024]{2,1,0:T(8,128)(2,1)}), bf16[4,128,1024]{2,1,0:T(8,128)(2,1)S(1)}, u32[]{:S(2)}, u32[]{:S(2)}) async-start(bf16[4,128,1024]{2,1,0:T(8,128)(2,1)} %bitcast.117), calls=%async_computation.2 | async-start | bytes 2097152 | tf_op jit(solution)/shard_map/all_to_all | solution.py:89
  87.4 12.6 %collective-permute-done.7.lower_ref = bf16[2,128,1152]{2,1,0:T(8,128)(2,1)} collective-permute-done((bf16[2,128,1152]{2,1,0:T(8,128)(2,1)}, bf16[2,128,1152]{2,1,0:T(8,128)(2,1)}, u32[]{:S(2)}, u32[]{:S(2)}) %collective-permute-start.7) | collective-permute-done | bytes 589856 | tf_op jit(solution)/shard_map/ppermute | solution.py:55
  102.9 3.8 %all-to-all-start.3 = ((bf16[4,128,1024]{2,1,0:T(8,128)(2,1)}), bf16[4,128,1024]{2,1,0:T(8,128)(2,1)S(1)}, u32[]{:S(2)}, u32[]{:S(2)}) async-start(bf16[4,128,1024]{2,1,0:T(8,128)(2,1)} %broadcast_in_dim.75), calls=%async_computation.3 | async-start | bytes 2097152 | tf_op jit(solution)/shard_map/all_to_all | solution.py:89
  109.5 7.0 %all-to-all-done.3 = bf16[4,128,1024]{2,1,0:T(8,128)(2,1)S(1)} async-done(((bf16[4,128,1024]{2,1,0:T(8,128)(2,1)}), bf16[4,128,1024]{2,1,0:T(8,128)(2,1)S(1)}, u32[]{:S(2)}, u32[]{:S(2)}) %all-to-all-start.3) | async-done | bytes 1048608 | tf_op jit(solution)/shard_map/all_to_all | solution.py:89
  117.4 6.6 %collective-permute-start.10 = (bf16[512,1024]{1,0:T(8,128)(2,1)S(1)}, bf16[512,1024]{1,0:T(8,128)(2,1)}, u32[]{:S(2)}, u32[]{:S(2)}) collective-permute-start(bf16[512,1024]{1,0:T(8,128)(2,1)S(1)} %bitcast.120), channel_id=1, source_target_pairs={{0,1},{1,0},{16,17},{17,16},{2,3},{3,2},{18,19},{19,18},{4,5},{5,4... | collective-permute-start | bytes 3145736 | tf_op jit(solution)/shard_map/ppermute | solution.py:55
  128.2 15.2 %shard_map.249 = (bf16[512,1024]{1,0:T(8,128)(2,1)}, bf16[512,1024]{1,0:T(8,128)(2,1)}, bf16[1024,576]{1,0:T(8,128)(2,1)}, bf16[1024,1152]{1,0:T(8,128)(2,1)}, b...) custom-call(s32[3]{0:T(128)} %pad_add_fusion.2.spot_ref, bf16[512,1024]{1,0:T(8,128)(2,1)} %bitcast.121, ...), custom_call_target="tpu_custom_call" | custom-call | flops 6442450944 | bytes 7733248 | tf_op jit(solution)/shard_map/pallas_call | solution.py:188
  150.8 4.6 %convolution_convert_fusion = bf16[1024,1152]{1,0:T(8,128)(2,1)S(1)} fusion(bf16[1024,1024]{1,0:T(8,128)(2,1)} %get-tuple-element.154, bf16[1024,1152]{1,0:T(8,128)(2,1)S(1)} %copy-done.21), kind=kOutput, calls=%fused_computation | convolution fusion | flops 2417098752 | bytes 6815744 | tf_op jit(solution)/shard_map/dot_general | solution.py:216
  162.7 6.2 %all-to-all-start.4 = ((bf16[16,36,8,128]{3,2,1,0:T(8,128)(2,1)}), bf16[16,36,8,128]{3,2,1,0:T(8,128)(2,1)S(1)}, u32[]{:S(2)}, u32[]{:S(2)}) async-start(bf16[16,36,8,128]{3,2,1,0:T(8,128)(2,1)} %bitcast.26), calls=%async_computation.4 | async-start | bytes 2359296 | tf_op jit(solution)/shard_map/all_to_all | solution.py:89
  174.3 3.1 convolution_convert_fusion.1
  181.9 6.6 %collective-permute-done.18 = bf16[128,1024]{1,0:T(8,128)(2,1)S(1)} collective-permute-done((bf16[128,1024]{1,0:T(8,128)(2,1)S(1)}, bf16[128,1024]{1,0:T(8,128)(2,1)S(1)}, u32[]{:S(2)}, u32[]{:S(2)}) %collective-permute-start.18) | collective-permute-done | bytes 262176 | tf_op jit(solution)/shard_map/ppermute | solution.py:55
  192.3 6.7 %all-to-all-start.5 = ((bf16[16,72,8,128]{3,2,1,0:T(8,128)(2,1)}), bf16[16,72,8,128]{3,2,1,0:T(8,128)(2,1)S(1)}, u32[]{:S(2)}, u32[]{:S(2)}) async-start(bf16[16,72,8,128]{3,2,1,0:T(8,128)(2,1)} %bitcast.23), calls=%async_computation.5 | async-start | bytes 4718592 | tf_op jit(solution)/shard_map/all_to_all | solution.py:89
  199.7 17.8 %shard_map.250 = (bf16[512,1024]{1,0:T(8,128)(2,1)}, bf16[512,1024]{1,0:T(8,128)(2,1)}, f32[4,4,32,8,128]{4,3,2,1,0:T(8,128)}) custom-call(s32[1]{0:T(128)} %bitcast.spot_ref, bf16[512,1024]{1,0:T(8,128)(2,1)} %constant_dynamic-update-slice_fusion.near_ref, bf16[512,1024]{1,0:T(8,128)(2,1)} %collective-permute-done.19.far_ref, bf16[128,1024]{1,0:T(8,128)(2,1)} %copy-done.5, ...), custom_call_target="tpu_custom_call" | custom-call | flops 4294967296 | bytes 9028608 | tf_op jit(solution)/shard_map/pallas_call | solution.py:188
  234.9 4.2 %collective-permute-done.24 = bf16[4,32,8,128]{3,2,1,0:T(8,128)(2,1)} collective-permute-done((bf16[4,32,8,128]{3,2,1,0:T(8,128)(2,1)}, bf16[4,32,8,128]{3,2,1,0:T(8,128)(2,1)}, u32[]{:S(2)}, u32[]{:S(2)}) %collective-permute-start.24) | collective-permute-done | bytes 262176 | tf_op jit(solution)/shard_map/ppermute | solution.py:55
  240.7 3.3 all-to-all-start.6
  244.8 4.1 %all-to-all-done.6 = bf16[4,2,9,8,128]{4,3,2,1,0:T(8,128)(2,1)S(1)} async-done(((bf16[4,2,9,8,128]{4,3,2,1,0:T(8,128)(2,1)}), bf16[4,2,9,8,128]{4,3,2,1,0:T(8,128)(2,1)S(1)}, u32[]{:S(2)}, u32[]{:S(2)}) %all-to-all-start.6) | async-done | bytes 147488 | tf_op jit(solution)/shard_map/all_to_all | solution.py:89
  250.5 4.7 %all-to-all-start.7 = ((bf16[16,432,128]{2,1,0:T(8,128)(2,1)}), bf16[16,432,128]{2,1,0:T(8,128)(2,1)S(1)}, u32[]{:S(2)}, u32[]{:S(2)}) async-start(bf16[16,432,128]{2,1,0:T(8,128)(2,1)} %bitcast.116), calls=%async_computation.8 | async-start | bytes 3538944 | tf_op jit(solution)/shard_map/all_to_all | solution.py:89
  266.8 12.5 %collective-permute-done.28 = bf16[32,8,128]{2,1,0:T(8,128)(2,1)S(1)} collective-permute-done((bf16[32,8,128]{2,1,0:T(8,128)(2,1)}, bf16[32,8,128]{2,1,0:T(8,128)(2,1)S(1)}, u32[]{:S(2)}, u32[]{:S(2)}) %collective-permute-start.28) | collective-permute-done | bytes 65568 | tf_op jit(solution)/shard_map/ppermute | solution.py:55
  289.6 3.4 %collective-permute-done.32 = bf16[2,3,8,128]{3,2,1,0:T(8,128)(2,1)S(1)} collective-permute-done((bf16[2,3,8,128]{3,2,1,0:T(8,128)(2,1)S(1)}, bf16[2,3,8,128]{3,2,1,0:T(8,128)(2,1)S(1)}, u32[]{:S(2)}, u32[]{:S(2)}) %collective-permute-start.32) | collective-permute-done | bytes 12320 | tf_op jit(solution)/shard_map/ppermute | solution.py:55
  293.2 3.8 %collective-permute-start.36 = (bf16[160,128]{1,0:T(8,128)(2,1)S(1)}, bf16[160,128]{1,0:T(8,128)(2,1)S(1)}, u32[]{:S(2)}, u32[]{:S(2)}) collective-permute-start(bf16[160,128]{1,0:T(8,128)(2,1)S(1)} %get-tuple-element.259), channel_id=1, source_target_pairs={{0,2},{1,3},{16,18},{17,19},{2,0},{3,1},{18,16},{19,17},{4,6},{5,7... | collective-permute-start | bytes 122888 | tf_op jit(solution)/shard_map/ppermute | solution.py:55
  303.5 3.9 %collective-permute-start.38 = (bf16[4,160,128]{2,1,0:T(8,128)(2,1)S(1)}, bf16[4,160,128]{2,1,0:T(8,128)(2,1)S(1)}, u32[]{:S(2)}, u32[]{:S(2)}) collective-permute-start(bf16[4,160,128]{2,1,0:T(8,128)(2,1)S(1)} %pad_maximum_fusion.3), channel_id=1, source_target_pairs={{0,12},{1,13},{16,28},{17,29},{2,14},{3,15},{18,30},{19,31},{4,0},... | collective-permute-start | bytes 491528 | tf_op jit(solution)/shard_map/ppermute | solution.py:55
  308.0 6.5 %collective-permute-done.38 = bf16[4,160,128]{2,1,0:T(8,128)(2,1)S(1)} collective-permute-done((bf16[4,160,128]{2,1,0:T(8,128)(2,1)S(1)}, bf16[4,160,128]{2,1,0:T(8,128)(2,1)S(1)}, u32[]{:S(2)}, u32[]{:S(2)}) %collective-permute-start.38) | collective-permute-done | bytes 163872 | tf_op jit(solution)/shard_map/ppermute | solution.py:55
  314.6 3.4 %collective-permute-done.40 = bf16[4,160,128]{2,1,0:T(8,128)(2,1)S(1)} collective-permute-done((bf16[4,160,128]{2,1,0:T(8,128)(2,1)S(1)}, bf16[4,160,128]{2,1,0:T(8,128)(2,1)S(1)}, u32[]{:S(2)}, u32[]{:S(2)}) %collective-permute-start.40) | collective-permute-done | bytes 163872 | tf_op jit(solution)/shard_map/ppermute | solution.py:55
  318.1 4.1 %shard_map.251 = (f32[128,4608]{1,0:T(8,128)}, f32[128,4608]{1,0:T(8,128)}, f32[576,1024]{1,0:T(8,128)}) custom-call(s32[2]{0:T(128)S(1)} %pad_add_fusion.3.spot_ref, bf16[16,432,128]{2,1,0:T(8,128)(2,1)S(1)} %all-to-all-done.7.mine_ref, bf16[16,432,128]{2,1,0:T(8,128)(2,1)S(1)} %collective-permute-done.41.other_ref), custom_call_target="tpu_custom_call" | custom-call | bytes 3538944 | tf_op jit(solution)/shard_map/pallas_call | solution.py:188
  (213 shorter events, 129.9 us)
Async XLA Ops:
  26.4 19.7 %all-to-all-start = ((bf16[4,144,1280]{2,1,0:T(8,128)(2,1)}), bf16[4,144,1280]{2,1,0:T(8,128)(2,1)}, u32[]{:S(2)}, u32[]{:S(2)}) async-start(bf16[4,144,1280]{2,1,0:T(8,128)(2,1)} %get-tuple-element.117), calls=%async_computation | async-start | bytes 2949120 | tf_op jit(solution)/shard_map/all_to_all | solution.py:89
  46.1 11.7 %collective-permute-start.4 = (bf16[4,144,1280]{2,1,0:T(8,128)(2,1)}, bf16[4,144,1280]{2,1,0:T(8,128)(2,1)}, u32[]{:S(2)}, u32[]{:S(2)}) collective-permute-start(bf16[4,144,1280]{2,1,0:T(8,128)(2,1)} %all-to-all-done.half_ref), channel_id=1, source_target_pairs={{0,1},{1,0},{16,17},{17,16},{2,3},{3,2},{18,19},{19,18},{4,5},{5,4... | collective-permute-start | bytes 4423688 | tf_op jit(solution)/shard_map/ppermute | solution.py:55
  47.1 10.7 %collective-permute-start.5 = (bf16[4,128,256]{2,1,0:T(8,128)(2,1)S(1)}, bf16[4,128,256]{2,1,0:T(8,128)(2,1)S(1)}, u32[]{:S(2)}, u32[]{:S(2)}) collective-permute-start(bf16[4,128,256]{2,1,0:T(8,128)(2,1)S(1)} %slice.128), channel_id=1, source_target_pairs={{0,16},{1,17},{16,2},{17,3},{2,18},{3,19},{18,0},{19,1},{4,20},{5,... | collective-permute-start | bytes 786440 | tf_op jit(solution)/shard_map/ppermute | solution.py:55
  51.3 22.6 %all-to-all-start.1 = ((bf16[4,128,1152]{2,1,0:T(8,128)(2,1)}), bf16[4,128,1152]{2,1,0:T(8,128)(2,1)S(1)}, u32[]{:S(2)}, u32[]{:S(2)}) async-start(bf16[4,128,1152]{2,1,0:T(8,128)(2,1)} %get-tuple-element.133), calls=%async_computation.1 | async-start | bytes 2359296 | tf_op jit(solution)/shard_map/all_to_all | solution.py:89
  79.2 20.8 %all-to-all-start.2 = ((bf16[4,128,1024]{2,1,0:T(8,128)(2,1)}), bf16[4,128,1024]{2,1,0:T(8,128)(2,1)S(1)}, u32[]{:S(2)}, u32[]{:S(2)}) async-start(bf16[4,128,1024]{2,1,0:T(8,128)(2,1)} %bitcast.117), calls=%async_computation.2 | async-start | bytes 2097152 | tf_op jit(solution)/shard_map/all_to_all | solution.py:89
  82.7 26.7 %all-gather.2.cloned.1.call-start = ((), (), s32[]{:S(2)}) async-start(), calls=%async_computation.9 | async-start | bytes 1310720 | tf_op jit(solution)/shard_map/all_gather | solution.py:707
  83.9 16.1 %collective-permute-start.7 = (bf16[2,128,1152]{2,1,0:T(8,128)(2,1)}, bf16[2,128,1152]{2,1,0:T(8,128)(2,1)}, u32[]{:S(2)}, u32[]{:S(2)}) collective-permute-start(bf16[2,128,1152]{2,1,0:T(8,128)(2,1)} %get-tuple-element.239), channel_id=1, source_target_pairs={{0,16},{1,17},{16,2},{17,3},{2,18},{3,19},{18,0},{19,1},{4,20},{5,... | collective-permute-start | bytes 1769480 | tf_op jit(solution)/shard_map/ppermute | solution.py:55
  83.9 16.1 %collective-permute-start.8 = (bf16[2,128,1152]{2,1,0:T(8,128)(2,1)}, bf16[2,128,1152]{2,1,0:T(8,128)(2,1)}, u32[]{:S(2)}, u32[]{:S(2)}) collective-permute-start(bf16[2,128,1152]{2,1,0:T(8,128)(2,1)} %get-tuple-element.238), channel_id=1, source_target_pairs={{0,18},{1,19},{16,0},{17,1},{2,16},{3,17},{18,2},{19,3},{4,22},{5,... | collective-permute-start | bytes 1769480 | tf_op jit(solution)/shard_map/ppermute | solution.py:55
  100.2 17.2 %collective-permute-start.9 = (bf16[576,1024]{1,0:T(8,128)(2,1)S(1)}, bf16[576,1024]{1,0:T(8,128)(2,1)}, u32[]{:S(2)}, u32[]{:S(2)}) collective-permute-start(bf16[576,1024]{1,0:T(8,128)(2,1)S(1)} %copy-done.8), channel_id=1, source_target_pairs={{0,18},{17,1},{2,16},{19,3},{4,22},{21,5},{6,20},{23,7},{8,26},{25... | collective-permute-start | bytes 3538952 | tf_op jit(solution)/shard_map/ppermute | solution.py:55
  102.9 13.6 %all-to-all-start.3 = ((bf16[4,128,1024]{2,1,0:T(8,128)(2,1)}), bf16[4,128,1024]{2,1,0:T(8,128)(2,1)S(1)}, u32[]{:S(2)}, u32[]{:S(2)}) async-start(bf16[4,128,1024]{2,1,0:T(8,128)(2,1)} %broadcast_in_dim.75), calls=%async_computation.3 | async-start | bytes 2097152 | tf_op jit(solution)/shard_map/all_to_all | solution.py:89
  117.4 10.2 %collective-permute-start.10 = (bf16[512,1024]{1,0:T(8,128)(2,1)S(1)}, bf16[512,1024]{1,0:T(8,128)(2,1)}, u32[]{:S(2)}, u32[]{:S(2)}) collective-permute-start(bf16[512,1024]{1,0:T(8,128)(2,1)S(1)} %bitcast.120), channel_id=1, source_target_pairs={{0,1},{1,0},{16,17},{17,16},{2,3},{3,2},{18,19},{19,18},{4,5},{5,4... | collective-permute-start | bytes 3145736 | tf_op jit(solution)/shard_map/ppermute | solution.py:55
  147.9 11.8 %collective-permute-start.13 = (bf16[128,1024]{1,0:T(8,128)(2,1)S(1)}, bf16[128,1024]{1,0:T(8,128)(2,1)S(1)}, u32[]{:S(2)}, u32[]{:S(2)}) collective-permute-start(bf16[128,1024]{1,0:T(8,128)(2,1)S(1)} %get-tuple-element.151), channel_id=1, source_target_pairs={{0,32},{1,33},{16,48},{17,49},{2,34},{3,35},{18,50},{19,51},{4,36}... | collective-permute-start | bytes 786440 | tf_op jit(solution)/shard_map/ppermute | solution.py:55
  148.3 13.5 %collective-permute-start.14 = (bf16[128,1024]{1,0:T(8,128)(2,1)S(1)}, bf16[128,1024]{1,0:T(8,128)(2,1)S(1)}, u32[]{:S(2)}, u32[]{:S(2)}) collective-permute-start(bf16[128,1024]{1,0:T(8,128)(2,1)S(1)} %get-tuple-element.152), channel_id=1, source_target_pairs={{0,64},{1,65},{16,80},{17,81},{2,66},{3,67},{18,82},{19,83},{4,68}... | collective-permute-start | bytes 786440 | tf_op jit(solution)/shard_map/ppermute | solution.py:55
  150.1 12.6 %collective-permute-start.15 = (bf16[128,1024]{1,0:T(8,128)(2,1)S(1)}, bf16[128,1024]{1,0:T(8,128)(2,1)S(1)}, u32[]{:S(2)}, u32[]{:S(2)}) collective-permute-start(bf16[128,1024]{1,0:T(8,128)(2,1)S(1)} %get-tuple-element.153), channel_id=1, source_target_pairs={{0,96},{1,97},{16,112},{17,113},{2,98},{3,99},{18,114},{19,115},{4... | collective-permute-start | bytes 786440 | tf_op jit(solution)/shard_map/ppermute | solution.py:55
  162.7 25.8 %all-to-all-start.4 = ((bf16[16,36,8,128]{3,2,1,0:T(8,128)(2,1)}), bf16[16,36,8,128]{3,2,1,0:T(8,128)(2,1)S(1)}, u32[]{:S(2)}, u32[]{:S(2)}) async-start(bf16[16,36,8,128]{3,2,1,0:T(8,128)(2,1)} %bitcast.26), calls=%async_computation.4 | async-start | bytes 2359296 | tf_op jit(solution)/shard_map/all_to_all | solution.py:89
  173.7 14.7 %collective-permute-start.18 = (bf16[128,1024]{1,0:T(8,128)(2,1)S(1)}, bf16[128,1024]{1,0:T(8,128)(2,1)S(1)}, u32[]{:S(2)}, u32[]{:S(2)}) collective-permute-start(bf16[128,1024]{1,0:T(8,128)(2,1)S(1)} %get-tuple-element.165), channel_id=1, source_target_pairs={{0,32},{1,33},{16,48},{17,49},{2,34},{3,35},{18,50},{19,51},{4,36}... | collective-permute-start | bytes 786440 | tf_op jit(solution)/shard_map/ppermute | solution.py:55
  192.3 47.4 %all-to-all-start.5 = ((bf16[16,72,8,128]{3,2,1,0:T(8,128)(2,1)}), bf16[16,72,8,128]{3,2,1,0:T(8,128)(2,1)S(1)}, u32[]{:S(2)}, u32[]{:S(2)}) async-start(bf16[16,72,8,128]{3,2,1,0:T(8,128)(2,1)} %bitcast.23), calls=%async_computation.5 | async-start | bytes 4718592 | tf_op jit(solution)/shard_map/all_to_all | solution.py:89
  199.0 66.8 %reduce-scatter.2.cloned.1.call-start = ((), (), s32[]{:S(2)}) async-start(), calls=%async_computation.10 | async-start | bytes 2359296 | tf_op jit(solution)/shard_map/reduce_scatter | solution.py:763
  225.6 13.4 %collective-permute-start.24 = (bf16[4,32,8,128]{3,2,1,0:T(8,128)(2,1)}, bf16[4,32,8,128]{3,2,1,0:T(8,128)(2,1)}, u32[]{:S(2)}, u32[]{:S(2)}) collective-permute-start(bf16[4,32,8,128]{3,2,1,0:T(8,128)(2,1)} %get-tuple-element.229), channel_id=1, source_target_pairs={{0,4},{1,5},{16,20},{17,21},{2,6},{3,7},{18,22},{19,23},{4,8},{5,9... | collective-permute-start | bytes 786440 | tf_op jit(solution)/shard_map/ppermute | solution.py:55
  229.5 19.5 %collective-permute-start.25 = (bf16[4,32,8,128]{3,2,1,0:T(8,128)(2,1)}, bf16[4,32,8,128]{3,2,1,0:T(8,128)(2,1)}, u32[]{:S(2)}, u32[]{:S(2)}) collective-permute-start(bf16[4,32,8,128]{3,2,1,0:T(8,128)(2,1)} %get-tuple-element.228), channel_id=1, source_target_pairs={{0,8},{1,9},{16,24},{17,25},{2,10},{3,11},{18,26},{19,27},{4,12},{... | collective-permute-start | bytes 786440 | tf_op jit(solution)/shard_map/ppermute | solution.py:55
  231.9 17.1 %collective-permute-start.26 = (bf16[4,32,8,128]{3,2,1,0:T(8,128)(2,1)}, bf16[4,32,8,128]{3,2,1,0:T(8,128)(2,1)}, u32[]{:S(2)}, u32[]{:S(2)}) collective-permute-start(bf16[4,32,8,128]{3,2,1,0:T(8,128)(2,1)} %get-tuple-element.227), channel_id=1, source_target_pairs={{0,12},{1,13},{16,28},{17,29},{2,14},{3,15},{18,30},{19,31},{4,0},... | collective-permute-start | bytes 786440 | tf_op jit(solution)/shard_map/ppermute | solution.py:55
  233.0 15.9 %collective-permute-start.21 = (bf16[128,1024]{1,0:T(8,128)(2,1)}, bf16[128,1024]{1,0:T(8,128)(2,1)}, u32[]{:S(2)}, u32[]{:S(2)}) collective-permute-start(bf16[128,1024]{1,0:T(8,128)(2,1)} %get-tuple-element.180), channel_id=1, source_target_pairs={{0,32},{1,33},{16,48},{17,49},{2,34},{3,35},{18,50},{19,51},{4,36}... | collective-permute-start | bytes 786440 | tf_op jit(solution)/shard_map/ppermute | solution.py:55
  233.0 15.9 %collective-permute-start.22 = (bf16[128,1024]{1,0:T(8,128)(2,1)}, bf16[128,1024]{1,0:T(8,128)(2,1)}, u32[]{:S(2)}, u32[]{:S(2)}) collective-permute-start(bf16[128,1024]{1,0:T(8,128)(2,1)} %get-tuple-element.181), channel_id=1, source_target_pairs={{0,64},{1,65},{16,80},{17,81},{2,66},{3,67},{18,82},{19,83},{4,68}... | collective-permute-start | bytes 786440 | tf_op jit(solution)/shard_map/ppermute | solution.py:55
  239.1 9.9 %collective-permute-start.23 = (bf16[128,1024]{1,0:T(8,128)(2,1)}, bf16[128,1024]{1,0:T(8,128)(2,1)}, u32[]{:S(2)}, u32[]{:S(2)}) collective-permute-start(bf16[128,1024]{1,0:T(8,128)(2,1)} %get-tuple-element.182), channel_id=1, source_target_pairs={{0,96},{1,97},{16,112},{17,113},{2,98},{3,99},{18,114},{19,115},{4... | collective-permute-start | bytes 786440 | tf_op jit(solution)/shard_map/ppermute | solution.py:55
  250.5 50.6 %all-to-all-start.7 = ((bf16[16,432,128]{2,1,0:T(8,128)(2,1)}), bf16[16,432,128]{2,1,0:T(8,128)(2,1)S(1)}, u32[]{:S(2)}, u32[]{:S(2)}) async-start(bf16[16,432,128]{2,1,0:T(8,128)(2,1)} %bitcast.116), calls=%async_computation.8 | async-start | bytes 3538944 | tf_op jit(solution)/shard_map/all_to_all | solution.py:89
  258.3 20.9 %collective-permute-start.28 = (bf16[32,8,128]{2,1,0:T(8,128)(2,1)}, bf16[32,8,128]{2,1,0:T(8,128)(2,1)S(1)}, u32[]{:S(2)}, u32[]{:S(2)}) collective-permute-start(bf16[32,8,128]{2,1,0:T(8,128)(2,1)} %get-tuple-element.244), channel_id=1, source_target_pairs={{0,16},{1,17},{16,2},{17,3},{2,18},{3,19},{18,0},{19,1},{4,20},{5,... | collective-permute-start | bytes 196616 | tf_op jit(solution)/shard_map/ppermute | solution.py:55
  259.7 19.6 %collective-permute-start.29 = (bf16[32,8,128]{2,1,0:T(8,128)(2,1)}, bf16[32,8,128]{2,1,0:T(8,128)(2,1)S(1)}, u32[]{:S(2)}, u32[]{:S(2)}) collective-permute-start(bf16[32,8,128]{2,1,0:T(8,128)(2,1)} %get-tuple-element.243), channel_id=1, source_target_pairs={{0,2},{1,3},{16,18},{17,19},{2,0},{3,1},{18,16},{19,17},{4,6},{5,7... | collective-permute-start | bytes 196616 | tf_op jit(solution)/shard_map/ppermute | solution.py:55
  262.1 17.3 %collective-permute-start.30 = (bf16[32,8,128]{2,1,0:T(8,128)(2,1)}, bf16[32,8,128]{2,1,0:T(8,128)(2,1)S(1)}, u32[]{:S(2)}, u32[]{:S(2)}) collective-permute-start(bf16[32,8,128]{2,1,0:T(8,128)(2,1)} %get-tuple-element.242), channel_id=1, source_target_pairs={{0,18},{1,19},{16,0},{17,1},{2,16},{3,17},{18,2},{19,3},{4,22},{5,... | collective-permute-start | bytes 196616 | tf_op jit(solution)/shard_map/ppermute | solution.py:55
  281.0 12.0 %collective-permute-start.34 = (bf16[2,128,1024]{2,1,0:T(8,128)(2,1)S(1)}, bf16[2,128,1024]{2,1,0:T(8,128)(2,1)S(1)}, u32[]{:S(2)}, u32[]{:S(2)}) collective-permute-start(bf16[2,128,1024]{2,1,0:T(8,128)(2,1)S(1)} %pad_maximum_fusion.1), channel_id=1, source_target_pairs={{0,0},{1,16},{16,1},{17,17},{2,2},{3,18},{18,3},{19,19},{4,4},{5,2... | collective-permute-start | bytes 1572872 | tf_op jit(solution)/shard_map/ppermute | solution.py:55
  301.1 17.0 %collective-permute-start.41 = (bf16[16,432,128]{2,1,0:T(8,128)(2,1)S(1)}, bf16[16,432,128]{2,1,0:T(8,128)(2,1)S(1)}, u32[]{:S(2)}, u32[]{:S(2)}) collective-permute-start(bf16[16,432,128]{2,1,0:T(8,128)(2,1)S(1)} %all-to-all-done.7.mine_ref), channel_id=1, source_target_pairs={{0,1},{1,0},{16,17},{17,16},{2,3},{3,2},{18,19},{19,18},{4,5},{5,4... | collective-permute-start | bytes 5308424 | tf_op jit(solution)/shard_map/ppermute | solution.py:55
  303.5 11.1 %collective-permute-start.38 = (bf16[4,160,128]{2,1,0:T(8,128)(2,1)S(1)}, bf16[4,160,128]{2,1,0:T(8,128)(2,1)S(1)}, u32[]{:S(2)}, u32[]{:S(2)}) collective-permute-start(bf16[4,160,128]{2,1,0:T(8,128)(2,1)S(1)} %pad_maximum_fusion.3), channel_id=1, source_target_pairs={{0,12},{1,13},{16,28},{17,29},{2,14},{3,15},{18,30},{19,31},{4,0},... | collective-permute-start | bytes 491528 | tf_op jit(solution)/shard_map/ppermute | solution.py:55
  307.4 10.6 %collective-permute-start.40 = (bf16[4,160,128]{2,1,0:T(8,128)(2,1)S(1)}, bf16[4,160,128]{2,1,0:T(8,128)(2,1)S(1)}, u32[]{:S(2)}, u32[]{:S(2)}) collective-permute-start(bf16[4,160,128]{2,1,0:T(8,128)(2,1)S(1)} %pad_maximum_fusion.3), channel_id=1, source_target_pairs={{0,4},{1,5},{16,20},{17,21},{2,6},{3,7},{18,22},{19,23},{4,8},{5,9... | collective-permute-start | bytes 491528 | tf_op jit(solution)/shard_map/ppermute | solution.py:55
  (43 other events, 334.6 us)
Sparse Core Ops, SparseCore 0:
  86.7 22.6 all-gather.1
  202.2 30.2 reduce-scatter.1

commit v7 on v6

--- a/solution.py
+++ b/solution.py
@@ -250,12 +250,15 @@
     return call(columns_kernel, spot([core]), arrays, outs, limit=58)
 
 
-def pack_kernel(tokens_ref, first_ref, second_ref, small_ref, out_ref):
+def pack_kernel(tokens_ref, first_ref, second_ref, query_ref, key_ref, out_ref):
     out_ref[:128, :] = tokens_ref[...]
     out_ref[128:, :] = jnp.zeros((16, 1024), bf16)
-    for step, ref in enumerate((first_ref, second_ref, small_ref)):
-        row = jnp.broadcast_to(ref[...].astype(f32), (16, 128)).astype(bf16)
-        out_ref[128:, step * 128 : step * 128 + 128] = row
+    low = 0
+    for ref in (first_ref, second_ref, query_ref, key_ref):
+        width = ref.shape[1]
+        row = jnp.broadcast_to(ref[...].astype(f32), (16, width)).astype(bf16)
+        out_ref[128:, low : low + width] = row
+        low += width
 
 
 def pack(*arrays):
@@ -615,7 +618,7 @@
 
 def feed_grads(mine, other, where):
     outs = [((128, 4608), f32), ((128, 4608), f32), ((576, 1024), f32)]
-    return call(feed_grads_kernel, spot(where[3:]), (mine, other), outs, (), 40)
+    return call(feed_grads_kernel, spot(where[3:]), (mine, other), outs, (), 40, 5 * 1024**3)
 
 
 def attention_grads_kernel(spot_ref, mine_ref, other_ref, q_ref, k_ref, v_ref, out_ref, extra_ref):
@@ -685,10 +688,12 @@
     y, z, core = replica // 4, (replica // 2) % 2 * 2 + z_low, replica % 2
     where = (x, y, z, core, z_low)
 
+    packed = pack(
+        tokens[0], attention_gain[None], feedforward_gain[None], query_gain[None], key_gain[None]
+    )
+    packed, token_places = join(packed, token_places)
+    packed = send(packed, regroup)
     facts = cat([token_places, jnp.broadcast_to(seq_lengths[:, :1], (1, 128))], 1)
-    small = cat([query_gain, key_gain, jnp.zeros((112,), bf16)])
-    packed = pack(tokens[0], attention_gain[None], feedforward_gain[None], small[None])
-    packed = send(packed, regroup)
     facts = jnp.where(core == z_low, facts, send(facts, other_core))
     packed_out, for_feed = pick_columns(
         query_weight, key_weight, value_weight, gate_weight, up_weight, packed, core
@@ -754,12 +759,13 @@
     middle_norm_grad, second_gain_terms = norm_back(middle, second_scale, gain_second, second_grad)
     middle_grad = upstream_own.astype(f32) + middle_norm_grad
     second_gain_grad = jnp.sum(second_gain_terms, axis=0)
-    near = gather_x(middle_grad.astype(bf16))
+    near = cat(gather_x(middle_grad.astype(bf16)))
+    far = send(near, other_core)
     result_rows = matmul(hidden, down_slot).astype(bf16)
-    near, result_rows, down_parts, feed_parts = join(near, result_rows, down_parts, feed_parts)
+    near, far, result_rows, down_parts, feed_parts = join(
+        near, far, result_rows, down_parts, feed_parts
+    )
     feed_parts = exchange(feed_parts, planes)
-    near = cat(near)
-    far = send(near, other_core)
     result_sum = lax.psum_scatter(
         result_rows, AXES, scatter_dimension=0, axis_index_groups=x_groups, tiled=True
     )

time: 340 us -> 338 us (level)
  transfers between devices with their start and end apart: 53 -> 53, of which waited for: 28 -> 31; matrix products, arithmetic and copies ran while one was open for 16% -> 15% of each run, Pallas kernels for 10% -> 9%
where the time goes in v7:
time: 338 us; the launch traced here: 333 us
  starting transfers between devices  102 us (30%)
  waiting for transfers between devices  95.6 us (28%)
  Pallas kernels  58.5 us (17%)
  other arithmetic  29.7 us (9%)
  local copies, waits for them, and re-layouts  19.9 us (6%)
  between operations  14.9 us (4%)
  matrix products  12.8 us (4%)
    ppermute x43, waiting for transfers between devices, send(): return lax.ppermute(values, AXES, moves)  76.9 us
    ppermute x43, starting transfers between devices, send(): return lax.ppermute(values, AXES, moves)  67 us
    pallas_call x6, Pallas kernels, call(): pl.pallas_call(kernel, out_shape=[jax.ShapeDtypeStruct(shape, kind) for s...  56.8 us
    all_to_all x8, starting transfers between devices, exchange(): return lax.all_to_all(values, AXES, 0, 0, axis_index_groups=groups)  34.6 us
    all_to_all x8, waiting for transfers between devices, exchange(): return lax.all_to_all(values, AXES, 0, 0, axis_index_groups=groups)  15.8 us
    dot_general x3, matrix products, matmul(): return jnp.dot(left_side, right_side, preferred_element_type=f32)  6.77 us
  transfers between devices with their start and end apart: 53, of which 31 were waited for; matrix products, arithmetic and copies ran while one was open for 15% of the time, Pallas kernels for 9%

profile of v7, /device:TPU:1, one launch (start us, length us, event | category | flops | bytes accessed | tf_op | source)
XLA Modules:
  0.0 333.3 jit_solution(5665250800408695167)
XLA Ops:
  11.7 3.5 %collective-permute-start = (bf16[144,1024]{1,0:T(8,128)(2,1)}, bf16[144,1024]{1,0:T(8,128)(2,1)S(1)}, u32[]{:S(2)}, u32[]{:S(2)}) collective-permute-start(bf16[144,1024]{1,0:T(8,128)(2,1)} %shard_map.246), channel_id=1, source_target_pairs={{0,0},{1,16},{16,1},{17,17},{2,2},{3,18},{18,3},{19,19},{4,4},{5,2... | collective-permute-start | bytes 884744 | tf_op jit(solution)/shard_map/ppermute | solution.py:55
  16.6 3.3 %collective-permute-done.packed_ref = bf16[144,1024]{1,0:T(8,128)(2,1)S(1)} collective-permute-done((bf16[144,1024]{1,0:T(8,128)(2,1)}, bf16[144,1024]{1,0:T(8,128)(2,1)S(1)}, u32[]{:S(2)}, u32[]{:S(2)}) %collective-permute-start) | collective-permute-done | bytes 294944 | tf_op jit(solution)/shard_map/ppermute | solution.py:55
  20.7 4.5 %shard_map.247 = (bf16[4,144,1280]{2,1,0:T(8,128)(2,1)}, bf16[4,128,1152]{2,1,0:T(8,128)(2,1)}) custom-call(s32[1]{0:T(128)} %bitcast.1.spot_ref, bf16[128,1024]{1,0:T(8,128)(2,1)} %q_ref.1, bf16[128,512]{1,0:T(8,128)(2,1)} %k_ref.1, bf16[128,512]{1,0:T(8,128)(2,1)} %v_ref.1, bf16[128,4608]{1,0:T(8,128)(2,1)} %gate_ref.1, bf16[128,4608]{1,0:T(8,128)(2,1)} %up_ref.1, ...), custom_call_target="tpu_custom_call" | custom-call | bytes 3178496 | tf_op jit(solution)/shard_map/pallas_call | solution.py:188
  25.2 4.5 %all-to-all-start = ((bf16[4,144,1280]{2,1,0:T(8,128)(2,1)}), bf16[4,144,1280]{2,1,0:T(8,128)(2,1)}, u32[]{:S(2)}, u32[]{:S(2)}) async-start(bf16[4,144,1280]{2,1,0:T(8,128)(2,1)} %get-tuple-element.119), calls=%async_computation | async-start | bytes 2949120 | tf_op jit(solution)/shard_map/all_to_all | solution.py:89
  33.4 3.5 %collective-permute-start.2 = (bf16[128,1024]{1,0:T(8,128)(2,1)S(1)}, bf16[128,1024]{1,0:T(8,128)(2,1)S(1)}, u32[]{:S(2)}, u32[]{:S(2)}) collective-permute-start(bf16[128,1024]{1,0:T(8,128)(2,1)S(1)} %bitcast.170), channel_id=1, source_target_pairs={{0,0},{1,16},{16,1},{17,17},{2,2},{3,18},{18,3},{19,19},{4,4},{5,2... | collective-permute-start | bytes 786440 | tf_op jit(solution)/shard_map/ppermute | solution.py:55
  37.0 3.1 fusion.7
  41.1 3.8 %all-to-all-done.half_ref = bf16[4,144,1280]{2,1,0:T(8,128)(2,1)} async-done(((bf16[4,144,1280]{2,1,0:T(8,128)(2,1)}), bf16[4,144,1280]{2,1,0:T(8,128)(2,1)}, u32[]{:S(2)}, u32[]{:S(2)}) %all-to-all-start) | async-done | bytes 1474592 | tf_op jit(solution)/shard_map/all_to_all | solution.py:89
  50.1 3.7 %all-to-all-start.1 = ((bf16[4,128,1152]{2,1,0:T(8,128)(2,1)}), bf16[4,128,1152]{2,1,0:T(8,128)(2,1)S(1)}, u32[]{:S(2)}, u32[]{:S(2)}) async-start(bf16[4,128,1152]{2,1,0:T(8,128)(2,1)} %get-tuple-element.135), calls=%async_computation.1 | async-start | bytes 2359296 | tf_op jit(solution)/shard_map/all_to_all | solution.py:89
  58.3 13.1 %shard_map.248 = (bf16[1024,256]{1,0:T(8,128)(2,1)}, bf16[1024,1024]{1,0:T(8,128)(2,1)}, bf16[1024,256]{1,0:T(8,128)(2,1)}, f32[1024,256]{1,0:T(8,128)}, f32[102...) custom-call(s32[2]{0:T(128)} %pad_add_fusion.1.spot_ref, ...), custom_call_target="tpu_custom_call" | custom-call | flops 2147483648 | bytes 4273152 | tf_op jit(solution)/shard_map/pallas_call | solution.py:188
  78.0 3.5 %all-to-all-start.2 = ((bf16[4,128,1024]{2,1,0:T(8,128)(2,1)}), bf16[4,128,1024]{2,1,0:T(8,128)(2,1)S(1)}, u32[]{:S(2)}, u32[]{:S(2)}) async-start(bf16[4,128,1024]{2,1,0:T(8,128)(2,1)} %bitcast.117), calls=%async_computation.2 | async-start | bytes 2097152 | tf_op jit(solution)/shard_map/all_to_all | solution.py:89
  86.2 12.5 %collective-permute-done.7.lower_ref = bf16[2,128,1152]{2,1,0:T(8,128)(2,1)S(1)} collective-permute-done((bf16[2,128,1152]{2,1,0:T(8,128)(2,1)}, bf16[2,128,1152]{2,1,0:T(8,128)(2,1)S(1)}, u32[]{:S(2)}, u32[]{:S(2)}) %collective-permute-start.7) | collective-permute-done | bytes 589856 | tf_op jit(solution)/shard_map/ppermute | solution.py:55
  101.6 4.3 %all-to-all-start.3 = ((bf16[4,128,1024]{2,1,0:T(8,128)(2,1)}), bf16[4,128,1024]{2,1,0:T(8,128)(2,1)}, u32[]{:S(2)}, u32[]{:S(2)}) async-start(bf16[4,128,1024]{2,1,0:T(8,128)(2,1)} %broadcast_in_dim.75), calls=%async_computation.3 | async-start | bytes 2097152 | tf_op jit(solution)/shard_map/all_to_all | solution.py:89
  108.2 7.5 %all-to-all-done.3 = bf16[4,128,1024]{2,1,0:T(8,128)(2,1)} async-done(((bf16[4,128,1024]{2,1,0:T(8,128)(2,1)}), bf16[4,128,1024]{2,1,0:T(8,128)(2,1)}, u32[]{:S(2)}, u32[]{:S(2)}) %all-to-all-start.3) | async-done | bytes 1048608 | tf_op jit(solution)/shard_map/all_to_all | solution.py:89
  116.4 5.6 %collective-permute-start.10 = (bf16[512,1024]{1,0:T(8,128)(2,1)}, bf16[512,1024]{1,0:T(8,128)(2,1)}, u32[]{:S(2)}, u32[]{:S(2)}) collective-permute-start(bf16[512,1024]{1,0:T(8,128)(2,1)} %bitcast.21.half_ref), channel_id=1, source_target_pairs={{0,1},{1,0},{16,17},{17,16},{2,3},{3,2},{18,19},{19,18},{4,5},{5,4... | collective-permute-start | bytes 3145736 | tf_op jit(solution)/shard_map/ppermute | solution.py:55
  126.2 15.1 %shard_map.249 = (bf16[512,1024]{1,0:T(8,128)(2,1)}, bf16[512,1024]{1,0:T(8,128)(2,1)}, bf16[1024,576]{1,0:T(8,128)(2,1)}, bf16[1024,1152]{1,0:T(8,128)(2,1)}, b...) custom-call(s32[3]{0:T(128)} %pad_add_fusion.2.spot_ref, bf16[512,1024]{1,0:T(8,128)(2,1)} %bitcast.21.half_ref, ...), custom_call_target="tpu_custom_call" | custom-call | flops 6442450944 | bytes 7733248 | tf_op jit(solution)/shard_map/pallas_call | solution.py:188
  148.7 4.6 %convolution_convert_fusion = bf16[1024,1152]{1,0:T(8,128)(2,1)S(1)} fusion(bf16[1024,1024]{1,0:T(8,128)(2,1)} %get-tuple-element.156, bf16[1024,1152]{1,0:T(8,128)(2,1)S(1)} %copy-done.22), kind=kOutput, calls=%fused_computation | convolution fusion | flops 2417098752 | bytes 6815744 | tf_op jit(solution)/shard_map/dot_general | solution.py:216
  166.1 6.4 %all-to-all-start.4 = ((bf16[16,36,8,128]{3,2,1,0:T(8,128)(2,1)}), bf16[16,36,8,128]{3,2,1,0:T(8,128)(2,1)S(1)}, u32[]{:S(2)}, u32[]{:S(2)}) async-start(bf16[16,36,8,128]{3,2,1,0:T(8,128)(2,1)} %bitcast.27), calls=%async_computation.4 | async-start | bytes 2359296 | tf_op jit(solution)/shard_map/all_to_all | solution.py:89
  172.6 3.4 %collective-permute-done.16 = bf16[128,1024]{1,0:T(8,128)(2,1)S(1)} collective-permute-done((bf16[128,1024]{1,0:T(8,128)(2,1)S(1)}, bf16[128,1024]{1,0:T(8,128)(2,1)S(1)}, u32[]{:S(2)}, u32[]{:S(2)}) %collective-permute-start.16) | collective-permute-done | bytes 262176 | tf_op jit(solution)/shard_map/ppermute | solution.py:55
  176.0 4.4 %collective-permute-done.18 = bf16[128,1024]{1,0:T(8,128)(2,1)} collective-permute-done((bf16[128,1024]{1,0:T(8,128)(2,1)S(1)}, bf16[128,1024]{1,0:T(8,128)(2,1)}, u32[]{:S(2)}, u32[]{:S(2)}) %collective-permute-start.18) | collective-permute-done | bytes 262176 | tf_op jit(solution)/shard_map/ppermute | solution.py:55
  183.3 3.1 convolution_convert_fusion.1
  190.1 4.1 %all-to-all-start.5 = ((bf16[16,72,8,128]{3,2,1,0:T(8,128)(2,1)}), bf16[16,72,8,128]{3,2,1,0:T(8,128)(2,1)S(1)}, u32[]{:S(2)}, u32[]{:S(2)}) async-start(bf16[16,72,8,128]{3,2,1,0:T(8,128)(2,1)} %bitcast.24), calls=%async_computation.5 | async-start | bytes 4718592 | tf_op jit(solution)/shard_map/all_to_all | solution.py:89
  195.0 17.8 %shard_map.250 = (bf16[512,1024]{1,0:T(8,128)(2,1)}, bf16[512,1024]{1,0:T(8,128)(2,1)}, f32[4,4,32,8,128]{4,3,2,1,0:T(8,128)}) custom-call(s32[1]{0:T(128)} %bitcast.spot_ref, bf16[512,1024]{1,0:T(8,128)(2,1)} %pad_maximum_fusion.near_ref, bf16[512,1024]{1,0:T(8,128)(2,1)} %collective-permute-done.19.far_ref, bf16[128,1024]{1,0:T(8,128)(2,1)} %copy-done.5, ...), custom_call_target="tpu_custom_call" | custom-call | flops 4294967296 | bytes 9028608 | tf_op jit(solution)/shard_map/pallas_call | solution.py:188
  212.8 3.3 collective-permute-start.20
  236.4 3.3 %all-to-all-start.6 = ((bf16[4,2,9,8,128]{4,3,2,1,0:T(8,128)(2,1)}), bf16[4,2,9,8,128]{4,3,2,1,0:T(8,128)(2,1)S(1)}, u32[]{:S(2)}, u32[]{:S(2)}) async-start(bf16[4,2,9,8,128]{4,3,2,1,0:T(8,128)(2,1)} %bitcast.36), calls=%async_computation.6 | async-start | bytes 294912 | tf_op jit(solution)/shard_map/all_to_all | solution.py:89
  241.2 4.6 %collective-permute-done.22 = bf16[128,1024]{1,0:T(8,128)(2,1)} collective-permute-done((bf16[128,1024]{1,0:T(8,128)(2,1)}, bf16[128,1024]{1,0:T(8,128)(2,1)}, u32[]{:S(2)}, u32[]{:S(2)}) %collective-permute-start.22) | collective-permute-done | bytes 262176 | tf_op jit(solution)/shard_map/ppermute | solution.py:55
  249.5 4.8 %all-to-all-start.7 = ((bf16[16,432,128]{2,1,0:T(8,128)(2,1)}), bf16[16,432,128]{2,1,0:T(8,128)(2,1)S(1)}, u32[]{:S(2)}, u32[]{:S(2)}) async-start(bf16[16,432,128]{2,1,0:T(8,128)(2,1)} %bitcast.116), calls=%async_computation.8 | async-start | bytes 3538944 | tf_op jit(solution)/shard_map/all_to_all | solution.py:89
  265.3 13.1 %collective-permute-done.28 = bf16[32,8,128]{2,1,0:T(8,128)(2,1)S(1)} collective-permute-done((bf16[32,8,128]{2,1,0:T(8,128)(2,1)}, bf16[32,8,128]{2,1,0:T(8,128)(2,1)S(1)}, u32[]{:S(2)}, u32[]{:S(2)}) %collective-permute-start.28) | collective-permute-done | bytes 65568 | tf_op jit(solution)/shard_map/ppermute | solution.py:55
  290.3 3.9 %collective-permute-start.36 = (bf16[160,128]{1,0:T(8,128)(2,1)S(1)}, bf16[160,128]{1,0:T(8,128)(2,1)S(1)}, u32[]{:S(2)}, u32[]{:S(2)}) collective-permute-start(bf16[160,128]{1,0:T(8,128)(2,1)S(1)} %get-tuple-element.259), channel_id=1, source_target_pairs={{0,2},{1,3},{16,18},{17,19},{2,0},{3,1},{18,16},{19,17},{4,6},{5,7... | collective-permute-start | bytes 122888 | tf_op jit(solution)/shard_map/ppermute | solution.py:55
  301.2 4.2 %collective-permute-start.38 = (bf16[4,160,128]{2,1,0:T(8,128)(2,1)S(1)}, bf16[4,160,128]{2,1,0:T(8,128)(2,1)S(1)}, u32[]{:S(2)}, u32[]{:S(2)}) collective-permute-start(bf16[4,160,128]{2,1,0:T(8,128)(2,1)S(1)} %pad_maximum_fusion.4), channel_id=1, source_target_pairs={{0,12},{1,13},{16,28},{17,29},{2,14},{3,15},{18,30},{19,31},{4,0},... | collective-permute-start | bytes 491528 | tf_op jit(solution)/shard_map/ppermute | solution.py:55
  306.1 6.5 %collective-permute-done.38 = bf16[4,160,128]{2,1,0:T(8,128)(2,1)S(1)} collective-permute-done((bf16[4,160,128]{2,1,0:T(8,128)(2,1)S(1)}, bf16[4,160,128]{2,1,0:T(8,128)(2,1)S(1)}, u32[]{:S(2)}, u32[]{:S(2)}) %collective-permute-start.38) | collective-permute-done | bytes 163872 | tf_op jit(solution)/shard_map/ppermute | solution.py:55
  312.6 3.4 %collective-permute-done.40 = bf16[4,160,128]{2,1,0:T(8,128)(2,1)S(1)} collective-permute-done((bf16[4,160,128]{2,1,0:T(8,128)(2,1)S(1)}, bf16[4,160,128]{2,1,0:T(8,128)(2,1)S(1)}, u32[]{:S(2)}, u32[]{:S(2)}) %collective-permute-start.40) | collective-permute-done | bytes 163872 | tf_op jit(solution)/shard_map/ppermute | solution.py:55
  316.1 4.1 %shard_map.251 = (f32[128,4608]{1,0:T(8,128)}, f32[128,4608]{1,0:T(8,128)}, f32[576,1024]{1,0:T(8,128)}) custom-call(s32[2]{0:T(128)S(1)} %pad_add_fusion.3.spot_ref, bf16[16,432,128]{2,1,0:T(8,128)(2,1)S(1)} %all-to-all-done.7.mine_ref, bf16[16,432,128]{2,1,0:T(8,128)(2,1)S(1)} %collective-permute-done.41.other_ref), custom_call_target="tpu_custom_call" | custom-call | flops 5368709120 | bytes 3538944 | tf_op jit(solution)/shard_map/pallas_call | solution.py:188
  (210 shorter events, 131.8 us)
Async XLA Ops:
  25.2 19.7 %all-to-all-start = ((bf16[4,144,1280]{2,1,0:T(8,128)(2,1)}), bf16[4,144,1280]{2,1,0:T(8,128)(2,1)}, u32[]{:S(2)}, u32[]{:S(2)}) async-start(bf16[4,144,1280]{2,1,0:T(8,128)(2,1)} %get-tuple-element.119), calls=%async_computation | async-start | bytes 2949120 | tf_op jit(solution)/shard_map/all_to_all | solution.py:89
  44.9 11.7 %collective-permute-start.4 = (bf16[4,144,1280]{2,1,0:T(8,128)(2,1)}, bf16[4,144,1280]{2,1,0:T(8,128)(2,1)}, u32[]{:S(2)}, u32[]{:S(2)}) collective-permute-start(bf16[4,144,1280]{2,1,0:T(8,128)(2,1)} %all-to-all-done.half_ref), channel_id=1, source_target_pairs={{0,1},{1,0},{16,17},{17,16},{2,3},{3,2},{18,19},{19,18},{4,5},{5,4... | collective-permute-start | bytes 4423688 | tf_op jit(solution)/shard_map/ppermute | solution.py:55
  45.9 10.7 %collective-permute-start.5 = (bf16[4,128,256]{2,1,0:T(8,128)(2,1)S(1)}, bf16[4,128,256]{2,1,0:T(8,128)(2,1)S(1)}, u32[]{:S(2)}, u32[]{:S(2)}) collective-permute-start(bf16[4,128,256]{2,1,0:T(8,128)(2,1)S(1)} %slice.128), channel_id=1, source_target_pairs={{0,16},{1,17},{16,2},{17,3},{2,18},{3,19},{18,0},{19,1},{4,20},{5,... | collective-permute-start | bytes 786440 | tf_op jit(solution)/shard_map/ppermute | solution.py:55
  50.1 22.6 %all-to-all-start.1 = ((bf16[4,128,1152]{2,1,0:T(8,128)(2,1)}), bf16[4,128,1152]{2,1,0:T(8,128)(2,1)S(1)}, u32[]{:S(2)}, u32[]{:S(2)}) async-start(bf16[4,128,1152]{2,1,0:T(8,128)(2,1)} %get-tuple-element.135), calls=%async_computation.1 | async-start | bytes 2359296 | tf_op jit(solution)/shard_map/all_to_all | solution.py:89
  78.0 20.7 %all-to-all-start.2 = ((bf16[4,128,1024]{2,1,0:T(8,128)(2,1)}), bf16[4,128,1024]{2,1,0:T(8,128)(2,1)S(1)}, u32[]{:S(2)}, u32[]{:S(2)}) async-start(bf16[4,128,1024]{2,1,0:T(8,128)(2,1)} %bitcast.117), calls=%async_computation.2 | async-start | bytes 2097152 | tf_op jit(solution)/shard_map/all_to_all | solution.py:89
  81.5 26.7 %all-gather.2.cloned.1.call-start = ((), (), s32[]{:S(2)}) async-start(), calls=%async_computation.9 | async-start | bytes 1310720 | tf_op jit(solution)/shard_map/all_gather | solution.py:712
  82.7 16.0 %collective-permute-start.7 = (bf16[2,128,1152]{2,1,0:T(8,128)(2,1)}, bf16[2,128,1152]{2,1,0:T(8,128)(2,1)S(1)}, u32[]{:S(2)}, u32[]{:S(2)}) collective-permute-start(bf16[2,128,1152]{2,1,0:T(8,128)(2,1)} %get-tuple-element.239), channel_id=1, source_target_pairs={{0,16},{1,17},{16,2},{17,3},{2,18},{3,19},{18,0},{19,1},{4,20},{5,... | collective-permute-start | bytes 1769480 | tf_op jit(solution)/shard_map/ppermute | solution.py:55
  82.7 16.0 %collective-permute-start.8 = (bf16[2,128,1152]{2,1,0:T(8,128)(2,1)}, bf16[2,128,1152]{2,1,0:T(8,128)(2,1)S(1)}, u32[]{:S(2)}, u32[]{:S(2)}) collective-permute-start(bf16[2,128,1152]{2,1,0:T(8,128)(2,1)} %get-tuple-element.238), channel_id=1, source_target_pairs={{0,18},{1,19},{16,0},{17,1},{2,16},{3,17},{18,2},{19,3},{4,22},{5,... | collective-permute-start | bytes 1769480 | tf_op jit(solution)/shard_map/ppermute | solution.py:55
  98.9 17.6 %collective-permute-start.9 = (bf16[576,1024]{1,0:T(8,128)(2,1)}, bf16[576,1024]{1,0:T(8,128)(2,1)S(1)}, u32[]{:S(2)}, u32[]{:S(2)}) collective-permute-start(bf16[576,1024]{1,0:T(8,128)(2,1)} %param.28), channel_id=1, source_target_pairs={{0,18},{17,1},{2,16},{19,3},{4,22},{21,5},{6,20},{23,7},{8,26},{25... | collective-permute-start | bytes 3538952 | tf_op jit(solution)/shard_map/ppermute | solution.py:55
  101.6 14.1 %all-to-all-start.3 = ((bf16[4,128,1024]{2,1,0:T(8,128)(2,1)}), bf16[4,128,1024]{2,1,0:T(8,128)(2,1)}, u32[]{:S(2)}, u32[]{:S(2)}) async-start(bf16[4,128,1024]{2,1,0:T(8,128)(2,1)} %broadcast_in_dim.75), calls=%async_computation.3 | async-start | bytes 2097152 | tf_op jit(solution)/shard_map/all_to_all | solution.py:89
  145.9 11.8 %collective-permute-start.13 = (bf16[128,1024]{1,0:T(8,128)(2,1)S(1)}, bf16[128,1024]{1,0:T(8,128)(2,1)S(1)}, u32[]{:S(2)}, u32[]{:S(2)}) collective-permute-start(bf16[128,1024]{1,0:T(8,128)(2,1)S(1)} %get-tuple-element.153), channel_id=1, source_target_pairs={{0,32},{1,33},{16,48},{17,49},{2,34},{3,35},{18,50},{19,51},{4,36}... | collective-permute-start | bytes 786440 | tf_op jit(solution)/shard_map/ppermute | solution.py:55
  146.2 13.5 %collective-permute-start.14 = (bf16[128,1024]{1,0:T(8,128)(2,1)S(1)}, bf16[128,1024]{1,0:T(8,128)(2,1)S(1)}, u32[]{:S(2)}, u32[]{:S(2)}) collective-permute-start(bf16[128,1024]{1,0:T(8,128)(2,1)S(1)} %get-tuple-element.154), channel_id=1, source_target_pairs={{0,64},{1,65},{16,80},{17,81},{2,66},{3,67},{18,82},{19,83},{4,68}... | collective-permute-start | bytes 786440 | tf_op jit(solution)/shard_map/ppermute | solution.py:55
  148.0 12.6 %collective-permute-start.15 = (bf16[128,1024]{1,0:T(8,128)(2,1)S(1)}, bf16[128,1024]{1,0:T(8,128)(2,1)S(1)}, u32[]{:S(2)}, u32[]{:S(2)}) collective-permute-start(bf16[128,1024]{1,0:T(8,128)(2,1)S(1)} %get-tuple-element.155), channel_id=1, source_target_pairs={{0,96},{1,97},{16,112},{17,113},{2,98},{3,99},{18,114},{19,115},{4... | collective-permute-start | bytes 786440 | tf_op jit(solution)/shard_map/ppermute | solution.py:55
  162.6 13.3 %collective-permute-start.16 = (bf16[128,1024]{1,0:T(8,128)(2,1)S(1)}, bf16[128,1024]{1,0:T(8,128)(2,1)S(1)}, u32[]{:S(2)}, u32[]{:S(2)}) collective-permute-start(bf16[128,1024]{1,0:T(8,128)(2,1)S(1)} %get-tuple-element.223), channel_id=1, source_target_pairs={{0,96},{1,97},{16,112},{17,113},{2,98},{3,99},{18,114},{19,115},{4... | collective-permute-start | bytes 786440 | tf_op jit(solution)/shard_map/ppermute | solution.py:55
  165.5 14.8 %collective-permute-start.18 = (bf16[128,1024]{1,0:T(8,128)(2,1)S(1)}, bf16[128,1024]{1,0:T(8,128)(2,1)}, u32[]{:S(2)}, u32[]{:S(2)}) collective-permute-start(bf16[128,1024]{1,0:T(8,128)(2,1)S(1)} %get-tuple-element.223), channel_id=1, source_target_pairs={{0,32},{1,33},{16,48},{17,49},{2,34},{3,35},{18,50},{19,51},{4,36}... | collective-permute-start | bytes 786440 | tf_op jit(solution)/shard_map/ppermute | solution.py:55
  166.1 23.0 %all-to-all-start.4 = ((bf16[16,36,8,128]{3,2,1,0:T(8,128)(2,1)}), bf16[16,36,8,128]{3,2,1,0:T(8,128)(2,1)S(1)}, u32[]{:S(2)}, u32[]{:S(2)}) async-start(bf16[16,36,8,128]{3,2,1,0:T(8,128)(2,1)} %bitcast.27), calls=%async_computation.4 | async-start | bytes 2359296 | tf_op jit(solution)/shard_map/all_to_all | solution.py:89
  190.1 45.2 %all-to-all-start.5 = ((bf16[16,72,8,128]{3,2,1,0:T(8,128)(2,1)}), bf16[16,72,8,128]{3,2,1,0:T(8,128)(2,1)S(1)}, u32[]{:S(2)}, u32[]{:S(2)}) async-start(bf16[16,72,8,128]{3,2,1,0:T(8,128)(2,1)} %bitcast.24), calls=%async_computation.5 | async-start | bytes 4718592 | tf_op jit(solution)/shard_map/all_to_all | solution.py:89
  194.2 70.0 %reduce-scatter.2.cloned.1.call-start = ((), (), s32[]{:S(2)}) async-start(), calls=%async_computation.10 | async-start | bytes 2359296 | tf_op jit(solution)/shard_map/reduce_scatter | solution.py:769
  223.6 10.6 %collective-permute-start.24 = (bf16[4,32,8,128]{3,2,1,0:T(8,128)(2,1)}, bf16[4,32,8,128]{3,2,1,0:T(8,128)(2,1)}, u32[]{:S(2)}, u32[]{:S(2)}) collective-permute-start(bf16[4,32,8,128]{3,2,1,0:T(8,128)(2,1)} %get-tuple-element.229), channel_id=1, source_target_pairs={{0,4},{1,5},{16,20},{17,21},{2,6},{3,7},{18,22},{19,23},{4,8},{5,9... | collective-permute-start | bytes 786440 | tf_op jit(solution)/shard_map/ppermute | solution.py:55
  227.3 13.2 %collective-permute-start.25 = (bf16[4,32,8,128]{3,2,1,0:T(8,128)(2,1)}, bf16[4,32,8,128]{3,2,1,0:T(8,128)(2,1)}, u32[]{:S(2)}, u32[]{:S(2)}) collective-permute-start(bf16[4,32,8,128]{3,2,1,0:T(8,128)(2,1)} %get-tuple-element.228), channel_id=1, source_target_pairs={{0,8},{1,9},{16,24},{17,25},{2,10},{3,11},{18,26},{19,27},{4,12},{... | collective-permute-start | bytes 786440 | tf_op jit(solution)/shard_map/ppermute | solution.py:55
  229.8 11.4 %collective-permute-start.26 = (bf16[4,32,8,128]{3,2,1,0:T(8,128)(2,1)}, bf16[4,32,8,128]{3,2,1,0:T(8,128)(2,1)}, u32[]{:S(2)}, u32[]{:S(2)}) collective-permute-start(bf16[4,32,8,128]{3,2,1,0:T(8,128)(2,1)} %get-tuple-element.227), channel_id=1, source_target_pairs={{0,12},{1,13},{16,28},{17,29},{2,14},{3,15},{18,30},{19,31},{4,0},... | collective-permute-start | bytes 786440 | tf_op jit(solution)/shard_map/ppermute | solution.py:55
  232.9 12.8 %collective-permute-start.22 = (bf16[128,1024]{1,0:T(8,128)(2,1)}, bf16[128,1024]{1,0:T(8,128)(2,1)}, u32[]{:S(2)}, u32[]{:S(2)}) collective-permute-start(bf16[128,1024]{1,0:T(8,128)(2,1)} %get-tuple-element.181), channel_id=1, source_target_pairs={{0,64},{1,65},{16,80},{17,81},{2,66},{3,67},{18,82},{19,83},{4,68}... | collective-permute-start | bytes 786440 | tf_op jit(solution)/shard_map/ppermute | solution.py:55
  234.3 11.8 %collective-permute-start.23 = (bf16[128,1024]{1,0:T(8,128)(2,1)}, bf16[128,1024]{1,0:T(8,128)(2,1)}, u32[]{:S(2)}, u32[]{:S(2)}) collective-permute-start(bf16[128,1024]{1,0:T(8,128)(2,1)} %get-tuple-element.182), channel_id=1, source_target_pairs={{0,96},{1,97},{16,112},{17,113},{2,98},{3,99},{18,114},{19,115},{4... | collective-permute-start | bytes 786440 | tf_op jit(solution)/shard_map/ppermute | solution.py:55
  236.4 11.6 %all-to-all-start.6 = ((bf16[4,2,9,8,128]{4,3,2,1,0:T(8,128)(2,1)}), bf16[4,2,9,8,128]{4,3,2,1,0:T(8,128)(2,1)S(1)}, u32[]{:S(2)}, u32[]{:S(2)}) async-start(bf16[4,2,9,8,128]{4,3,2,1,0:T(8,128)(2,1)} %bitcast.36), calls=%async_computation.6 | async-start | bytes 294912 | tf_op jit(solution)/shard_map/all_to_all | solution.py:89
  249.5 48.9 %all-to-all-start.7 = ((bf16[16,432,128]{2,1,0:T(8,128)(2,1)}), bf16[16,432,128]{2,1,0:T(8,128)(2,1)S(1)}, u32[]{:S(2)}, u32[]{:S(2)}) async-start(bf16[16,432,128]{2,1,0:T(8,128)(2,1)} %bitcast.116), calls=%async_computation.8 | async-start | bytes 3538944 | tf_op jit(solution)/shard_map/all_to_all | solution.py:89
  257.5 20.9 %collective-permute-start.28 = (bf16[32,8,128]{2,1,0:T(8,128)(2,1)}, bf16[32,8,128]{2,1,0:T(8,128)(2,1)S(1)}, u32[]{:S(2)}, u32[]{:S(2)}) collective-permute-start(bf16[32,8,128]{2,1,0:T(8,128)(2,1)} %get-tuple-element.244), channel_id=1, source_target_pairs={{0,16},{1,17},{16,2},{17,3},{2,18},{3,19},{18,0},{19,1},{4,20},{5,... | collective-permute-start | bytes 196616 | tf_op jit(solution)/shard_map/ppermute | solution.py:55
  258.9 19.5 %collective-permute-start.29 = (bf16[32,8,128]{2,1,0:T(8,128)(2,1)}, bf16[32,8,128]{2,1,0:T(8,128)(2,1)S(1)}, u32[]{:S(2)}, u32[]{:S(2)}) collective-permute-start(bf16[32,8,128]{2,1,0:T(8,128)(2,1)} %get-tuple-element.243), channel_id=1, source_target_pairs={{0,2},{1,3},{16,18},{17,19},{2,0},{3,1},{18,16},{19,17},{4,6},{5,7... | collective-permute-start | bytes 196616 | tf_op jit(solution)/shard_map/ppermute | solution.py:55
  261.3 17.3 %collective-permute-start.30 = (bf16[32,8,128]{2,1,0:T(8,128)(2,1)}, bf16[32,8,128]{2,1,0:T(8,128)(2,1)}, u32[]{:S(2)}, u32[]{:S(2)}) collective-permute-start(bf16[32,8,128]{2,1,0:T(8,128)(2,1)} %get-tuple-element.242), channel_id=1, source_target_pairs={{0,18},{1,19},{16,0},{17,1},{2,16},{3,17},{18,2},{19,3},{4,22},{5,... | collective-permute-start | bytes 196616 | tf_op jit(solution)/shard_map/ppermute | solution.py:55
  279.1 11.1 %collective-permute-start.34 = (bf16[2,128,1024]{2,1,0:T(8,128)(2,1)S(1)}, bf16[2,128,1024]{2,1,0:T(8,128)(2,1)S(1)}, u32[]{:S(2)}, u32[]{:S(2)}) collective-permute-start(bf16[2,128,1024]{2,1,0:T(8,128)(2,1)S(1)} %pad_maximum_fusion.2), channel_id=1, source_target_pairs={{0,0},{1,16},{16,1},{17,17},{2,2},{3,18},{18,3},{19,19},{4,4},{5,2... | collective-permute-start | bytes 1572872 | tf_op jit(solution)/shard_map/ppermute | solution.py:55
  298.4 17.7 %collective-permute-start.41 = (bf16[16,432,128]{2,1,0:T(8,128)(2,1)S(1)}, bf16[16,432,128]{2,1,0:T(8,128)(2,1)S(1)}, u32[]{:S(2)}, u32[]{:S(2)}) collective-permute-start(bf16[16,432,128]{2,1,0:T(8,128)(2,1)S(1)} %all-to-all-done.7.mine_ref), channel_id=1, source_target_pairs={{0,1},{1,0},{16,17},{17,16},{2,3},{3,2},{18,19},{19,18},{4,5},{5,4... | collective-permute-start | bytes 5308424 | tf_op jit(solution)/shard_map/ppermute | solution.py:55
  301.2 11.4 %collective-permute-start.38 = (bf16[4,160,128]{2,1,0:T(8,128)(2,1)S(1)}, bf16[4,160,128]{2,1,0:T(8,128)(2,1)S(1)}, u32[]{:S(2)}, u32[]{:S(2)}) collective-permute-start(bf16[4,160,128]{2,1,0:T(8,128)(2,1)S(1)} %pad_maximum_fusion.4), channel_id=1, source_target_pairs={{0,12},{1,13},{16,28},{17,29},{2,14},{3,15},{18,30},{19,31},{4,0},... | collective-permute-start | bytes 491528 | tf_op jit(solution)/shard_map/ppermute | solution.py:55
  305.4 10.6 %collective-permute-start.40 = (bf16[4,160,128]{2,1,0:T(8,128)(2,1)S(1)}, bf16[4,160,128]{2,1,0:T(8,128)(2,1)S(1)}, u32[]{:S(2)}, u32[]{:S(2)}) collective-permute-start(bf16[4,160,128]{2,1,0:T(8,128)(2,1)S(1)} %pad_maximum_fusion.4), channel_id=1, source_target_pairs={{0,4},{1,5},{16,20},{17,21},{2,6},{3,7},{18,22},{19,23},{4,8},{5,9... | collective-permute-start | bytes 491528 | tf_op jit(solution)/shard_map/ppermute | solution.py:55
  (44 other events, 358.5 us)
Sparse Core Ops, SparseCore 0:
  85.5 22.6 all-gather.1
  197.5 34.8 reduce-scatter.1
